TPU v7x, 128 devices: a whole 4x4x4 slice. The times are simulated.
128 devices in a mesh: rows: 32 (over x, y, core), cols: 4 (over z).
Axes of the slice: x: 4, y: 4, z: 4, core: 2. Of those that a mesh axis runs over, the one named last changes fastest.
Arguments:
- blocks: bfloat16 [16384, 128, 128], P(('rows', 'cols')), may hold values from -20 to 20
- owner: int32 [16384, 1], P(('rows', 'cols')), may hold values from 0 to 127; in each aligned block of 128 rows (0 to 127, 128 to 255, ...) at most 2 rows name the same one
- block_pos: int32 [16384], P(('rows', 'cols')), may hold values from 0 to 415
- omega: bfloat16 [53248, 512], P('cols'), may hold values from -0.02734375 to 0.02734375
Outputs:
- basis: bfloat16 [16384, 512], P('rows', 'cols')
- coefficients: float32 [512, 53248], P('rows', 'cols')
Inputs may be any that keep to these rules, and one draw needn't show every extreme that they name: `owner`: among the slots of one device no tile is named more than 2 times, and on at least one device some tile is named exactly 2 times. `block_pos`: several slots may name the same block of the same tile; their blocks add.
All inputs are finite; a program needn't handle non-finite values.
Results may differ from a plain program's by a relative error of at most 0.0038.
Values may be sent and summed in bfloat16 or wider, within the bound.
No kernel may reach another device: no remote copies, remote signals or barrier semaphores. Data moves between devices by JAX's collectives and lax.ppermute only.
A program may use at most 192 MiB of HBM per device.

v0:
```python
import math

import jax
import jax.numpy as jnp
from jax import lax
from jax.sharding import PartitionSpec as P

PBR = 4
TBC = 104


def on_device(blocks, owner, block_pos, omega):
    slot_count = blocks.shape[0]
    block_edge = blocks.shape[1]
    rank_width = omega.shape[1]
    row_devices = lax.axis_size("rows")
    col_devices = lax.axis_size("cols")
    devices_all = row_devices * col_devices
    capacity = max(2, 2 * slot_count // devices_all)
    tile_slots = PBR * TBC
    target = owner[:, 0]
    onehot = (target[:, None] == jnp.arange(devices_all, dtype=jnp.int32)[None, :]).astype(
        jnp.int32
    )
    before = jnp.cumsum(onehot, axis=0) - onehot
    within = jnp.sum(before * onehot, axis=1)
    placing = target * capacity + within
    send_blocks = (
        jnp.zeros((devices_all * capacity, block_edge, block_edge), blocks.dtype)
        .at[placing]
        .set(blocks)
    )
    send_where = jnp.full((devices_all * capacity,), -1, jnp.int32).at[placing].set(block_pos)
    got_blocks, got_where = (
        lax.all_to_all(
            send_blocks.reshape(devices_all, capacity, block_edge, block_edge),
            ("rows", "cols"),
            split_axis=0,
            concat_axis=0,
            tiled=True,
        ),
        lax.all_to_all(
            send_where.reshape(devices_all, capacity),
            ("rows", "cols"),
            split_axis=0,
            concat_axis=0,
            tiled=True,
        ),
    )
    flat_where = got_where.reshape(-1)
    flat_where = jnp.where(flat_where < 0, tile_slots, flat_where)
    summed = (
        jnp.zeros((tile_slots, block_edge, block_edge), jnp.float32)
        .at[flat_where]
        .add(got_blocks.reshape(-1, block_edge, block_edge).astype(jnp.float32), mode="drop")
    )
    dense_tile = summed.astype(jnp.bfloat16).reshape(PBR, TBC, block_edge, block_edge)
    omega_blocks = omega.reshape(TBC, block_edge, rank_width)
    partial_value = jnp.einsum(
        "pcij,cjr->pir", dense_tile, omega_blocks, preferred_element_type=jnp.float32
    ).reshape(PBR * block_edge, rank_width)
    total_rows = PBR * block_edge * row_devices
    sketch = lax.psum(partial_value, "cols")
    local_gram = jnp.dot(
        sketch.T, sketch, precision=lax.Precision.HIGHEST, preferred_element_type=jnp.float32
    )
    gram_sum = lax.psum(local_gram, "rows")
    factor = jnp.linalg.cholesky(gram_sum / total_rows)
    basis_full = lax.linalg.triangular_solve(
        factor, sketch, left_side=False, lower=True, transpose_a=True
    ).astype(jnp.bfloat16)
    slice_width = rank_width // col_devices
    basis_out = lax.dynamic_slice_in_dim(
        basis_full, lax.axis_index("cols") * slice_width, slice_width, 1
    )
    basis_blocks = basis_full.reshape(PBR, block_edge, rank_width)
    scaling = 1.0 / math.sqrt(total_rows)
    product = jnp.einsum(
        "pir,pcij->rcj", basis_blocks, dense_tile, preferred_element_type=jnp.float32
    )
    coefficients = lax.psum_scatter(
        product.reshape(rank_width // row_devices * lax.axis_size("rows"), TBC * block_edge)
        * scaling,
        "rows",
        scatter_dimension=0,
        tiled=True,
    )
    return (basis_out, coefficients)


def solution(mesh):
    in_specs = (
        P(("rows", "cols"), None, None),
        P(("rows", "cols"), None),
        P(("rows", "cols")),
        P("cols", None),
    )
    out_specs = (P("rows", "cols"), P("rows", "cols"))
    return jax.shard_map(
        on_device, mesh=mesh, in_specs=in_specs, out_specs=out_specs, check_vma=False
    )
```

profile of v0, /device:TPU:0, one launch (start us, length us, event | category | flops | bytes accessed | tf_op | source)
XLA Modules:
  0.0 737.8 jit_solution(12992096855828615097)
XLA Ops:
  7.2 0.7 fusion.37
  7.9 0.2 reduce_window_sum.11
  8.1 0.8 select_reduce_fusion.4
  8.9 0.7 fusion.38
  9.6 1.1 scatter_custom_fusion
  10.7 0.8 all_to_all.9
  11.5 11.1 %all-to-all-start = ((s32[128,1,2]{2,1,0:T(1,128)}), s32[128,1,2]{2,1,0:T(1,128)S(1)}, u32[]{:S(2)}, u32[]{:S(2)}) async-start(s32[128,1,2]{2,1,0:T(1,128)} %bitcast.3), calls=%async_computation | async-start | bytes 131072 | tf_op jit(solution)/shard_map/all_to_all | solution.py:42
  22.6 5.3 broadcast_in_dim.22
  27.9 19.3 %scatter_fusion = bf16[256,128,128]{2,1,0:T(8,128)(2,1)} fusion(bf16[256,128,128]{2,1,0:T(8,128)(2,1)} %broadcast_in_dim.22, s32[128]{0:T(128)S(1)} %fusion.38, bf16[128,128,128]{2,1,0:T(8,128)(2,1)} %param.4), kind=kCustom, calls=%fused_computation.1 | custom fusion | bytes 12583424 | tf_op jit(solution)/shard_map/scatter | solution.py:31
  47.3 10.3 %all-to-all-start.1 = ((bf16[128,2,128,128]{3,2,1,0:T(8,128)(2,1)}), bf16[128,2,128,128]{3,2,1,0:T(8,128)(2,1)}, u32[]{:S(2)}, u32[]{:S(2)}) async-start(bf16[128,2,128,128]{3,2,1,0:T(8,128)(2,1)} %bitcast.91), calls=%async_computation.1 | async-start | bytes 16777216 | tf_op jit(solution)/shard_map/all_to_all | solution.py:35
  57.6 0.5 broadcast.246
  58.1 0.8 reduce.27
  59.0 0.1 reshape.101
  59.1 106.5 %all-to-all-done.1 = bf16[128,2,128,128]{3,2,1,0:T(8,128)(2,1)} async-done(((bf16[128,2,128,128]{3,2,1,0:T(8,128)(2,1)}), bf16[128,2,128,128]{3,2,1,0:T(8,128)(2,1)}, u32[]{:S(2)}, u32[]{:S(2)}) %all-to-all-start.1) | async-done | bytes 8388640 | tf_op jit(solution)/shard_map/all_to_all | solution.py:35
  165.7 11.3 %bitcast_convert_fusion = f32[256,128,128]{2,1,0:T(8,128)} fusion(bf16[128,2,128,128]{3,2,1,0:T(8,128)(2,1)} %all-to-all-done.1), kind=kLoop, calls=%fused_computation.6 | loop fusion | flops 4194304 | bytes 25165824 | tf_op jit(solution)/shard_map/convert_element_type | solution.py:55
  177.0 12.5 %broadcast_in_dim.19 = f32[416,128,128]{2,1,0:T(8,128)} broadcast(f32[]{:T(128)} %constant.157.clone.1), dimensions={} | broadcast | bytes 27262980 | tf_op jit(solution)/shard_map/broadcast_in_dim | solution.py:53
  189.5 49.9 %scatter_fusion.1 = f32[416,128,128]{2,1,0:T(8,128)} fusion(f32[416,128,128]{2,1,0:T(8,128)} %broadcast_in_dim.19, s32[256]{0:T(256)S(1)} %bitcast.97, f32[256,128,128]{2,1,0:T(8,128)} %bitcast_convert_fusion), kind=kCustom, calls=%fused_computation.2 | custom fusion | flops 4194304 | bytes 50332672 | tf_op jit(solution)/shard_map/scatter-add | solution.py:55
  239.4 12.8 %convert_element_type.17 = bf16[416,128,128]{2,1,0:T(8,128)(2,1)S(1)} convert(f32[416,128,128]{2,1,0:T(8,128)} %scatter_fusion.1) | non-fusion elementwise | flops 6815744 | bytes 40894464 | tf_op jit(solution)/shard_map/convert_element_type | solution.py:57
  252.2 1.6 copy.22
  253.9 3.2 copy-done
  257.1 8.2 %convolution_bitcast_fusion = f32[512,512]{1,0:T(8,128)} fusion(bf16[512,104,128]{2,0,1:T(8,128)(2,1)S(1)} %bitcast.92, bf16[104,128,512]{2,1,0:T(8,128)(2,1)S(1)} %bitcast.102), kind=kOutput, calls=%fused_computation.7 | convolution fusion | flops 6979321856 | bytes 28311552 | tf_op jit(solution)/shard_map/pcij,cjr->pir/dot_general | solution.py:59
  265.4 44.3 %all-reduce.4.cloned.1.call-done = f32[512,512]{1,0:T(8,128)} async-done(((f32[512,512]{1,0:T(8,128)}), f32[512,512]{1,0:T(8,128)}) %all-reduce.4.cloned.1.call-update) | async-done | bytes 1048592 | tf_op jit(solution)/shard_map/psum | solution.py:63
  309.7 4.5 fusion.48
  314.2 17.7 %copy.29 = bf16[104,128,128,4]{2,1,0,3:T(8,128)(2,1)} copy(bf16[104,128,128,4]{1,2,0,3:T(8,128)(2,1)} %bitcast.89) | data formatting | bytes 27262976 | tf_op jit(solution)/shard_map/pir,pcij->rcj/dot_general | solution.py:78
  331.9 87.7 %all-reduce.6.cloned.1.call-done = f32[512,512]{0,1:T(8,128)} async-done(((f32[512,512]{0,1:T(8,128)}), f32[512,512]{0,1:T(8,128)}) %all-reduce.6.cloned.1.call-update) | async-done | bytes 1048592 | tf_op jit(solution)/shard_map/psum | solution.py:67
  419.6 1.3 broadcast_multiply_fusion
  420.9 0.3 copy.24
  421.3 1.5 fusion
  422.7 11.7 %cholesky.104 = f32[128,128]{1,0:T(8,128)S(1)} custom-call(f32[128,128]{1,0:T(8,128)S(1)} %cholesky.266), custom_call_target="Cholesky" | custom-call | tf_op jit(solution)/shard_map/jit(cholesky)/cholesky | solution.py:68
  434.6 9.8 %custom-call.30 = f32[1,128,128]{1,2,0:T(8,128)S(1)} custom-call(f32[1,128,128]{2,1,0:T(8,128)S(1)} %get-tuple-element.29), custom_call_target="InvertDiagBlocksLowerTriangular" | custom-call | tf_op jit(solution)/shard_map/jit(cholesky)/cholesky | solution.py:68
  444.4 0.3 constant_dynamic-update-slice_fusion
  444.8 0.3 convolution_subtract_fusion.3
  445.1 11.7 %cholesky.217 = f32[128,128]{1,0:T(8,128)S(1)} custom-call(f32[128,128]{1,0:T(8,128)S(1)} %cholesky.270), custom_call_target="Cholesky" | custom-call | tf_op jit(solution)/shard_map/jit(cholesky)/cholesky | solution.py:68
  456.9 10.0 %custom-call.31 = f32[1,128,128]{1,2,0:T(8,128)S(1)} custom-call(f32[1,128,128]{2,1,0:T(8,128)S(1)} %get-tuple-element.26), custom_call_target="InvertDiagBlocksLowerTriangular" | custom-call | tf_op jit(solution)/shard_map/jit(cholesky)/cholesky | solution.py:68
  466.9 0.3 convolution_dynamic-update-slice_fusion
  467.1 0.4 convolution_subtract_fusion.4
  467.5 11.7 %cholesky.238 = f32[128,128]{1,0:T(8,128)S(1)} custom-call(f32[128,128]{1,0:T(8,128)S(1)} %cholesky.275), custom_call_target="Cholesky" | custom-call | tf_op jit(solution)/shard_map/jit(cholesky)/cholesky | solution.py:68
  479.3 0.7 compare_reduce_fusion.1
  480.0 9.8 %custom-call.32 = f32[1,128,128]{1,2,0:T(8,128)S(1)} custom-call(f32[1,128,128]{2,1,0:T(8,128)S(1)} %get-tuple-element.23), custom_call_target="InvertDiagBlocksLowerTriangular" | custom-call | tf_op jit(solution)/shard_map/jit(cholesky)/cholesky | solution.py:68
  489.8 0.2 convolution_dynamic-update-slice_fusion.1
  490.0 0.4 convolution_subtract_fusion.5
  490.4 11.7 %cholesky.255 = f32[128,128]{1,0:T(8,128)S(1)} custom-call(f32[128,128]{1,0:T(8,128)S(1)} %convolution_subtract_fusion.5), custom_call_target="Cholesky" | custom-call | tf_op jit(solution)/shard_map/jit(cholesky)/cholesky | solution.py:68
  502.1 0.7 compare_reduce_fusion
  502.9 0.7 compare_reduce_fusion.2
  506.6 10.9 %while.1 = (s32[]{:T(128)}, f32[512,512]{1,0:T(8,128)S(1)}, s32[4,2]{0,1:T(2,128)S(1)}, f32[4,128,128]{2,1,0:T(8,128)}, s32[]{:T(128)}) while((s32[]{:T(128)}, f32[512,512]{1,0:T(8,128)S(1)}, s32[4,2]{0,1:T(2,128)S(1)}, f32[4,128,128]{2,1,0:T(8,128)}, s32[]{:T(128)}) %tuple.34), condition=%wide.while_cond, body=%wide.while_body.sunk | while | flops 2 | bytes 132705 | solution.py:69
  506.7 0.6 fusion.60
  507.3 2.0 bitcast_dynamic-update-slice_fusion.2
  509.4 0.6 fusion.60
  510.0 2.0 bitcast_dynamic-update-slice_fusion.2
  512.2 0.6 fusion.60
  512.8 2.0 bitcast_dynamic-update-slice_fusion.2
  514.9 0.6 fusion.60
  515.5 2.0 bitcast_dynamic-update-slice_fusion.2
  517.5 40.1 %custom-call.33 = f32[4,128,128]{1,2,0:T(8,128)S(1)} custom-call(f32[4,128,128]{2,1,0:T(8,128)} %get-tuple-element.9), custom_call_target="InvertDiagBlocksLowerTriangular" | custom-call | tf_op jit(solution)/shard_map/triangular_solve | solution.py:69
  557.7 0.4 fusion.45
  558.0 0.4 convolution_subtract_fusion.1
  558.4 0.4 fusion.46
  558.8 0.6 convolution_subtract_fusion
  559.4 0.4 fusion.47
  559.8 0.8 convolution_subtract_fusion.2
  560.6 0.4 convolution_convert_fusion
  561.5 22.8 %bitcast_multiply_fusion = f32[512,13312]{1,0:T(8,128)} fusion(bf16[13312,128,4]{1,0,2:T(8,128)(2,1)} %bitcast.90, bf16[4,128,128]{1,2,0:T(8,128)(2,1)S(1)} %copy.28, bf16[4,128,128]{1,2,0:T(8,128)(2,1)S(1)} %copy.27, bf16[4,128,128]{1,2,0:T(8,128)(2,1)S(1)} %copy.26, bf16[4,128,128]{1,2,0:T(8,128)(2,1)S(1)} %copy.25), kind=kOutput, calls=%fused_computation.5 | convolution fusion | flops 6988234752 | bytes 41418752 | tf_op jit(solution)/shard_map/pir,pcij->rcj/dot_general | solution.py:78
  584.3 0.8 fusion.25
  585.1 145.7 %reduce-scatter.2.cloned.1.call-done = f32[16,13312]{1,0:T(8,128)} async-done(((f32[512,13312]{1,0:T(8,128)}), f32[16,13312]{1,0:T(8,128)}) %reduce-scatter.2.cloned.1.call-update) | async-done | bytes 851984 | tf_op jit(solution)/shard_map/reduce_scatter | solution.py:81
  (40 shorter events, 1.5 us)
Async XLA Ops:
  11.5 35.8 %all-to-all-start = ((s32[128,1,2]{2,1,0:T(1,128)}), s32[128,1,2]{2,1,0:T(1,128)S(1)}, u32[]{:S(2)}, u32[]{:S(2)}) async-start(s32[128,1,2]{2,1,0:T(1,128)} %bitcast.3), calls=%async_computation | async-start | bytes 131072 | tf_op jit(solution)/shard_map/all_to_all | solution.py:42
  47.3 118.4 %all-to-all-start.1 = ((bf16[128,2,128,128]{3,2,1,0:T(8,128)(2,1)}), bf16[128,2,128,128]{3,2,1,0:T(8,128)(2,1)}, u32[]{:S(2)}, u32[]{:S(2)}) async-start(bf16[128,2,128,128]{3,2,1,0:T(8,128)(2,1)} %bitcast.91), calls=%async_computation.1 | async-start | bytes 16777216 | tf_op jit(solution)/shard_map/all_to_all | solution.py:35
  57.6 252.1 %all-reduce.4.cloned.1.call-start = ((), (), s32[]{:S(2)}) async-start(), calls=%async_computation.3 | async-start | bytes 2097152 | tf_op jit(solution)/shard_map/psum | solution.py:63
  239.4 17.7 %slice-start = ((s8[13631488]{0:T(1024)(128)(4,1)}), s8[4194304]{0:T(1024)(128)(4,1)S(1)}, s32[]{:S(2)}) async-start(s8[13631488]{0:T(1024)(128)(4,1)} %bitcast.100), calls=%async_computation.6 | async-start | bytes 8388608
  239.4 17.7 %slice-start.1 = ((s8[13631488]{0:T(1024)(128)(4,1)}), s8[4194304]{0:T(1024)(128)(4,1)S(1)}, s32[]{:S(2)}) async-start(s8[13631488]{0:T(1024)(128)(4,1)} %bitcast.100), calls=%async_computation.7 | async-start | bytes 8388608
  239.4 17.7 %slice-start.2 = ((s8[13631488]{0:T(1024)(128)(4,1)}), s8[4194304]{0:T(1024)(128)(4,1)S(1)}, s32[]{:S(2)}) async-start(s8[13631488]{0:T(1024)(128)(4,1)} %bitcast.100), calls=%async_computation.8 | async-start | bytes 8388608
  252.2 4.9 copy-start
  252.2 4.9 slice-start.3
  265.3 154.3 %all-reduce.6.cloned.1.call-start = ((), (), s32[]{:S(2)}) async-start(), calls=%async_computation.4 | async-start | bytes 2097152 | tf_op jit(solution)/shard_map/psum | solution.py:67
  314.2 416.7 %reduce-scatter.2.cloned.1.call-start = ((), (), s32[]{:S(2)}) async-start(), calls=%async_computation.5 | async-start | bytes 28114944 | tf_op jit(solution)/shard_map/reduce_scatter | solution.py:81
  331.9 225.7 %copy-start.1 = (f32[512,512]{1,0:T(8,128)S(1)}, f32[512,512]{1,0:T(8,128)}, u32[]{:S(2)}) copy-start(f32[512,512]{1,0:T(8,128)} %all-reduce.4.cloned.1.call-done) | copy-start | bytes 3145732
Sparse Core Ops, SparseCore 0:
  265.4 44.1 all-reduce.3
  314.3 105.2 all-reduce.5
  584.4 146.3 reduce-scatter.1
where the time goes:
time: 750 us; the launch traced here: 738 us
  waiting for transfers between devices  384 us (51%)
  other arithmetic  200 us (27%)
  local copies, waits for them, and re-layouts  74.1 us (10%)
  matrix products  40.5 us (5%)
  starting transfers between devices  21.5 us (3%)
  between operations  17.4 us (2%)
    reduce_scatter x1, waiting for transfers between devices, on_device(): lax.psum_scatter(product.reshape(rank_width // row_devices * lax.axis_siz...  146 us
    all_to_all x1, waiting for transfers between devices, on_device(): lax.all_to_all(send_blocks.reshape(devices_all, capacity, block_edge, blo...  107 us
    psum x1, waiting for transfers between devices, on_device(): gram_sum = lax.psum(local_gram, 'rows')  87.7 us
    another operation x14, other arithmetic, on_device(): factor = jnp.linalg.cholesky(gram_sum / total_rows)  78.8 us
    scatter-add x1, other arithmetic, on_device(): summed = jnp.zeros((tile_slots, block_edge, block_edge), jnp.float32).at[...  49.9 us
    psum x1, waiting for transfers between devices, on_device(): sketch = lax.psum(partial_value, 'cols')  44.3 us
    another operation x4, other arithmetic, on_device(): lax.linalg.triangular_solve(factor, sketch, left_side=False, lower=True,...  41 us
    dot_general x1, matrix products, on_device(): jnp.einsum('pir,pcij->rcj', basis_blocks, dense_tile, preferred_element_t...  22.8 us
  transfers between devices with their start and end apart: 5, of which 4 were waited for; matrix products, arithmetic and copies ran while one was open for 6% of the time, Pallas kernels for 0%

commit v1 on v0

v1 whole, which is shorter than its diff:
```python
import functools
import math

import jax
import jax.numpy as jnp
from jax import lax
from jax.experimental import pallas as pl
from jax.experimental.pallas import tpu as pltpu
from jax.sharding import PartitionSpec as P

PBR = 4
TBC = 104
BLK = 128
HIGHEST = lax.Precision.HIGHEST
MIB = 1 << 20


def bucket_kernel(place_ref, blocks_ref, out_ref, sem):
    count = blocks_ref.shape[0]

    def issue(slot, carry):
        pltpu.make_async_copy(blocks_ref.at[slot], out_ref.at[place_ref[slot]], sem).start()
        return carry

    lax.fori_loop(0, count, issue, 0)
    pltpu.make_async_copy(blocks_ref, out_ref.at[pl.ds(0, count)], sem).wait()


def bucket(place, blocks, slots):
    return pl.pallas_call(
        bucket_kernel,
        grid_spec=pltpu.PrefetchScalarGridSpec(
            num_scalar_prefetch=1,
            grid=(),
            in_specs=[pl.BlockSpec(memory_space=pl.ANY)],
            out_specs=pl.BlockSpec(memory_space=pl.ANY),
            scratch_shapes=[pltpu.SemaphoreType.DMA],
        ),
        out_shape=jax.ShapeDtypeStruct((slots,) + blocks.shape[1:], blocks.dtype),
        cost_estimate=pl.CostEstimate(flops=0, bytes_accessed=2 * blocks.size * 2, transcendentals=0),
        name="bucket",
    )(place, blocks)


def tile_kernel(code_ref, got_hbm, omega_hbm, tile_hbm, sketch_ref, got, omega, tile, total, sems):
    slots = got.shape[0]
    rows, cols = tile.shape
    get_blocks = pltpu.make_async_copy(got_hbm, got, sems.at[0])
    get_omega = pltpu.make_async_copy(omega_hbm, omega, sems.at[1])
    get_blocks.start()
    get_omega.start()

    def clear(step, carry):
        tile[pl.ds(pl.multiple_of(step * 16, 16), 16), :] = jnp.zeros((16, cols), tile.dtype)
        return carry

    lax.fori_loop(0, rows // 16, clear, 0)
    get_blocks.wait()

    def insert(step, carry):
        code = code_ref[step]
        slot = code & 255
        row = pl.multiple_of(((code >> 8) & 3) * BLK, BLK)
        col = pl.multiple_of(((code >> 10) & 127) * BLK, BLK)
        again = (code >> 17) & 1
        later = (code >> 18) & 1

        @pl.when(again == 0)
        def _():
            tile[pl.ds(row, BLK), pl.ds(col, BLK)] = got[slot]

        @pl.when(again == 1)
        def _():
            @pl.when(later == 0)
            def _():
                total[...] = got[code_ref[step - 1] & 255].astype(jnp.float32)

            value = total[...] + got[slot].astype(jnp.float32)
            total[...] = value
            tile[pl.ds(row, BLK), pl.ds(col, BLK)] = value.astype(tile.dtype)

        return carry

    lax.fori_loop(0, code_ref[slots], insert, 0)
    put_tile = pltpu.make_async_copy(tile, tile_hbm, sems.at[2])
    put_tile.start()
    get_omega.wait()
    sketch_ref[...] = jnp.zeros_like(sketch_ref)
    depth = 1024

    def multiply(step, carry):
        at = pl.ds(pl.multiple_of(step * depth, depth), depth)
        sketch_ref[...] += jnp.dot(tile[:, at], omega[at, :], preferred_element_type=jnp.float32)
        return carry

    lax.fori_loop(0, cols // depth, multiply, 0)
    put_tile.wait()


def tile_and_sketch(code, got, omega, rows, cols):
    slots, rank = got.shape[0], omega.shape[1]
    return pl.pallas_call(
        tile_kernel,
        grid_spec=pltpu.PrefetchScalarGridSpec(
            num_scalar_prefetch=1,
            grid=(),
            in_specs=[pl.BlockSpec(memory_space=pl.ANY)] * 2,
            out_specs=[
                pl.BlockSpec(memory_space=pl.ANY),
                pl.BlockSpec(memory_space=pltpu.VMEM),
            ],
            scratch_shapes=[
                pltpu.VMEM((slots, BLK, BLK), jnp.bfloat16),
                pltpu.VMEM((cols, rank), jnp.bfloat16),
                pltpu.VMEM((rows, cols), jnp.bfloat16),
                pltpu.VMEM((BLK, BLK), jnp.float32),
                pltpu.SemaphoreType.DMA((3,)),
            ],
        ),
        out_shape=[
            jax.ShapeDtypeStruct((rows, cols), jnp.bfloat16),
            jax.ShapeDtypeStruct((rows, rank), jnp.float32),
        ],
        compiler_params=pltpu.CompilerParams(vmem_limit_bytes=52 * MIB),
        cost_estimate=pl.CostEstimate(
            flops=2 * rows * cols * rank,
            bytes_accessed=2 * (got.size + omega.size + rows * cols),
            transcendentals=0,
        ),
        name="tile_and_sketch",
    )(code, got, omega)


def factor_kernel(scale, gram_ref, out_ref, work):
    n = gram_ref.shape[0]
    work[...] = gram_ref[...] * scale
    row = lax.broadcasted_iota(jnp.int32, (n, n), 0)
    lane = lax.broadcasted_iota(jnp.int32, (n, n), 1)
    out_ref[...] = jnp.where(row == lane, 1.0, 0.0)
    sub = lax.broadcasted_iota(jnp.int32, (8, BLK), 0)
    lane8 = lax.broadcasted_iota(jnp.int32, (8, BLK), 1)
    groups = BLK // 8

    def block(k, carry):
        at = pl.ds(pl.multiple_of(k * BLK, BLK), BLK)
        left = [work[pl.ds(pl.multiple_of(k * BLK + 8 * g, 8), 8), at] for g in range(groups)]
        right = [jnp.where(lane8 == sub + 8 * g, 1.0, 0.0) for g in range(groups)]
        for j in range(BLK):
            g0, s0 = divmod(j, 8)
            columns = [
                jnp.broadcast_to(left[g][:, j : j + 1], (8, BLK)) for g in range(g0, groups)
            ]
            inverse = 1.0 / columns[0][s0 : s0 + 1, :]
            pivot_left = left[g0][s0 : s0 + 1, :] * inverse
            pivot_right = right[g0][s0 : s0 + 1, :] * inverse
            for g in range(g0, groups):
                column = columns[g - g0]
                if g == g0:
                    column = jnp.where(sub > s0, column, 0.0)
                left[g] = left[g] - column * pivot_left
                right[g] = right[g] - column * pivot_right
        halves = []
        for g in range(groups):
            pivot = jnp.sum(
                jnp.where(lane8 == sub + 8 * g, left[g], 0.0), axis=1, keepdims=True
            )
            halves.append(right[g] * (1.0 / jnp.sqrt(pivot)))
        inverse_block = jnp.concatenate(halves, axis=0)
        both = jnp.concatenate([work[at, :], out_ref[at, :]], axis=1)
        upper = jnp.dot(inverse_block, both, precision=HIGHEST, preferred_element_type=jnp.float32)
        lanes = lax.broadcasted_iota(jnp.int32, (BLK, n), 1)
        later = jnp.where(lanes >= (k + 1) * BLK, upper[:, :n], 0.0)
        change = lax.dot_general(
            later, upper, (((0,), (0,)), ((), ())), precision=HIGHEST, preferred_element_type=jnp.float32
        )
        work[...] -= change[:, :n]
        out_ref[...] -= change[:, n:]
        out_ref[at, :] = upper[:, n:]
        return carry

    lax.fori_loop(0, n // BLK, block, 0)


def inverse_factor(gram, scale):
    n = gram.shape[0]
    return pl.pallas_call(
        functools.partial(factor_kernel, scale),
        in_specs=[pl.BlockSpec(memory_space=pltpu.VMEM)],
        out_specs=pl.BlockSpec(memory_space=pltpu.VMEM),
        out_shape=jax.ShapeDtypeStruct((n, n), jnp.float32),
        scratch_shapes=[pltpu.VMEM((n, n), jnp.float32)],
        compiler_params=pltpu.CompilerParams(vmem_limit_bytes=24 * MIB),
        cost_estimate=pl.CostEstimate(
            flops=1 << 35, bytes_accessed=2 * n * n * 4, transcendentals=0
        ),
        name="inverse_factor",
    )(gram)


def product_kernel(left_ref, own_ref, other_ref, out_ref):
    rows = own_ref.shape[0]
    own, other = own_ref[...], other_ref[...]
    total = None
    for part in range(4):
        term = jnp.dot(
            left_ref[:, part * rows : (part + 1) * rows],
            own if part % 2 == 0 else other,
            preferred_element_type=jnp.float32,
        )
        total = term if total is None else total + term
    out_ref[0] = total


def product(left, own, other, chunks, width):
    rows, cols = own.shape
    half = left.shape[0]
    pair = 2 * cols // chunks
    step = pair // BLK // 2 * BLK

    def start(k):
        return pl.multiple_of((k // 2) * pair + (k % 2) * step, BLK)

    spec = pl.BlockSpec((pl.Element(rows), pl.Element(width)), lambda k: (0, start(k)))
    return pl.pallas_call(
        product_kernel,
        grid=(chunks,),
        in_specs=[pl.BlockSpec((half, 4 * rows), lambda k: (0, 0)), spec, spec],
        out_specs=pl.BlockSpec((1, half, width), lambda k: (k, 0, 0)),
        out_shape=jax.ShapeDtypeStruct((chunks, half, width), jnp.float32),
        compiler_params=pltpu.CompilerParams(vmem_limit_bytes=40 * MIB),
        cost_estimate=pl.CostEstimate(
            flops=2 * half * 4 * rows * chunks * width,
            bytes_accessed=4 * rows * cols + 4 * chunks * half * width,
            transcendentals=0,
        ),
        name="product",
    )(left, own, other)


def on_device(blocks, owner, block_pos, omega):
    slot_count = blocks.shape[0]
    rank = omega.shape[1]
    row_devices = lax.axis_size("rows")
    col_devices = lax.axis_size("cols")
    devices_all = row_devices * col_devices
    everywhere = ("rows", "cols")
    capacity = max(2, 2 * slot_count // devices_all)
    slots = devices_all * capacity
    panel, cols = PBR * BLK, TBC * BLK
    total_rows = panel * row_devices
    core = lax.axis_index("rows") % 2
    swap = [(i, i ^ 1) for i in range(row_devices)]

    target = owner[:, 0]
    numbers = jnp.arange(slot_count, dtype=jnp.int32)
    same = (target[:, None] == target[None, :]) & (numbers[None, :] < numbers[:, None])
    place = target * capacity + jnp.sum(same.astype(jnp.int32), axis=1)
    spots = jnp.arange(slots, dtype=jnp.int32)
    hit = place[None, :] == spots[:, None]
    send_where = jnp.sum(jnp.where(hit, block_pos[None, :] + 1, 0), axis=1)
    send_blocks = bucket(place, blocks, slots)
    got_blocks = lax.all_to_all(
        send_blocks.reshape(devices_all, capacity, BLK, BLK), everywhere, 0, 0, tiled=True
    ).reshape(slots, BLK, BLK)
    got_where = lax.all_to_all(
        send_where.reshape(devices_all, capacity), everywhere, 0, 0, tiled=True
    ).reshape(slots)

    key = jnp.where(got_where == 0, PBR * TBC, got_where - 1)
    before = (key[None, :] < key[:, None]) | (
        (key[None, :] == key[:, None]) & (spots[None, :] < spots[:, None])
    )
    order = jnp.sum(before.astype(jnp.int32), axis=1)
    packed = key * slots + spots
    ordered = jnp.sum(jnp.where(order[None, :] == spots[:, None], packed[None, :], 0), axis=1)
    slot, where = ordered % slots, ordered // slots
    again = jnp.concatenate([jnp.zeros((1,), jnp.int32), (where[1:] == where[:-1]).astype(jnp.int32)])
    later = jnp.concatenate([jnp.zeros((1,), jnp.int32), again[:-1]])
    code = slot + (where // TBC) * 256 + (where % TBC) * 1024 + (again << 17) + (later << 18)
    filled = jnp.sum((key < PBR * TBC).astype(jnp.int32))
    code = jnp.concatenate([code, filled[None]])

    tile, part = tile_and_sketch(code, got_blocks, omega, panel, cols)
    other_tile = lax.ppermute(tile, "rows", swap)

    share = panel // col_devices
    parts = lax.all_to_all(part.reshape(col_devices, share, rank), "cols", 0, 0, tiled=True)
    own_share = jnp.sum(parts, axis=0)
    local_gram = lax.dot_general(
        own_share, own_share, (((0,), (0,)), ((), ())), precision=HIGHEST, preferred_element_type=jnp.float32
    )
    grams = lax.all_to_all(
        local_gram.reshape(devices_all, rank // devices_all, rank), everywhere, 0, 0, tiled=True
    )
    gram_rows = jnp.sum(grams, axis=0)
    gram = lax.all_to_all(
        jnp.broadcast_to(gram_rows[None], (devices_all,) + gram_rows.shape), everywhere, 0, 0, tiled=True
    ).reshape(rank, rank)
    inverse = inverse_factor(gram, 1.0 / total_rows)

    sketch = lax.all_to_all(
        jnp.broadcast_to(own_share[None], (col_devices, share, rank)), "cols", 0, 0, tiled=True
    ).reshape(panel, rank)
    half = rank // 2
    mine = lax.dynamic_slice_in_dim(sketch, core * half, half, 1)
    theirs = lax.ppermute(lax.dynamic_slice_in_dim(sketch, (1 - core) * half, half, 1), "rows", swap)
    both = jnp.concatenate([mine, theirs], axis=0).T
    high = lax.reduce_precision(both, 8, 7)
    left = jnp.concatenate([high, both - high], axis=1).astype(jnp.bfloat16)

    chips = row_devices // 2
    width = -(-TBC // chips) * BLK
    terms = product(left, tile, other_tile, chips, width)
    groups = [[2 * i + c for i in range(chips)] for c in range(2)]
    summed = lax.psum_scatter(
        terms.reshape(chips * half, width), "rows", scatter_dimension=0, axis_index_groups=groups, tiled=True
    )
    quarter = width // BLK // 2 * BLK
    take = width - quarter
    kept = lax.dynamic_slice_in_dim(summed, core * quarter, take, 1)
    come = lax.ppermute(
        lax.dynamic_slice_in_dim(summed, (1 - core) * quarter, take, 1), "rows", swap
    )
    columns = jnp.where(
        core == 0, jnp.concatenate([kept, come], axis=0), jnp.concatenate([come, kept], axis=0)
    )
    solved = jnp.dot(
        inverse * (1.0 / math.sqrt(total_rows)), columns, precision=HIGHEST, preferred_element_type=jnp.float32
    )
    ranks = rank // row_devices
    pieces = lax.all_to_all(
        solved.reshape(row_devices, ranks, take), "rows", 0, 0, tiled=True
    ).reshape(row_devices // 4, 4, ranks, take)
    overlap = 4 * take - 4 * cols // row_devices
    skip = overlap // 3
    run = jnp.concatenate(
        [pieces[:, 0]] + [pieces[:, i, :, skip:] for i in range(1, 4)], axis=2
    )
    coefficients = run.transpose(1, 0, 2).reshape(ranks, cols)

    slice_width = rank // col_devices
    my_rows = lax.dynamic_slice_in_dim(inverse, lax.axis_index("cols") * slice_width, slice_width, 0)
    basis = lax.dot_general(
        sketch, my_rows, (((1,), (1,)), ((), ())), precision=HIGHEST, preferred_element_type=jnp.float32
    ).astype(jnp.bfloat16)
    return basis, coefficients


def solution(mesh):
    in_specs = (
        P(("rows", "cols"), None, None),
        P(("rows", "cols"), None),
        P(("rows", "cols")),
        P("cols", None),
    )
    out_specs = (P("rows", "cols"), P("rows", "cols"))
    return jax.shard_map(
        on_device, mesh=mesh, in_specs=in_specs, out_specs=out_specs, check_vma=False
    )
```

time: 750 us -> 564 us (0.75); the launches traced: 738 us -> 562 us
  Pallas kernels: 0 us -> 225 us
  other arithmetic: 200 us -> 4.46 us
  waiting for transfers between devices: 384 us -> 213 us
  local copies, waits for them, and re-layouts: 74.1 us -> 7.35 us
  blocking collectives: 0 us -> 55.8 us
  matrix products: 40.5 us -> 6.33 us
  starting transfers between devices: 21.5 us -> 35 us
    pallas_call x0 -> x4, Pallas kernels: none -> 225 us  [the longest x1 129 us: bucket(): pl.pallas_call(bucket_kernel, grid_spec=pltpu.PrefetchScalarGridSpec(num_...]
    psum x2 -> x0, waiting for transfers between devices: 132 us -> none  [the longest x1 87.7 us: on_device(): gram_sum = lax.psum(local_gram, 'rows')]
    another operation x19 -> x1, other arithmetic: 120 us -> 0.19 us  [the longest x14 78.8 us: on_device(): factor = jnp.linalg.cholesky(gram_sum / total_rows)]
    reduce_scatter x1, waiting for transfers between devices: 146 us -> 46 us  [on_device(): lax.psum_scatter(terms.reshape(chips * half, width), 'rows', scatter_dime...]
    all_to_all x2 -> x5, waiting for transfers between devices: 107 us -> 165 us  [the longest x1 106 us: on_device(): lax.all_to_all(send_blocks.reshape(devices_all, capacity, BLK, BLK), ever...]
    all_to_all x0 -> x2, blocking collectives: none -> 55.8 us  [the longest x1 37.4 us: on_device(): lax.all_to_all(local_gram.reshape(devices_all, rank // devices_all, rank)...]
    scatter-add x1 -> x0, other arithmetic: 49.9 us -> none  [on_device(): summed = jnp.zeros((tile_slots, block_edge, block_edge), jnp.float32).at[...]
    dot_general x3, matrix products: 35.4 us -> 6.33 us  [the longest x1 2.88 us: on_device(): jnp.dot(inverse * (1.0 / math.sqrt(total_rows)), columns, precision=HIGHE...]
  transfers between devices with their start and end apart: 5 -> 9, of which waited for: 4 -> 6; matrix products, arithmetic and copies ran while one was open for 6% -> 2% of each run, Pallas kernels for 0% -> 32%
where the time goes in v1:
time: 564 us; the launch traced here: 562 us
  Pallas kernels  225 us (40%)
  waiting for transfers between devices  213 us (38%)
  blocking collectives  55.8 us (10%)
  starting transfers between devices  35 us (6%)
  between operations  14.3 us (3%)
  local copies, waits for them, and re-layouts  7.35 us (1%)
  matrix products  6.33 us (1%)
    pallas_call x1, Pallas kernels, bucket(): pl.pallas_call(bucket_kernel, grid_spec=pltpu.PrefetchScalarGridSpec(num_...  129 us
    all_to_all x1, waiting for transfers between devices, on_device(): lax.all_to_all(send_blocks.reshape(devices_all, capacity, BLK, BLK), ever...  106 us
    pallas_call x1, Pallas kernels, inverse_factor(): pl.pallas_call(functools.partial(factor_kernel, scale), in_specs=[pl.Bloc...  52.3 us
    reduce_scatter x1, waiting for transfers between devices, on_device(): lax.psum_scatter(terms.reshape(chips * half, width), 'rows', scatter_dime...  46 us
    all_to_all x1, blocking collectives, on_device(): lax.all_to_all(local_gram.reshape(devices_all, rank // devices_all, rank)...  37.4 us
    all_to_all x1, waiting for transfers between devices, on_device(): lax.all_to_all(jnp.broadcast_to(gram_rows[None], (devices_all,) + gram_ro...  30.5 us
    pallas_call x1, Pallas kernels, product(): pl.pallas_call(product_kernel, grid=(chunks,), in_specs=[pl.BlockSpec((ha...  27.1 us
    all_to_all x1, blocking collectives, on_device(): lax.all_to_all(part.reshape(col_devices, share, rank), 'cols', 0, 0, tile...  18.4 us
  transfers between devices with their start and end apart: 9, of which 6 were waited for; matrix products, arithmetic and copies ran while one was open for 2% of the time, Pallas kernels for 32%

profile of v1, /device:TPU:0, one launch (start us, length us, event | category | flops | bytes accessed | tf_op | source)
XLA Modules:
  0.0 562.0 jit_solution(10870624996833470871)
XLA Ops:
  7.2 0.9 convert_reduce_fusion.1
  8.1 0.7 multiply_add_fusion
  8.8 0.0 copy-start
  8.8 0.1 select_reduce_fusion.1
  8.9 0.8 all_to_all.24
  9.6 11.1 %all-to-all-start = ((s32[128,1,2]{2,1,0:T(1,128)}), s32[128,1,2]{2,1,0:T(1,128)S(1)}, u32[]{:S(2)}, u32[]{:S(2)}) async-start(s32[128,1,2]{2,1,0:T(1,128)} %bitcast.1), calls=%async_computation | async-start | bytes 131072 | tf_op jit(solution)/shard_map/all_to_all | solution.py:265
  20.8 0.0 copy-done
  20.8 128.8 %bucket.1 = bf16[256,128,128]{2,1,0:T(8,128)(2,1)} custom-call(s32[128]{0:T(128)} %copy-done, bf16[128,128,128]{2,1,0:T(8,128)(2,1)} %blocks_ref.1), custom_call_target="tpu_custom_call" | custom-call | bytes 8388608 | tf_op jit(solution)/shard_map/bucket/pallas_call | solution.py:30
  149.6 0.0 all-to-all-done
  149.7 10.3 %all-to-all-start.1 = ((bf16[128,2,128,128]{3,2,1,0:T(8,128)(2,1)}), bf16[128,2,128,128]{3,2,1,0:T(8,128)(2,1)}, u32[]{:S(2)}, u32[]{:S(2)}) async-start(bf16[128,2,128,128]{3,2,1,0:T(8,128)(2,1)} %bitcast.47), calls=%async_computation.1 | async-start | bytes 16777216 | tf_op jit(solution)/shard_map/all_to_all | solution.py:262
  160.0 0.9 fusion.26
  160.9 0.1 select_n.78
  161.0 0.2 convert_reduce_fusion
  161.2 0.1 select_reduce_fusion
  161.4 0.1 slice_compare_fusion
  161.4 0.1 add_convert_fusion
  161.5 0.1 fusion.23
  161.6 0.7 pad_add_fusion.code_ref
  162.3 105.8 %all-to-all-done.1 = bf16[128,2,128,128]{3,2,1,0:T(8,128)(2,1)} async-done(((bf16[128,2,128,128]{3,2,1,0:T(8,128)(2,1)}), bf16[128,2,128,128]{3,2,1,0:T(8,128)(2,1)}, u32[]{:S(2)}, u32[]{:S(2)}) %all-to-all-start.1) | async-done | bytes 8388640 | tf_op jit(solution)/shard_map/all_to_all | solution.py:262
  268.0 17.1 %tile_and_sketch.1 = (bf16[512,13312]{1,0:T(8,128)(2,1)}, f32[512,512]{1,0:T(8,128)S(1)}) custom-call(s32[257]{0:T(512)S(1)} %pad_add_fusion.code_ref, bf16[256,128,128]{2,1,0:T(8,128)(2,1)} %bitcast.4.got_hbm, bf16[13312,512]{1,0:T(8,128)(2,1)} %omega_hbm.1), custom_call_target="tpu_custom_call" | custom-call | flops 6979321856 | bytes 35651584 | tf_op jit(solution)/shard_map/tile_and_sketch/pallas_call | solution.py:102
  285.2 0.1 collective-permute-start.1
  285.3 18.4 %all_to_all.39 = f32[4,128,512]{2,1,0:T(8,128)S(1)} all-to-all(f32[4,128,512]{2,1,0:T(8,128)S(1)} %bitcast.46), channel_id=1, replica_groups=mesh['rows'=32,'cols'=4] {'cols'}, dimensions={0} | all-to-all | bytes 2097152 | tf_op jit(solution)/shard_map/all_to_all | solution.py:287
  303.7 0.1 reduce_sum.68
  303.8 0.1 copy.28
  303.9 1.1 broadcast_in_dim.40
  305.0 3.5 all-to-all-start.3
  308.5 0.0 reduce-scatter.2.cloned.1.call-start
  308.6 14.8 %all-to-all-done.3 = f32[4,128,512]{1,2,0:T(8,128)S(1)} async-done(((f32[4,128,512]{1,2,0:T(8,128)}), f32[4,128,512]{1,2,0:T(8,128)S(1)}, u32[]{:S(2)}, u32[]{:S(2)}) %all-to-all-start.3) | async-done | bytes 1048608 | tf_op jit(solution)/shard_map/all_to_all | solution.py:301
  323.4 0.1 copy_bitcast_fusion
  323.6 0.1 constant_dynamic-slice_fusion.3
  323.7 0.1 collective-permute-start
  323.7 1.9 collective-permute-done
  325.6 0.2 reduce-precision_convert_fusion
  325.8 0.1 pad_maximum_fusion.left_ref
  325.9 0.0 collective-permute-done.1.other_ref
  325.9 27.1 %product.1 = f32[16,256,896]{2,1,0:T(8,128)} custom-call(bf16[256,2048]{1,0:T(8,128)(2,1)S(1)} %pad_maximum_fusion.left_ref, bf16[512,13312]{1,0:T(8,128)(2,1)} %get-tuple-element.5.own_ref, bf16[512,13312]{1,0:T(8,128)(2,1)} %collective-permute-done.1.other_ref), custom_call_target="tpu_custom_call" | custom-call | flops 15032385536 | bytes 41943040 | tf_op jit(solution)/shard_map/product/pallas_call | solution.py:224
  353.0 0.0 reduce-scatter.2.cloned.1.call-update
  353.0 0.1 copy.30
  353.1 1.0 fusion.10
  354.1 0.7 copy.32
  354.8 37.4 %all_to_all.40 = f32[128,4,512]{2,1,0:T(4,128)S(1)} all-to-all(f32[128,4,512]{2,1,0:T(4,128)S(1)} %copy.32), channel_id=1, replica_groups=mesh['rows'=32,'cols'=4] {'rows','cols'}, dimensions={0} | all-to-all | bytes 2097152 | tf_op jit(solution)/shard_map/all_to_all | solution.py:292
  392.2 0.2 reduce_sum.69
  392.4 1.1 broadcast_in_dim.64
  393.5 4.6 all-to-all-start.5
  398.2 30.5 %all-to-all-done.5 = f32[128,4,512]{2,1,0:T(4,128)S(1)} async-done(((f32[128,4,512]{2,1,0:T(4,128)}), f32[128,4,512]{2,1,0:T(4,128)S(1)}, u32[]{:S(2)}, u32[]{:S(2)}) %all-to-all-start.5) | async-done | bytes 1048608 | tf_op jit(solution)/shard_map/all_to_all | solution.py:296
  428.7 0.4 reshape.104.gram_ref
  429.0 46.0 %reduce-scatter.2.cloned.1.call-done = f32[256,896]{1,0:T(8,128)} async-done(((f32[4096,896]{1,0:T(8,128)}), f32[256,896]{1,0:T(8,128)}) %reduce-scatter.2.cloned.1.call-update) | async-done | bytes 917520 | tf_op jit(solution)/shard_map/reduce_scatter | solution.py:315
  475.1 1.3 constant_dynamic-slice_fusion.1
  476.3 0.3 collective-permute-start.2
  476.6 52.3 %inverse_factor.1 = f32[512,512]{1,0:T(8,128)S(1)} custom-call(f32[512,512]{1,0:T(8,128)S(1)} %reshape.104.gram_ref), custom_call_target="tpu_custom_call" | custom-call | flops 34359738368 | bytes 2097152 | tf_op jit(solution)/shard_map/inverse_factor/pallas_call | solution.py:186
  528.9 0.0 collective-permute-done.2
  528.9 2.9 fusion.1
  531.8 5.0 all-to-all-start.6
  536.8 2.5 convolution_convert_fusion
  539.2 14.3 %all-to-all-done.6 = f32[32,16,512]{2,1,0:T(8,128)S(1)} async-done(((f32[32,16,512]{2,1,0:T(8,128)}), f32[32,16,512]{2,1,0:T(8,128)S(1)}, u32[]{:S(2)}, u32[]{:S(2)}) %all-to-all-start.6) | async-done | bytes 1048608 | tf_op jit(solution)/shard_map/all_to_all | solution.py:331
  553.6 0.1 fusion.27
  553.7 0.1 copy.52
  553.7 0.1 copy.53
  553.8 0.1 copy.54
  553.9 0.2 copy.51
  554.1 0.1 pad_maximum_fusion.1
  554.1 1.1 copy.42
  (3 shorter events, 0.0 us)
Async XLA Ops:
  8.8 12.0 %copy-start = (s32[128]{0:T(128)}, s32[128]{0:T(128)S(1)}, u32[]{:S(2)}) copy-start(s32[128]{0:T(128)S(1)} %get-tuple-element.17.place_ref) | copy-start | bytes 1540
  9.6 140.0 %all-to-all-start = ((s32[128,1,2]{2,1,0:T(1,128)}), s32[128,1,2]{2,1,0:T(1,128)S(1)}, u32[]{:S(2)}, u32[]{:S(2)}) async-start(s32[128,1,2]{2,1,0:T(1,128)} %bitcast.1), calls=%async_computation | async-start | bytes 131072 | tf_op jit(solution)/shard_map/all_to_all | solution.py:265
  149.7 118.4 %all-to-all-start.1 = ((bf16[128,2,128,128]{3,2,1,0:T(8,128)(2,1)}), bf16[128,2,128,128]{3,2,1,0:T(8,128)(2,1)}, u32[]{:S(2)}, u32[]{:S(2)}) async-start(bf16[128,2,128,128]{3,2,1,0:T(8,128)(2,1)} %bitcast.47), calls=%async_computation.1 | async-start | bytes 16777216 | tf_op jit(solution)/shard_map/all_to_all | solution.py:262
  285.2 40.8 %collective-permute-start.1 = (bf16[512,13312]{1,0:T(8,128)(2,1)}, bf16[512,13312]{1,0:T(8,128)(2,1)}, u32[]{:S(2)}, u32[]{:S(2)}) collective-permute-start(bf16[512,13312]{1,0:T(8,128)(2,1)} %get-tuple-element.5.own_ref), channel_id=1, source_target_pairs={{0,4},{4,0},{8,12},{12,8},{16,20},{20,16},{24,28},{28,24},{32,36},... | collective-permute-start | bytes 40894472 | tf_op jit(solution)/shard_map/ppermute | solution.py:284
  305.0 18.4 %all-to-all-start.3 = ((f32[4,128,512]{1,2,0:T(8,128)}), f32[4,128,512]{1,2,0:T(8,128)S(1)}, u32[]{:S(2)}, u32[]{:S(2)}) async-start(f32[4,128,512]{1,2,0:T(8,128)} %broadcast_in_dim.40), calls=%async_computation.3 | async-start | bytes 2097152 | tf_op jit(solution)/shard_map/all_to_all | solution.py:301
  308.5 166.5 %reduce-scatter.2.cloned.1.call-start = ((), (), s32[]{:S(2)}) async-start(), calls=%async_computation.8 | async-start | bytes 15597568 | tf_op jit(solution)/shard_map/reduce_scatter | solution.py:315
  323.7 2.0 collective-permute-start
  393.5 35.2 %all-to-all-start.5 = ((f32[128,4,512]{2,1,0:T(4,128)}), f32[128,4,512]{2,1,0:T(4,128)S(1)}, u32[]{:S(2)}, u32[]{:S(2)}) async-start(f32[128,4,512]{2,1,0:T(4,128)} %broadcast_in_dim.64), calls=%async_computation.5 | async-start | bytes 2097152 | tf_op jit(solution)/shard_map/all_to_all | solution.py:296
  476.3 52.6 %collective-permute-start.2 = (f32[256,512]{1,0:T(8,128)S(1)}, f32[256,512]{1,0:T(8,128)S(1)}, u32[]{:S(2)}, u32[]{:S(2)}) collective-permute-start(f32[256,512]{1,0:T(8,128)S(1)} %get-tuple-element.16), channel_id=1, source_target_pairs={{0,4},{4,0},{8,12},{12,8},{16,20},{20,16},{24,28},{28,24},{32,36},... | collective-permute-start | bytes 1572872 | tf_op jit(solution)/shard_map/ppermute | solution.py:321
  531.8 21.8 %all-to-all-start.6 = ((f32[32,16,512]{2,1,0:T(8,128)}), f32[32,16,512]{2,1,0:T(8,128)S(1)}, u32[]{:S(2)}, u32[]{:S(2)}) async-start(f32[32,16,512]{2,1,0:T(8,128)} %bitcast.11), calls=%async_computation.7 | async-start | bytes 2097152 | tf_op jit(solution)/shard_map/all_to_all | solution.py:331
Sparse Core Ops, SparseCore 0:
  353.1 121.8 reduce-scatter.1

commit v2 on v1

--- a/solution.py
+++ b/solution.py
@@ -32,11 +32,12 @@
         grid_spec=pltpu.PrefetchScalarGridSpec(
             num_scalar_prefetch=1,
             grid=(),
-            in_specs=[pl.BlockSpec(memory_space=pl.ANY)],
+            in_specs=[pl.BlockSpec(memory_space=pltpu.VMEM)],
             out_specs=pl.BlockSpec(memory_space=pl.ANY),
             scratch_shapes=[pltpu.SemaphoreType.DMA],
         ),
         out_shape=jax.ShapeDtypeStruct((slots,) + blocks.shape[1:], blocks.dtype),
+        compiler_params=pltpu.CompilerParams(vmem_limit_bytes=56 * MIB),
         cost_estimate=pl.CostEstimate(flops=0, bytes_accessed=2 * blocks.size * 2, transcendentals=0),
         name="bucket",
     )(place, blocks)
@@ -141,24 +142,33 @@
     lane8 = lax.broadcasted_iota(jnp.int32, (8, BLK), 1)
     groups = BLK // 8
 
-    def block(k, carry):
-        at = pl.ds(pl.multiple_of(k * BLK, BLK), BLK)
-        left = [work[pl.ds(pl.multiple_of(k * BLK + 8 * g, 8), 8), at] for g in range(groups)]
+    def spread(value, j):
+        return jnp.broadcast_to(value[:, j : j + 1], (8, BLK))
+
+    def block(panel, carry):
+        at = pl.ds(pl.multiple_of(panel * BLK, BLK), BLK)
+        left = [work[pl.ds(pl.multiple_of(panel * BLK + 8 * g, 8), 8), at] for g in range(groups)]
         right = [jnp.where(lane8 == sub + 8 * g, 1.0, 0.0) for g in range(groups)]
-        for j in range(BLK):
-            g0, s0 = divmod(j, 8)
-            columns = [
-                jnp.broadcast_to(left[g][:, j : j + 1], (8, BLK)) for g in range(g0, groups)
-            ]
-            inverse = 1.0 / columns[0][s0 : s0 + 1, :]
-            pivot_left = left[g0][s0 : s0 + 1, :] * inverse
-            pivot_right = right[g0][s0 : s0 + 1, :] * inverse
-            for g in range(g0, groups):
-                column = columns[g - g0]
-                if g == g0:
-                    column = jnp.where(sub > s0, column, 0.0)
-                left[g] = left[g] - column * pivot_left
-                right[g] = right[g] - column * pivot_right
+        for g0 in range(groups):
+            own = [spread(left[g0], 8 * g0 + k) for k in range(8)]
+            factors, pivots_left, pivots_right = {}, [], []
+            for k in range(8):
+                inverse = 1.0 / own[k][k : k + 1, :]
+                for later in range(k + 1, 8):
+                    factors[k, later] = own[later][k : k + 1, :] * inverse
+                    own[later] = own[later] - own[k] * factors[k, later]
+                pivots_left.append(left[g0][k : k + 1, :] * inverse)
+                pivots_right.append(right[g0][k : k + 1, :] * inverse)
+                column = jnp.where(sub > k, own[k], 0.0)
+                left[g0] = left[g0] - column * pivots_left[k]
+                right[g0] = right[g0] - column * pivots_right[k]
+            for g in range(g0 + 1, groups):
+                below = [spread(left[g], 8 * g0 + k) for k in range(8)]
+                for k in range(8):
+                    for later in range(k + 1, 8):
+                        below[later] = below[later] - below[k] * factors[k, later]
+                    left[g] = left[g] - below[k] * pivots_left[k]
+                    right[g] = right[g] - below[k] * pivots_right[k]
         halves = []
         for g in range(groups):
             pivot = jnp.sum(
@@ -168,13 +178,17 @@
         inverse_block = jnp.concatenate(halves, axis=0)
         both = jnp.concatenate([work[at, :], out_ref[at, :]], axis=1)
         upper = jnp.dot(inverse_block, both, precision=HIGHEST, preferred_element_type=jnp.float32)
-        lanes = lax.broadcasted_iota(jnp.int32, (BLK, n), 1)
-        later = jnp.where(lanes >= (k + 1) * BLK, upper[:, :n], 0.0)
-        change = lax.dot_general(
-            later, upper, (((0,), (0,)), ((), ())), precision=HIGHEST, preferred_element_type=jnp.float32
-        )
-        work[...] -= change[:, :n]
-        out_ref[...] -= change[:, n:]
+
+        @pl.when(panel < n // BLK - 1)
+        def _():
+            lanes = lax.broadcasted_iota(jnp.int32, (BLK, n), 1)
+            later = jnp.where(lanes >= (panel + 1) * BLK, upper[:, :n], 0.0)
+            change = lax.dot_general(
+                later, upper, (((0,), (0,)), ((), ())), precision=HIGHEST, preferred_element_type=jnp.float32
+            )
+            work[...] -= change[:, :n]
+            out_ref[...] -= change[:, n:]
+
         out_ref[at, :] = upper[:, n:]
         return carry
 
@@ -199,38 +213,26 @@
 
 def product_kernel(left_ref, own_ref, other_ref, out_ref):
     rows = own_ref.shape[0]
-    own, other = own_ref[...], other_ref[...]
-    total = None
-    for part in range(4):
-        term = jnp.dot(
-            left_ref[:, part * rows : (part + 1) * rows],
-            own if part % 2 == 0 else other,
-            preferred_element_type=jnp.float32,
-        )
-        total = term if total is None else total + term
-    out_ref[0] = total
-
-
-def product(left, own, other, chunks, width):
+    total = jnp.dot(left_ref[:, :rows], own_ref[...], preferred_element_type=jnp.float32)
+    total += jnp.dot(left_ref[:, rows:], other_ref[...], preferred_element_type=jnp.float32)
+    out_ref[...] = total.astype(out_ref.dtype)
+
+
+def product(left, own, other, part, parts, width):
     rows, cols = own.shape
     half = left.shape[0]
-    pair = 2 * cols // chunks
-    step = pair // BLK // 2 * BLK
-
-    def start(k):
-        return pl.multiple_of((k // 2) * pair + (k % 2) * step, BLK)
-
-    spec = pl.BlockSpec((pl.Element(rows), pl.Element(width)), lambda k: (0, start(k)))
+    steps = cols // parts // width
+    spec = pl.BlockSpec((rows, width), lambda k: (0, part * steps + k))
     return pl.pallas_call(
         product_kernel,
-        grid=(chunks,),
-        in_specs=[pl.BlockSpec((half, 4 * rows), lambda k: (0, 0)), spec, spec],
-        out_specs=pl.BlockSpec((1, half, width), lambda k: (k, 0, 0)),
-        out_shape=jax.ShapeDtypeStruct((chunks, half, width), jnp.float32),
-        compiler_params=pltpu.CompilerParams(vmem_limit_bytes=40 * MIB),
+        grid=(steps,),
+        in_specs=[pl.BlockSpec((half, 2 * rows), lambda k: (0, 0)), spec, spec],
+        out_specs=pl.BlockSpec((half, width), lambda k: (0, k)),
+        out_shape=jax.ShapeDtypeStruct((half, cols // parts), jnp.bfloat16),
+        compiler_params=pltpu.CompilerParams(vmem_limit_bytes=56 * MIB),
         cost_estimate=pl.CostEstimate(
-            flops=2 * half * 4 * rows * chunks * width,
-            bytes_accessed=4 * rows * cols + 4 * chunks * half * width,
+            flops=2 * half * 2 * rows * cols // parts,
+            bytes_accessed=(4 * rows * cols + 2 * half * cols) // parts,
             transcendentals=0,
         ),
         name="product",
@@ -258,7 +260,7 @@
     spots = jnp.arange(slots, dtype=jnp.int32)
     hit = place[None, :] == spots[:, None]
     send_where = jnp.sum(jnp.where(hit, block_pos[None, :] + 1, 0), axis=1)
-    send_blocks = bucket(place, blocks, slots)
+    send_blocks, send_where = lax.optimization_barrier((bucket(place, blocks, slots), send_where))
     got_blocks = lax.all_to_all(
         send_blocks.reshape(devices_all, capacity, BLK, BLK), everywhere, 0, 0, tiled=True
     ).reshape(slots, BLK, BLK)
@@ -296,47 +298,35 @@
     gram = lax.all_to_all(
         jnp.broadcast_to(gram_rows[None], (devices_all,) + gram_rows.shape), everywhere, 0, 0, tiled=True
     ).reshape(rank, rank)
+    shares = [own_share] + [
+        lax.ppermute(own_share, "cols", [(i, (i + d) % col_devices) for i in range(col_devices)])
+        for d in range(1, col_devices)
+    ]
+    back = jnp.stack(shares[::-1] * 2)
+    start = col_devices - 1 - lax.axis_index("cols")
+    sketch = lax.dynamic_slice_in_dim(back, start, col_devices, 0).reshape(panel, rank)
+    other_sketch = lax.ppermute(sketch, "rows", swap)
     inverse = inverse_factor(gram, 1.0 / total_rows)
 
-    sketch = lax.all_to_all(
-        jnp.broadcast_to(own_share[None], (col_devices, share, rank)), "cols", 0, 0, tiled=True
-    ).reshape(panel, rank)
+    ranks = rank // row_devices
     half = rank // 2
-    mine = lax.dynamic_slice_in_dim(sketch, core * half, half, 1)
-    theirs = lax.ppermute(lax.dynamic_slice_in_dim(sketch, (1 - core) * half, half, 1), "rows", swap)
-    both = jnp.concatenate([mine, theirs], axis=0).T
-    high = lax.reduce_precision(both, 8, 7)
-    left = jnp.concatenate([high, both - high], axis=1).astype(jnp.bfloat16)
-
     chips = row_devices // 2
-    width = -(-TBC // chips) * BLK
-    terms = product(left, tile, other_tile, chips, width)
+    both = jnp.concatenate([sketch, other_sketch], axis=0)
+    my_ranks = lax.dynamic_index_in_dim(
+        inverse.reshape(chips, 2, ranks, rank), core, 1, keepdims=False
+    ).reshape(half, rank)
+    left = lax.dot_general(
+        my_ranks, both, (((1,), (1,)), ((), ())), precision=HIGHEST, preferred_element_type=jnp.float32
+    ).astype(jnp.bfloat16)
+
     groups = [[2 * i + c for i in range(chips)] for c in range(2)]
-    summed = lax.psum_scatter(
-        terms.reshape(chips * half, width), "rows", scatter_dimension=0, axis_index_groups=groups, tiled=True
-    )
-    quarter = width // BLK // 2 * BLK
-    take = width - quarter
-    kept = lax.dynamic_slice_in_dim(summed, core * quarter, take, 1)
-    come = lax.ppermute(
-        lax.dynamic_slice_in_dim(summed, (1 - core) * quarter, take, 1), "rows", swap
-    )
-    columns = jnp.where(
-        core == 0, jnp.concatenate([kept, come], axis=0), jnp.concatenate([come, kept], axis=0)
-    )
-    solved = jnp.dot(
-        inverse * (1.0 / math.sqrt(total_rows)), columns, precision=HIGHEST, preferred_element_type=jnp.float32
-    )
-    ranks = rank // row_devices
-    pieces = lax.all_to_all(
-        solved.reshape(row_devices, ranks, take), "rows", 0, 0, tiled=True
-    ).reshape(row_devices // 4, 4, ranks, take)
-    overlap = 4 * take - 4 * cols // row_devices
-    skip = overlap // 3
-    run = jnp.concatenate(
-        [pieces[:, 0]] + [pieces[:, i, :, skip:] for i in range(1, 4)], axis=2
-    )
-    coefficients = run.transpose(1, 0, 2).reshape(ranks, cols)
+    scaling = 1.0 / math.sqrt(total_rows)
+    halves = []
+    for part in range(2):
+        terms = product(left, tile, other_tile, part, 2, 512).reshape(chips, ranks, cols // 2)
+        terms = lax.all_to_all(terms, "rows", 0, 0, axis_index_groups=groups, tiled=True)
+        halves.append(jnp.sum(terms.astype(jnp.float32), axis=0) * scaling)
+    coefficients = jnp.concatenate(halves, axis=1)
 
     slice_width = rank // col_devices
     my_rows = lax.dynamic_slice_in_dim(inverse, lax.axis_index("cols") * slice_width, slice_width, 0)

time: 564 us -> 399 us (0.71)
  Pallas kernels: 225 us -> 69.6 us
  blocking collectives: 55.8 us -> 38.5 us
  between operations: 14.3 us -> 0.82 us
  starting transfers between devices: 35 us -> 44.8 us
  other arithmetic: 4.46 us -> 10.1 us
    pallas_call x1, Pallas kernels: 129 us -> 4.82 us  [bucket(): pl.pallas_call(bucket_kernel, grid_spec=pltpu.PrefetchScalarGridSpec(num_...]
    reduce_scatter x1 -> x0, waiting for transfers between devices: 46 us -> none  [on_device(): lax.psum_scatter(terms.reshape(chips * half, width), 'rows', scatter_dime...]
    all_to_all x3, waiting for transfers between devices: 29.2 us -> 74.5 us  [the longest x2 74.5 us: on_device(): lax.all_to_all(terms, 'rows', 0, 0, axis_index_groups=groups, tiled=True)]
    pallas_call x1, Pallas kernels: 52.3 us -> 20.8 us  [inverse_factor(): pl.pallas_call(functools.partial(factor_kernel, scale), in_specs=[pl.Bloc...]
    ppermute x2 -> x4, waiting for transfers between devices: 1.9 us -> 20.8 us  [the longest x3 20.8 us: on_device(): lax.ppermute(own_share, 'cols', [(i, (i + d) % col_devices) for i in rang...]
    all_to_all x1, blocking collectives: 37.4 us -> 20 us  [on_device(): lax.all_to_all(send_where.reshape(devices_all, capacity), everywhere, 0,...]
    all_to_all x1, waiting for transfers between devices: 30.5 us -> 14 us  [on_device(): lax.all_to_all(jnp.broadcast_to(gram_rows[None], (devices_all,) + gram_ro...]
    all_to_all x3, starting transfers between devices: 19.6 us -> 25.8 us  [the longest x2 16.5 us: on_device(): lax.all_to_all(terms, 'rows', 0, 0, axis_index_groups=groups, tiled=True)]
  transfers between devices with their start and end apart: 9 -> 10, of which waited for: 6 -> 6; matrix products, arithmetic and copies ran while one was open for 2% -> 6% of each run, Pallas kernels for 32% -> 9%
where the time goes in v2:
time: 399 us; the launch traced here: 398 us
  waiting for transfers between devices  215 us (54%)
  Pallas kernels  69.6 us (17%)
  starting transfers between devices  44.8 us (11%)
  blocking collectives  38.5 us (10%)
  local copies, waits for them, and re-layouts  12.3 us (3%)
  other arithmetic  10.1 us (3%)
  matrix products  6.56 us (2%)
    all_to_all x1, waiting for transfers between devices, on_device(): lax.all_to_all(send_blocks.reshape(devices_all, capacity, BLK, BLK), ever...  106 us
    all_to_all x2, waiting for transfers between devices, on_device(): lax.all_to_all(terms, 'rows', 0, 0, axis_index_groups=groups, tiled=True)  74.5 us
    pallas_call x2, Pallas kernels, product(): pl.pallas_call(product_kernel, grid=(steps,), in_specs=[pl.BlockSpec((hal...  26.8 us
    pallas_call x1, Pallas kernels, inverse_factor(): pl.pallas_call(functools.partial(factor_kernel, scale), in_specs=[pl.Bloc...  20.8 us
    ppermute x3, waiting for transfers between devices, on_device(): lax.ppermute(own_share, 'cols', [(i, (i + d) % col_devices) for i in rang...  20.8 us
    all_to_all x1, blocking collectives, on_device(): lax.all_to_all(send_where.reshape(devices_all, capacity), everywhere, 0,...  20 us
    all_to_all x1, blocking collectives, on_device(): lax.all_to_all(part.reshape(col_devices, share, rank), 'cols', 0, 0, tile...  18.4 us
    pallas_call x1, Pallas kernels, tile_and_sketch(): pl.pallas_call(tile_kernel, grid_spec=pltpu.PrefetchScalarGridSpec(num_sc...  17.1 us
  transfers between devices with their start and end apart: 10, of which 6 were waited for; matrix products, arithmetic and copies ran while one was open for 6% of the time, Pallas kernels for 9%

profile of v2, /device:TPU:0, one launch (start us, length us, event | category | flops | bytes accessed | tf_op | source)
XLA Modules:
  0.0 397.8 jit_solution(5623201235730070049)
XLA Ops:
  0.6 0.9 convert_reduce_fusion.3
  1.5 0.7 multiply_add_fusion
  2.2 0.0 copy-start
  2.2 0.1 select_reduce_fusion.1
  2.3 0.4 copy-done
  2.7 4.8 %bucket.1 = bf16[256,128,128]{2,1,0:T(8,128)(2,1)} custom-call(s32[128]{0:T(128)} %copy-done, bf16[128,128,128]{2,1,0:T(8,128)(2,1)} %blocks_ref.1), custom_call_target="tpu_custom_call" | custom-call | bytes 8388608 | tf_op jit(solution)/shard_map/bucket/pallas_call | solution.py:30
  7.6 0.1 all_to_all.24
  7.7 20.0 %all_to_all.39 = s32[128,1,2]{2,1,0:T(1,128)S(1)} all-to-all(s32[128,1,2]{2,1,0:T(1,128)S(1)} %bitcast.43), channel_id=1, replica_groups=mesh['rows'=32,'cols'=4] {'rows','cols'}, dimensions={0} | all-to-all | bytes 2048 | tf_op jit(solution)/shard_map/all_to_all | solution.py:267
  27.7 5.9 %all-to-all-start.1 = ((bf16[128,2,128,128]{3,2,1,0:T(8,128)(2,1)}), bf16[128,2,128,128]{3,2,1,0:T(8,128)(2,1)}, u32[]{:S(2)}, u32[]{:S(2)}) async-start(bf16[128,2,128,128]{3,2,1,0:T(8,128)(2,1)} %bitcast.34), calls=%async_computation.1 | async-start | bytes 16777216 | tf_op jit(solution)/shard_map/all_to_all | solution.py:264
  33.7 0.9 fusion.22
  34.6 0.1 select_n.65
  34.7 0.2 convert_reduce_fusion.2
  34.9 0.1 select_reduce_fusion
  35.1 0.1 slice_compare_fusion
  35.1 0.1 add_convert_fusion
  35.2 0.1 fusion.19
  35.3 0.7 pad_add_fusion.code_ref
  36.0 105.8 %all-to-all-done.1 = bf16[128,2,128,128]{3,2,1,0:T(8,128)(2,1)} async-done(((bf16[128,2,128,128]{3,2,1,0:T(8,128)(2,1)}), bf16[128,2,128,128]{3,2,1,0:T(8,128)(2,1)}, u32[]{:S(2)}, u32[]{:S(2)}) %all-to-all-start.1) | async-done | bytes 8388640 | tf_op jit(solution)/shard_map/all_to_all | solution.py:264
  141.7 17.1 %tile_and_sketch.1 = (bf16[512,13312]{1,0:T(8,128)(2,1)}, f32[512,512]{1,0:T(8,128)S(1)}) custom-call(s32[257]{0:T(512)S(1)} %pad_add_fusion.code_ref, bf16[256,128,128]{2,1,0:T(8,128)(2,1)} %bitcast.4.got_hbm, bf16[13312,512]{1,0:T(8,128)(2,1)} %omega_hbm.1), custom_call_target="tpu_custom_call" | custom-call | flops 6979321856 | bytes 35651584 | tf_op jit(solution)/shard_map/tile_and_sketch/pallas_call | solution.py:103
  158.9 0.1 collective-permute-start.4
  159.0 18.4 %all_to_all.40 = f32[4,128,512]{2,1,0:T(8,128)S(1)} all-to-all(f32[4,128,512]{2,1,0:T(8,128)S(1)} %bitcast.32), channel_id=1, replica_groups=mesh['rows'=32,'cols'=4] {'cols'}, dimensions={0} | all-to-all | bytes 2097152 | tf_op jit(solution)/shard_map/all_to_all | solution.py:289
  177.4 0.1 reduce_sum.86
  177.5 1.2 collective-permute-start
  178.7 0.1 copy.15
  178.9 1.0 fusion.7
  179.8 1.7 copy.17
  181.6 9.3 %all-to-all-start.3 = ((f32[128,4,512]{2,1,0:T(4,128)}), f32[128,4,512]{2,1,0:T(4,128)S(1)}, u32[]{:S(2)}, u32[]{:S(2)}) async-start(f32[128,4,512]{2,1,0:T(4,128)} %copy.17), calls=%async_computation.3 | async-start | bytes 2097152 | tf_op jit(solution)/shard_map/all_to_all | solution.py:294
  190.9 2.9 collective-permute-start.1
  193.8 0.8 collective-permute-start.2
  194.6 0.0 collective-permute-done
  194.6 0.7 bitcast_dynamic-update-slice_fusion.6
  195.4 16.7 %collective-permute-done.1 = f32[128,512]{1,0:T(8,128)S(1)} collective-permute-done((f32[128,512]{1,0:T(8,128)S(1)}, f32[128,512]{1,0:T(8,128)S(1)}, u32[]{:S(2)}, u32[]{:S(2)}) %collective-permute-start.1) | collective-permute-done | bytes 262176 | tf_op jit(solution)/shard_map/ppermute | solution.py:302
  212.0 0.7 bitcast_dynamic-update-slice_fusion.4
  212.8 4.1 %collective-permute-done.2 = f32[128,512]{1,0:T(8,128)S(1)} collective-permute-done((f32[128,512]{1,0:T(8,128)S(1)}, f32[128,512]{1,0:T(8,128)S(1)}, u32[]{:S(2)}, u32[]{:S(2)}) %collective-permute-start.2) | collective-permute-done | bytes 262176 | tf_op jit(solution)/shard_map/ppermute | solution.py:302
  216.9 0.7 bitcast_dynamic-update-slice_fusion.2
  217.6 0.7 bitcast_dynamic-update-slice_fusion
  218.4 0.0 all-to-all-done.3
  218.4 0.2 reduce_sum.87
  218.6 1.1 broadcast_in_dim.57
  219.7 7.7 %all-to-all-start.4 = ((f32[128,4,512]{2,1,0:T(4,128)}), f32[128,4,512]{2,1,0:T(4,128)}, u32[]{:S(2)}, u32[]{:S(2)}) async-start(f32[128,4,512]{2,1,0:T(4,128)} %broadcast_in_dim.57), calls=%async_computation.4 | async-start | bytes 2097152 | tf_op jit(solution)/shard_map/all_to_all | solution.py:298
  227.4 0.7 bitcast_dynamic-update-slice_fusion.7
  228.1 0.7 bitcast_dynamic-update-slice_fusion.5
  228.8 0.7 bitcast_dynamic-update-slice_fusion.3
  229.5 0.7 bitcast_dynamic-update-slice_fusion.1
  230.2 1.3 constant_dynamic-slice_fusion.1
  231.5 0.3 collective-permute-start.3
  231.8 14.0 %all-to-all-done.4 = f32[128,4,512]{2,1,0:T(4,128)} async-done(((f32[128,4,512]{2,1,0:T(4,128)}), f32[128,4,512]{2,1,0:T(4,128)}, u32[]{:S(2)}, u32[]{:S(2)}) %all-to-all-start.4) | async-done | bytes 1048608 | tf_op jit(solution)/shard_map/all_to_all | solution.py:298
  245.8 1.6 reshape.104.gram_ref
  247.4 20.8 %inverse_factor.1 = f32[512,512]{1,0:T(8,128)S(1)} custom-call(f32[512,512]{1,0:T(8,128)S(1)} %reshape.104.gram_ref), custom_call_target="tpu_custom_call" | custom-call | flops 34359738368 | bytes 2097152 | tf_op jit(solution)/shard_map/inverse_factor/pallas_call | solution.py:200
  268.3 0.0 collective-permute-done.3
  268.3 3.9 fusion.4.left_ref
  272.3 0.0 collective-permute-done.4.other_ref
  272.3 13.4 %product.3 = bf16[256,6656]{1,0:T(8,128)(2,1)} custom-call(bf16[256,1024]{1,0:T(8,128)(2,1)} %fusion.4.left_ref, bf16[512,13312]{1,0:T(8,128)(2,1)} %get-tuple-element.9.own_ref, bf16[512,13312]{1,0:T(8,128)(2,1)} %collective-permute-done.4.other_ref), custom_call_target="tpu_custom_call" | custom-call | flops 3489660928 | bytes 17039360 | tf_op jit(solution)/shard_map/product/pallas_call | solution.py:226
  285.7 4.5 %all-to-all-start.6 = ((bf16[16,16,6656]{2,1,0:T(8,128)(2,1)}), bf16[16,16,6656]{2,1,0:T(8,128)(2,1)}, u32[]{:S(2)}, u32[]{:S(2)}) async-start(bf16[16,16,6656]{2,1,0:T(8,128)(2,1)} %bitcast.36), calls=%async_computation.6 | async-start | bytes 6815744 | tf_op jit(solution)/shard_map/all_to_all | solution.py:327
  290.2 13.4 %product.2 = bf16[256,6656]{1,0:T(8,128)(2,1)} custom-call(bf16[256,1024]{1,0:T(8,128)(2,1)} %fusion.4.left_ref, bf16[512,13312]{1,0:T(8,128)(2,1)} %get-tuple-element.9.own_ref, bf16[512,13312]{1,0:T(8,128)(2,1)} %collective-permute-done.4.other_ref), custom_call_target="tpu_custom_call" | custom-call | flops 3489660928 | bytes 17039360 | tf_op jit(solution)/shard_map/product/pallas_call | solution.py:226
  303.6 32.8 %all-to-all-done.6 = bf16[16,16,6656]{2,1,0:T(8,128)(2,1)} async-done(((bf16[16,16,6656]{2,1,0:T(8,128)(2,1)}), bf16[16,16,6656]{2,1,0:T(8,128)(2,1)}, u32[]{:S(2)}, u32[]{:S(2)}) %all-to-all-start.6) | async-done | bytes 3407904 | tf_op jit(solution)/shard_map/all_to_all | solution.py:327
  336.4 12.0 %all-to-all-start.5 = ((bf16[16,16,6656]{2,1,0:T(8,128)(2,1)}), bf16[16,16,6656]{2,1,0:T(8,128)(2,1)}, u32[]{:S(2)}, u32[]{:S(2)}) async-start(bf16[16,16,6656]{2,1,0:T(8,128)(2,1)} %bitcast.35), calls=%async_computation.5 | async-start | bytes 6815744 | tf_op jit(solution)/shard_map/all_to_all | solution.py:327
  348.4 1.6 convolution_convert_fusion
  350.1 2.5 convert_reduce_fusion
  352.6 41.7 %all-to-all-done.5 = bf16[16,16,6656]{2,1,0:T(8,128)(2,1)} async-done(((bf16[16,16,6656]{2,1,0:T(8,128)(2,1)}), bf16[16,16,6656]{2,1,0:T(8,128)(2,1)}, u32[]{:S(2)}, u32[]{:S(2)}) %all-to-all-start.5) | async-done | bytes 3407904 | tf_op jit(solution)/shard_map/all_to_all | solution.py:327
  394.3 2.5 convert_reduce_fusion.1
  396.8 1.0 pad_maximum_fusion
  (5 shorter events, 0.1 us)
Async XLA Ops:
  2.2 0.5 copy-start
  27.7 114.0 %all-to-all-start.1 = ((bf16[128,2,128,128]{3,2,1,0:T(8,128)(2,1)}), bf16[128,2,128,128]{3,2,1,0:T(8,128)(2,1)}, u32[]{:S(2)}, u32[]{:S(2)}) async-start(bf16[128,2,128,128]{3,2,1,0:T(8,128)(2,1)} %bitcast.34), calls=%async_computation.1 | async-start | bytes 16777216 | tf_op jit(solution)/shard_map/all_to_all | solution.py:264
  158.9 113.4 %collective-permute-start.4 = (bf16[512,13312]{1,0:T(8,128)(2,1)}, bf16[512,13312]{1,0:T(8,128)(2,1)}, u32[]{:S(2)}, u32[]{:S(2)}) collective-permute-start(bf16[512,13312]{1,0:T(8,128)(2,1)} %get-tuple-element.9.own_ref), channel_id=1, source_target_pairs={{0,4},{4,0},{8,12},{12,8},{16,20},{20,16},{24,28},{28,24},{32,36},... | collective-permute-start | bytes 40894472 | tf_op jit(solution)/shard_map/ppermute | solution.py:286
  177.5 17.1 %collective-permute-start = (f32[128,512]{1,0:T(8,128)S(1)}, f32[128,512]{1,0:T(8,128)S(1)}, u32[]{:S(2)}, u32[]{:S(2)}) collective-permute-start(f32[128,512]{1,0:T(8,128)S(1)} %reduce_sum.86), channel_id=1, source_target_pairs={{0,3},{1,0},{2,1},{3,2},{4,7},{5,4},{6,5},{7,6},{8,11},{9,8},{10,9... | collective-permute-start | bytes 786440 | tf_op jit(solution)/shard_map/ppermute | solution.py:302
  181.6 36.8 %all-to-all-start.3 = ((f32[128,4,512]{2,1,0:T(4,128)}), f32[128,4,512]{2,1,0:T(4,128)S(1)}, u32[]{:S(2)}, u32[]{:S(2)}) async-start(f32[128,4,512]{2,1,0:T(4,128)} %copy.17), calls=%async_computation.3 | async-start | bytes 2097152 | tf_op jit(solution)/shard_map/all_to_all | solution.py:294
  190.9 21.2 %collective-permute-start.1 = (f32[128,512]{1,0:T(8,128)S(1)}, f32[128,512]{1,0:T(8,128)S(1)}, u32[]{:S(2)}, u32[]{:S(2)}) collective-permute-start(f32[128,512]{1,0:T(8,128)S(1)} %reduce_sum.86), channel_id=1, source_target_pairs={{0,2},{1,3},{2,0},{3,1},{4,6},{5,7},{6,4},{7,5},{8,10},{9,11},{10,... | collective-permute-start | bytes 786440 | tf_op jit(solution)/shard_map/ppermute | solution.py:302
  193.8 23.1 %collective-permute-start.2 = (f32[128,512]{1,0:T(8,128)S(1)}, f32[128,512]{1,0:T(8,128)S(1)}, u32[]{:S(2)}, u32[]{:S(2)}) collective-permute-start(f32[128,512]{1,0:T(8,128)S(1)} %reduce_sum.86), channel_id=1, source_target_pairs={{0,1},{1,2},{2,3},{3,0},{4,5},{5,6},{6,7},{7,4},{8,9},{9,10},{10,1... | collective-permute-start | bytes 786440 | tf_op jit(solution)/shard_map/ppermute | solution.py:302
  219.7 26.2 %all-to-all-start.4 = ((f32[128,4,512]{2,1,0:T(4,128)}), f32[128,4,512]{2,1,0:T(4,128)}, u32[]{:S(2)}, u32[]{:S(2)}) async-start(f32[128,4,512]{2,1,0:T(4,128)} %broadcast_in_dim.57), calls=%async_computation.4 | async-start | bytes 2097152 | tf_op jit(solution)/shard_map/all_to_all | solution.py:298
  231.5 36.8 %collective-permute-start.3 = (f32[512,512]{1,0:T(8,128)S(1)}, f32[512,512]{1,0:T(8,128)}, u32[]{:S(2)}, u32[]{:S(2)}) collective-permute-start(f32[512,512]{1,0:T(8,128)S(1)} %bitcast.37), channel_id=1, source_target_pairs={{0,4},{4,0},{8,12},{12,8},{16,20},{20,16},{24,28},{28,24},{32,36},... | collective-permute-start | bytes 3145736 | tf_op jit(solution)/shard_map/ppermute | solution.py:308
  285.7 50.8 %all-to-all-start.6 = ((bf16[16,16,6656]{2,1,0:T(8,128)(2,1)}), bf16[16,16,6656]{2,1,0:T(8,128)(2,1)}, u32[]{:S(2)}, u32[]{:S(2)}) async-start(bf16[16,16,6656]{2,1,0:T(8,128)(2,1)} %bitcast.36), calls=%async_computation.6 | async-start | bytes 6815744 | tf_op jit(solution)/shard_map/all_to_all | solution.py:327
  336.4 57.9 %all-to-all-start.5 = ((bf16[16,16,6656]{2,1,0:T(8,128)(2,1)}), bf16[16,16,6656]{2,1,0:T(8,128)(2,1)}, u32[]{:S(2)}, u32[]{:S(2)}) async-start(bf16[16,16,6656]{2,1,0:T(8,128)(2,1)} %bitcast.35), calls=%async_computation.5 | async-start | bytes 6815744 | tf_op jit(solution)/shard_map/all_to_all | solution.py:327

commit v3 on v2

--- a/solution.py
+++ b/solution.py
@@ -218,21 +218,20 @@
     out_ref[...] = total.astype(out_ref.dtype)
 
 
-def product(left, own, other, part, parts, width):
+def product(left, own, other, width):
     rows, cols = own.shape
     half = left.shape[0]
-    steps = cols // parts // width
-    spec = pl.BlockSpec((rows, width), lambda k: (0, part * steps + k))
+    spec = pl.BlockSpec((rows, width), lambda k: (0, k))
     return pl.pallas_call(
         product_kernel,
-        grid=(steps,),
+        grid=(cols // width,),
         in_specs=[pl.BlockSpec((half, 2 * rows), lambda k: (0, 0)), spec, spec],
         out_specs=pl.BlockSpec((half, width), lambda k: (0, k)),
-        out_shape=jax.ShapeDtypeStruct((half, cols // parts), jnp.bfloat16),
+        out_shape=jax.ShapeDtypeStruct((half, cols), jnp.bfloat16),
         compiler_params=pltpu.CompilerParams(vmem_limit_bytes=56 * MIB),
         cost_estimate=pl.CostEstimate(
-            flops=2 * half * 2 * rows * cols // parts,
-            bytes_accessed=(4 * rows * cols + 2 * half * cols) // parts,
+            flops=2 * half * 2 * rows * cols,
+            bytes_accessed=4 * rows * cols + 2 * half * cols,
             transcendentals=0,
         ),
         name="product",
@@ -257,17 +256,25 @@
     numbers = jnp.arange(slot_count, dtype=jnp.int32)
     same = (target[:, None] == target[None, :]) & (numbers[None, :] < numbers[:, None])
     place = target * capacity + jnp.sum(same.astype(jnp.int32), axis=1)
-    spots = jnp.arange(slots, dtype=jnp.int32)
-    hit = place[None, :] == spots[:, None]
-    send_where = jnp.sum(jnp.where(hit, block_pos[None, :] + 1, 0), axis=1)
-    send_blocks, send_where = lax.optimization_barrier((bucket(place, blocks, slots), send_where))
+    send_blocks, listed = lax.optimization_barrier(
+        (bucket(place, blocks, slots), target * PBR * TBC + block_pos)
+    )
     got_blocks = lax.all_to_all(
         send_blocks.reshape(devices_all, capacity, BLK, BLK), everywhere, 0, 0, tiled=True
     ).reshape(slots, BLK, BLK)
-    got_where = lax.all_to_all(
-        send_where.reshape(devices_all, capacity), everywhere, 0, 0, tiled=True
-    ).reshape(slots)
-
+
+    listed = lax.all_gather(listed, everywhere, axis=0)
+    me = lax.axis_index("rows") * col_devices + lax.axis_index("cols")
+    place_here = listed - me * PBR * TBC
+    here = (place_here >= 0) & (place_here < PBR * TBC)
+    first = jnp.min(jnp.where(here, numbers[None, :], slot_count), axis=1)
+    last = jnp.max(jnp.where(here, numbers[None, :], -1), axis=1)
+    taken = jnp.where(here, place_here + 1, 0)
+    first_where = jnp.sum(jnp.where(numbers[None, :] == first[:, None], taken, 0), axis=1)
+    last_where = jnp.sum(jnp.where(numbers[None, :] == last[:, None], taken, 0), axis=1)
+    got_where = jnp.stack([first_where, jnp.where(last > first, last_where, 0)], axis=1).reshape(slots)
+
+    spots = jnp.arange(slots, dtype=jnp.int32)
     key = jnp.where(got_where == 0, PBR * TBC, got_where - 1)
     before = (key[None, :] < key[:, None]) | (
         (key[None, :] == key[:, None]) & (spots[None, :] < spots[:, None])
@@ -294,12 +301,12 @@
     grams = lax.all_to_all(
         local_gram.reshape(devices_all, rank // devices_all, rank), everywhere, 0, 0, tiled=True
     )
-    gram_rows = jnp.sum(grams, axis=0)
+    gram_rows, late_share = lax.optimization_barrier((jnp.sum(grams, axis=0), own_share))
     gram = lax.all_to_all(
         jnp.broadcast_to(gram_rows[None], (devices_all,) + gram_rows.shape), everywhere, 0, 0, tiled=True
     ).reshape(rank, rank)
-    shares = [own_share] + [
-        lax.ppermute(own_share, "cols", [(i, (i + d) % col_devices) for i in range(col_devices)])
+    shares = [late_share] + [
+        lax.ppermute(late_share, "cols", [(i, (i + d) % col_devices) for i in range(col_devices)])
         for d in range(1, col_devices)
     ]
     back = jnp.stack(shares[::-1] * 2)
@@ -321,12 +328,9 @@
 
     groups = [[2 * i + c for i in range(chips)] for c in range(2)]
     scaling = 1.0 / math.sqrt(total_rows)
-    halves = []
-    for part in range(2):
-        terms = product(left, tile, other_tile, part, 2, 512).reshape(chips, ranks, cols // 2)
-        terms = lax.all_to_all(terms, "rows", 0, 0, axis_index_groups=groups, tiled=True)
-        halves.append(jnp.sum(terms.astype(jnp.float32), axis=0) * scaling)
-    coefficients = jnp.concatenate(halves, axis=1)
+    terms = product(left, tile, other_tile, cols // 4).reshape(chips, ranks, cols)
+    terms = lax.all_to_all(terms, "rows", 0, 0, axis_index_groups=groups, tiled=True)
+    coefficients = jnp.sum(terms.astype(jnp.float32), axis=0) * scaling
 
     slice_width = rank // col_devices
     my_rows = lax.dynamic_slice_in_dim(inverse, lax.axis_index("cols") * slice_width, slice_width, 0)

time: 399 us -> 436 us (1.093)
  blocking collectives: 38.5 us -> 190 us
  waiting for transfers between devices: 215 us -> 138 us
  starting transfers between devices: 44.8 us -> 27.4 us
  Pallas kernels: 69.6 us -> 57.4 us
  local copies, waits for them, and re-layouts: 12.3 us -> 4.02 us
    all_gather x0 -> x1, blocking collectives: none -> 143 us  [on_device(): listed = lax.all_gather(listed, everywhere, axis=0)]
    all_to_all x1, waiting for transfers between devices: 106 us -> 0.01 us  [on_device(): lax.all_to_all(send_blocks.reshape(devices_all, capacity, BLK, BLK), ever...]
    all_to_all x2 -> x1, waiting for transfers between devices: 74.5 us -> 120 us  [on_device(): lax.all_to_all(terms, 'rows', 0, 0, axis_index_groups=groups, tiled=True)]
    pallas_call x2 -> x1, Pallas kernels: 26.8 us -> 14.6 us  [product(): pl.pallas_call(product_kernel, grid=(cols // width,), in_specs=[pl.BlockS...]
    all_to_all x2 -> x1, starting transfers between devices: 16.5 us -> 4.66 us  [on_device(): lax.all_to_all(terms, 'rows', 0, 0, axis_index_groups=groups, tiled=True)]
    all_to_all x1, waiting for transfers between devices: 14 us -> 4.58 us  [on_device(): lax.all_to_all(jnp.broadcast_to(gram_rows[None], (devices_all,) + gram_ro...]
    all_to_all x1 -> x0, starting transfers between devices: 9.29 us -> none  [on_device(): lax.all_to_all(local_gram.reshape(devices_all, rank // devices_all, rank)...]
    ppermute x3, waiting for transfers between devices: 20.8 us -> 13.3 us  [on_device(): lax.ppermute(late_share, 'cols', [(i, (i + d) % col_devices) for i in ran...]
  transfers between devices with their start and end apart: 10 -> 8, of which waited for: 6 -> 4; matrix products, arithmetic and copies ran while one was open for 6% -> 3% of each run, Pallas kernels for 9% -> 5%
where the time goes in v3:
time: 436 us; the launch traced here: 434 us
  blocking collectives  190 us (44%)
  waiting for transfers between devices  138 us (32%)
  Pallas kernels  57.4 us (13%)
  starting transfers between devices  27.4 us (6%)
  other arithmetic  9.48 us (2%)
  matrix products  6.56 us (2%)
    all_gather x1, blocking collectives, on_device(): listed = lax.all_gather(listed, everywhere, axis=0)  143 us
    all_to_all x1, waiting for transfers between devices, on_device(): lax.all_to_all(terms, 'rows', 0, 0, axis_index_groups=groups, tiled=True)  120 us
    all_to_all x1, blocking collectives, on_device(): lax.all_to_all(local_gram.reshape(devices_all, rank // devices_all, rank)...  26.4 us
    all_to_all x1, blocking collectives, on_device(): lax.all_to_all(part.reshape(col_devices, share, rank), 'cols', 0, 0, tile...  20.9 us
    pallas_call x1, Pallas kernels, inverse_factor(): pl.pallas_call(functools.partial(factor_kernel, scale), in_specs=[pl.Bloc...  20.8 us
    pallas_call x1, Pallas kernels, tile_and_sketch(): pl.pallas_call(tile_kernel, grid_spec=pltpu.PrefetchScalarGridSpec(num_sc...  17.1 us
    pallas_call x1, Pallas kernels, product(): pl.pallas_call(product_kernel, grid=(cols // width,), in_specs=[pl.BlockS...  14.6 us
    ppermute x3, waiting for transfers between devices, on_device(): lax.ppermute(late_share, 'cols', [(i, (i + d) % col_devices) for i in ran...  13.3 us
  transfers between devices with their start and end apart: 8, of which 4 were waited for; matrix products, arithmetic and copies ran while one was open for 3% of the time, Pallas kernels for 5%

profile of v3, /device:TPU:0, one launch (start us, length us, event | category | flops | bytes accessed | tf_op | source)
XLA Modules:
  0.0 433.6 jit_solution(16020655038345938760)
XLA Ops:
  0.6 0.9 convert_reduce_fusion.2
  1.5 1.2 multiply_add_fusion
  2.7 4.8 %bucket.1 = bf16[256,128,128]{2,1,0:T(8,128)(2,1)} custom-call(s32[128]{0:T(128)} %get-tuple-element.22.place_ref, bf16[128,128,128]{2,1,0:T(8,128)(2,1)} %blocks_ref.1), custom_call_target="tpu_custom_call" | custom-call | bytes 8388608 | tf_op jit(solution)/shard_map/bucket/pallas_call | solution.py:30
  7.5 11.7 %all-to-all-start = ((bf16[128,2,128,128]{3,2,1,0:T(8,128)(2,1)}), bf16[128,2,128,128]{3,2,1,0:T(8,128)(2,1)}, u32[]{:S(2)}, u32[]{:S(2)}) async-start(bf16[128,2,128,128]{3,2,1,0:T(8,128)(2,1)} %bitcast.52), calls=%async_computation | async-start | bytes 16777216 | tf_op jit(solution)/shard_map/all_to_all | solution.py:262
  19.2 142.9 %all-gather.1 = s32[128,1,128]{2,1,0:T(1,128)S(1)} all-gather(s32[1,1,128]{2,1,0:T(1,128)S(1)} %bitcast.63), channel_id=2, replica_groups=mesh['rows'=32,'cols'=4] {'rows','cols'}, dimensions={0}, use_global_device_ids=true | all-gather | bytes 66048 | tf_op jit(solution)/shard_map/all_gather | solution.py:266
  162.1 0.1 select_reduce_fusion.4
  162.2 0.2 select_reduce_fusion.3
  162.4 0.6 fusion.18
  163.1 0.1 copy.20
  163.2 0.1 select_n.97
  163.3 0.2 convert_reduce_fusion.1
  163.5 0.1 select_reduce_fusion
  163.7 0.1 slice_compare_fusion
  163.7 0.1 add_convert_fusion
  163.8 0.1 fusion.19
  163.9 0.7 pad_add_fusion.code_ref
  164.6 0.0 all-to-all-done
  164.6 17.1 %tile_and_sketch.1 = (bf16[512,13312]{1,0:T(8,128)(2,1)}, f32[512,512]{1,0:T(8,128)S(1)}) custom-call(s32[257]{0:T(512)S(1)} %pad_add_fusion.code_ref, bf16[256,128,128]{2,1,0:T(8,128)(2,1)} %bitcast.9.got_hbm, bf16[13312,512]{1,0:T(8,128)(2,1)} %omega_hbm.1), custom_call_target="tpu_custom_call" | custom-call | flops 6979321856 | bytes 35651584 | tf_op jit(solution)/shard_map/tile_and_sketch/pallas_call | solution.py:103
  181.7 0.6 collective-permute-start.4
  182.3 20.9 %all_to_all.25 = f32[4,128,512]{2,1,0:T(8,128)S(1)} all-to-all(f32[4,128,512]{2,1,0:T(8,128)S(1)} %bitcast.50), channel_id=1, replica_groups=mesh['rows'=32,'cols'=4] {'cols'}, dimensions={0} | all-to-all | bytes 2097152 | tf_op jit(solution)/shard_map/all_to_all | solution.py:296
  203.2 0.1 reduce_sum.87
  203.3 0.1 copy.21
  203.4 1.0 fusion.7
  204.4 0.7 copy.23
  205.1 26.4 %all_to_all.26 = f32[128,4,512]{2,1,0:T(4,128)S(1)} all-to-all(f32[128,4,512]{2,1,0:T(4,128)S(1)} %copy.23), channel_id=1, replica_groups=mesh['rows'=32,'cols'=4] {'rows','cols'}, dimensions={0} | all-to-all | bytes 2097152 | tf_op jit(solution)/shard_map/all_to_all | solution.py:301
  231.5 0.2 reduce_sum.88
  231.7 1.2 collective-permute-start
  233.0 1.8 collective-permute-start.1
  234.7 0.0 collective-permute-start.2
  234.7 1.1 broadcast_in_dim.73
  235.8 7.2 %all-to-all-start.3 = ((f32[128,4,512]{2,1,0:T(4,128)}), f32[128,4,512]{2,1,0:T(4,128)}, u32[]{:S(2)}, u32[]{:S(2)}) async-start(f32[128,4,512]{2,1,0:T(4,128)} %broadcast_in_dim.73), calls=%async_computation.3 | async-start | bytes 2097152 | tf_op jit(solution)/shard_map/all_to_all | solution.py:305
  243.0 0.0 collective-permute-done
  243.1 0.7 collective-permute-done.1
  243.8 12.6 %collective-permute-done.2 = f32[128,512]{1,0:T(8,128)S(1)} collective-permute-done((f32[128,512]{1,0:T(8,128)S(1)}, f32[128,512]{1,0:T(8,128)S(1)}, u32[]{:S(2)}, u32[]{:S(2)}) %collective-permute-start.2) | collective-permute-done | bytes 262176 | tf_op jit(solution)/shard_map/ppermute | solution.py:309
  256.6 0.1 constant_dynamic-slice_fusion.1
  256.7 0.3 collective-permute-start.3
  256.9 4.6 %all-to-all-done.3 = f32[128,4,512]{2,1,0:T(4,128)} async-done(((f32[128,4,512]{2,1,0:T(4,128)}), f32[128,4,512]{2,1,0:T(4,128)}, u32[]{:S(2)}, u32[]{:S(2)}) %all-to-all-start.3) | async-done | bytes 1048608 | tf_op jit(solution)/shard_map/all_to_all | solution.py:305
  261.5 1.6 reshape.98.gram_ref
  263.1 20.8 %inverse_factor.1 = f32[512,512]{1,0:T(8,128)S(1)} custom-call(f32[512,512]{1,0:T(8,128)S(1)} %reshape.98.gram_ref), custom_call_target="tpu_custom_call" | custom-call | flops 34359738368 | bytes 2097152 | tf_op jit(solution)/shard_map/inverse_factor/pallas_call | solution.py:200
  284.0 0.0 collective-permute-done.3
  284.0 3.9 fusion.4.left_ref
  287.9 0.0 collective-permute-done.4.other_ref
  287.9 14.6 %product.1 = bf16[256,13312]{1,0:T(8,128)(2,1)} custom-call(bf16[256,1024]{1,0:T(8,128)(2,1)} %fusion.4.left_ref, bf16[512,13312]{1,0:T(8,128)(2,1)} %get-tuple-element.13.own_ref, bf16[512,13312]{1,0:T(8,128)(2,1)} %collective-permute-done.4.other_ref), custom_call_target="tpu_custom_call" | custom-call | flops 6979321856 | bytes 34078720 | tf_op jit(solution)/shard_map/product/pallas_call | solution.py:225
  302.6 4.7 %all-to-all-start.4 = ((bf16[16,16,13312]{2,1,0:T(8,128)(2,1)}), bf16[16,16,13312]{2,1,0:T(8,128)(2,1)}, u32[]{:S(2)}, u32[]{:S(2)}) async-start(bf16[16,16,13312]{2,1,0:T(8,128)(2,1)} %bitcast.53), calls=%async_computation.4 | async-start | bytes 13631488 | tf_op jit(solution)/shard_map/all_to_all | solution.py:332
  307.2 1.6 convolution_convert_fusion
  308.9 119.7 %all-to-all-done.4 = bf16[16,16,13312]{2,1,0:T(8,128)(2,1)} async-done(((bf16[16,16,13312]{2,1,0:T(8,128)(2,1)}), bf16[16,16,13312]{2,1,0:T(8,128)(2,1)}, u32[]{:S(2)}, u32[]{:S(2)}) %all-to-all-start.4) | async-done | bytes 6815776 | tf_op jit(solution)/shard_map/all_to_all | solution.py:332
  428.6 4.0 convert_reduce_fusion
  432.6 1.0 broadcast_multiply_fusion
  (12 shorter events, 0.2 us)
Async XLA Ops:
  7.5 157.0 %all-to-all-start = ((bf16[128,2,128,128]{3,2,1,0:T(8,128)(2,1)}), bf16[128,2,128,128]{3,2,1,0:T(8,128)(2,1)}, u32[]{:S(2)}, u32[]{:S(2)}) async-start(bf16[128,2,128,128]{3,2,1,0:T(8,128)(2,1)} %bitcast.52), calls=%async_computation | async-start | bytes 16777216 | tf_op jit(solution)/shard_map/all_to_all | solution.py:262
  181.7 106.2 %collective-permute-start.4 = (bf16[512,13312]{1,0:T(8,128)(2,1)}, bf16[512,13312]{1,0:T(8,128)(2,1)}, u32[]{:S(2)}, u32[]{:S(2)}) collective-permute-start(bf16[512,13312]{1,0:T(8,128)(2,1)} %get-tuple-element.13.own_ref), channel_id=1, source_target_pairs={{0,4},{4,0},{8,12},{12,8},{16,20},{20,16},{24,28},{28,24},{32,36},... | collective-permute-start | bytes 40894472 | tf_op jit(solution)/shard_map/ppermute | solution.py:293
  231.7 11.3 %collective-permute-start = (f32[128,512]{1,0:T(8,128)S(1)}, f32[128,512]{1,0:T(8,128)S(1)}, u32[]{:S(2)}, u32[]{:S(2)}) collective-permute-start(f32[128,512]{1,0:T(8,128)S(1)} %reduce_sum.87), channel_id=1, source_target_pairs={{0,3},{1,0},{2,1},{3,2},{4,7},{5,4},{6,5},{7,6},{8,11},{9,8},{10,9... | collective-permute-start | bytes 786440 | tf_op jit(solution)/shard_map/ppermute | solution.py:309
  233.0 10.8 %collective-permute-start.1 = (f32[128,512]{1,0:T(8,128)S(1)}, f32[128,512]{1,0:T(8,128)S(1)}, u32[]{:S(2)}, u32[]{:S(2)}) collective-permute-start(f32[128,512]{1,0:T(8,128)S(1)} %reduce_sum.87), channel_id=1, source_target_pairs={{0,2},{1,3},{2,0},{3,1},{4,6},{5,7},{6,4},{7,5},{8,10},{9,11},{10,... | collective-permute-start | bytes 786440 | tf_op jit(solution)/shard_map/ppermute | solution.py:309
  234.7 21.7 %collective-permute-start.2 = (f32[128,512]{1,0:T(8,128)S(1)}, f32[128,512]{1,0:T(8,128)S(1)}, u32[]{:S(2)}, u32[]{:S(2)}) collective-permute-start(f32[128,512]{1,0:T(8,128)S(1)} %reduce_sum.87), channel_id=1, source_target_pairs={{0,1},{1,2},{2,3},{3,0},{4,5},{5,6},{6,7},{7,4},{8,9},{9,10},{10,1... | collective-permute-start | bytes 786440 | tf_op jit(solution)/shard_map/ppermute | solution.py:309
  235.8 25.7 %all-to-all-start.3 = ((f32[128,4,512]{2,1,0:T(4,128)}), f32[128,4,512]{2,1,0:T(4,128)}, u32[]{:S(2)}, u32[]{:S(2)}) async-start(f32[128,4,512]{2,1,0:T(4,128)} %broadcast_in_dim.73), calls=%async_computation.3 | async-start | bytes 2097152 | tf_op jit(solution)/shard_map/all_to_all | solution.py:305
  256.7 27.3 %collective-permute-start.3 = (f32[512,512]{1,0:T(8,128)S(1)}, f32[512,512]{1,0:T(8,128)}, u32[]{:S(2)}, u32[]{:S(2)}) collective-permute-start(f32[512,512]{1,0:T(8,128)S(1)} %bitcast.54), channel_id=1, source_target_pairs={{0,4},{4,0},{8,12},{12,8},{16,20},{20,16},{24,28},{28,24},{32,36},... | collective-permute-start | bytes 3145736 | tf_op jit(solution)/shard_map/ppermute | solution.py:315
  302.6 126.1 %all-to-all-start.4 = ((bf16[16,16,13312]{2,1,0:T(8,128)(2,1)}), bf16[16,16,13312]{2,1,0:T(8,128)(2,1)}, u32[]{:S(2)}, u32[]{:S(2)}) async-start(bf16[16,16,13312]{2,1,0:T(8,128)(2,1)} %bitcast.53), calls=%async_computation.4 | async-start | bytes 13631488 | tf_op jit(solution)/shard_map/all_to_all | solution.py:332

commit v4 on v3

--- a/solution.py
+++ b/solution.py
@@ -256,25 +256,17 @@
     numbers = jnp.arange(slot_count, dtype=jnp.int32)
     same = (target[:, None] == target[None, :]) & (numbers[None, :] < numbers[:, None])
     place = target * capacity + jnp.sum(same.astype(jnp.int32), axis=1)
-    send_blocks, listed = lax.optimization_barrier(
-        (bucket(place, blocks, slots), target * PBR * TBC + block_pos)
-    )
+    spots = jnp.arange(slots, dtype=jnp.int32)
+    hit = place[None, :] == spots[:, None]
+    send_where = jnp.sum(jnp.where(hit, block_pos[None, :] + 1, 0), axis=1)
+    send_blocks = bucket(place, blocks, slots)
     got_blocks = lax.all_to_all(
         send_blocks.reshape(devices_all, capacity, BLK, BLK), everywhere, 0, 0, tiled=True
     ).reshape(slots, BLK, BLK)
-
-    listed = lax.all_gather(listed, everywhere, axis=0)
-    me = lax.axis_index("rows") * col_devices + lax.axis_index("cols")
-    place_here = listed - me * PBR * TBC
-    here = (place_here >= 0) & (place_here < PBR * TBC)
-    first = jnp.min(jnp.where(here, numbers[None, :], slot_count), axis=1)
-    last = jnp.max(jnp.where(here, numbers[None, :], -1), axis=1)
-    taken = jnp.where(here, place_here + 1, 0)
-    first_where = jnp.sum(jnp.where(numbers[None, :] == first[:, None], taken, 0), axis=1)
-    last_where = jnp.sum(jnp.where(numbers[None, :] == last[:, None], taken, 0), axis=1)
-    got_where = jnp.stack([first_where, jnp.where(last > first, last_where, 0)], axis=1).reshape(slots)
-
-    spots = jnp.arange(slots, dtype=jnp.int32)
+    got_where = lax.all_to_all(
+        send_where.reshape(devices_all, capacity), everywhere, 0, 0, tiled=True
+    ).reshape(slots)
+
     key = jnp.where(got_where == 0, PBR * TBC, got_where - 1)
     before = (key[None, :] < key[:, None]) | (
         (key[None, :] == key[:, None]) & (spots[None, :] < spots[:, None])
@@ -326,17 +318,19 @@
         my_ranks, both, (((1,), (1,)), ((), ())), precision=HIGHEST, preferred_element_type=jnp.float32
     ).astype(jnp.bfloat16)
 
-    groups = [[2 * i + c for i in range(chips)] for c in range(2)]
-    scaling = 1.0 / math.sqrt(total_rows)
-    terms = product(left, tile, other_tile, cols // 4).reshape(chips, ranks, cols)
-    terms = lax.all_to_all(terms, "rows", 0, 0, axis_index_groups=groups, tiled=True)
-    coefficients = jnp.sum(terms.astype(jnp.float32), axis=0) * scaling
-
     slice_width = rank // col_devices
     my_rows = lax.dynamic_slice_in_dim(inverse, lax.axis_index("cols") * slice_width, slice_width, 0)
     basis = lax.dot_general(
         sketch, my_rows, (((1,), (1,)), ((), ())), precision=HIGHEST, preferred_element_type=jnp.float32
     ).astype(jnp.bfloat16)
+
+    groups = [[2 * i + c for i in range(chips)] for c in range(2)]
+    scaling = 1.0 / math.sqrt(total_rows)
+    terms = product(left, tile, other_tile, cols // 4).reshape(chips, ranks, cols)
+    terms, basis = lax.optimization_barrier((terms, basis))
+    terms = lax.all_to_all(terms, "rows", 0, 0, axis_index_groups=groups, tiled=True)
+    coefficients = jnp.sum(terms.astype(jnp.float32), axis=0) * scaling
+
     return basis, coefficients
 
 

time: 436 us -> 359 us (0.82)
  blocking collectives: 190 us -> 126 us
  waiting for transfers between devices: 138 us -> 128 us
    all_gather x1 -> x0, blocking collectives: 143 us -> none  [on_device(): listed = lax.all_gather(listed, everywhere, axis=0)]
    all_to_all x1, waiting for transfers between devices: 120 us -> 4.2 us  [on_device(): lax.all_to_all(send_where.reshape(devices_all, capacity), everywhere, 0,...]
    all_to_all x1, waiting for transfers between devices: 0.01 us -> 106 us  [on_device(): lax.all_to_all(send_blocks.reshape(devices_all, capacity, BLK, BLK), ever...]
    all_to_all x0 -> x1, blocking collectives: none -> 83.2 us  [on_device(): lax.all_to_all(terms, 'rows', 0, 0, axis_index_groups=groups, tiled=True)]
    all_to_all x1, starting transfers between devices: 4.66 us -> 11.1 us  [on_device(): lax.all_to_all(send_where.reshape(devices_all, capacity), everywhere, 0,...]
    all_to_all x1, starting transfers between devices: 11.7 us -> 6.12 us  [on_device(): lax.all_to_all(send_blocks.reshape(devices_all, capacity, BLK, BLK), ever...]
  transfers between devices with their start and end apart: 8 -> 8, of which waited for: 4 -> 5; matrix products, arithmetic and copies ran while one was open for 3% -> 3% of each run, Pallas kernels for 5% -> 7%
where the time goes in v4:
time: 359 us; the launch traced here: 356 us
  waiting for transfers between devices  128 us (36%)
  blocking collectives  126 us (35%)
  Pallas kernels  57.3 us (16%)
  starting transfers between devices  27.2 us (8%)
  matrix products  6.58 us (2%)
  other arithmetic  6.04 us (2%)
    all_to_all x1, waiting for transfers between devices, on_device(): lax.all_to_all(send_blocks.reshape(devices_all, capacity, BLK, BLK), ever...  106 us
    all_to_all x1, blocking collectives, on_device(): lax.all_to_all(terms, 'rows', 0, 0, axis_index_groups=groups, tiled=True)  83.2 us
    all_to_all x1, blocking collectives, on_device(): lax.all_to_all(local_gram.reshape(devices_all, rank // devices_all, rank)...  24.8 us
    pallas_call x1, Pallas kernels, inverse_factor(): pl.pallas_call(functools.partial(factor_kernel, scale), in_specs=[pl.Bloc...  20.8 us
    all_to_all x1, blocking collectives, on_device(): lax.all_to_all(part.reshape(col_devices, share, rank), 'cols', 0, 0, tile...  18.4 us
    pallas_call x1, Pallas kernels, tile_and_sketch(): pl.pallas_call(tile_kernel, grid_spec=pltpu.PrefetchScalarGridSpec(num_sc...  17.1 us
    pallas_call x1, Pallas kernels, product(): pl.pallas_call(product_kernel, grid=(cols // width,), in_specs=[pl.BlockS...  14.6 us
    ppermute x3, waiting for transfers between devices, on_device(): lax.ppermute(late_share, 'cols', [(i, (i + d) % col_devices) for i in ran...  13.9 us
  transfers between devices with their start and end apart: 8, of which 5 were waited for; matrix products, arithmetic and copies ran while one was open for 3% of the time, Pallas kernels for 7%

profile of v4, /device:TPU:0, one launch (start us, length us, event | category | flops | bytes accessed | tf_op | source)
XLA Modules:
  0.0 356.3 jit_solution(3225573714360170843)
XLA Ops:
  0.6 0.9 convert_reduce_fusion.2
  1.5 0.7 multiply_add_fusion
  2.2 0.0 copy-start
  2.2 0.1 select_reduce_fusion.1
  2.3 0.8 all_to_all.21
  3.1 11.1 %all-to-all-start = ((s32[128,1,2]{2,1,0:T(1,128)}), s32[128,1,2]{2,1,0:T(1,128)S(1)}, u32[]{:S(2)}, u32[]{:S(2)}) async-start(s32[128,1,2]{2,1,0:T(1,128)} %bitcast.1), calls=%async_computation | async-start | bytes 131072 | tf_op jit(solution)/shard_map/all_to_all | solution.py:266
  14.3 0.0 copy-done
  14.3 4.8 %bucket.1 = bf16[256,128,128]{2,1,0:T(8,128)(2,1)} custom-call(s32[128]{0:T(128)} %copy-done, bf16[128,128,128]{2,1,0:T(8,128)(2,1)} %blocks_ref.1), custom_call_target="tpu_custom_call" | custom-call | bytes 8388608 | tf_op jit(solution)/shard_map/bucket/pallas_call | solution.py:30
  19.0 4.2 %all-to-all-done = s32[128,1,2]{2,1,0:T(1,128)S(1)} async-done(((s32[128,1,2]{2,1,0:T(1,128)}), s32[128,1,2]{2,1,0:T(1,128)S(1)}, u32[]{:S(2)}, u32[]{:S(2)}) %all-to-all-start) | async-done | bytes 1056 | tf_op jit(solution)/shard_map/all_to_all | solution.py:266
  23.2 6.1 %all-to-all-start.1 = ((bf16[128,2,128,128]{3,2,1,0:T(8,128)(2,1)}), bf16[128,2,128,128]{3,2,1,0:T(8,128)(2,1)}, u32[]{:S(2)}, u32[]{:S(2)}) async-start(bf16[128,2,128,128]{3,2,1,0:T(8,128)(2,1)} %bitcast.33), calls=%async_computation.1 | async-start | bytes 16777216 | tf_op jit(solution)/shard_map/all_to_all | solution.py:263
  29.4 0.9 fusion.22
  30.3 0.1 select_n.65
  30.4 0.2 convert_reduce_fusion.1
  30.6 0.1 select_reduce_fusion
  30.8 0.1 slice_compare_fusion
  30.8 0.1 add_convert_fusion
  30.9 0.1 fusion.19
  31.0 0.7 pad_add_fusion.code_ref
  31.7 105.8 %all-to-all-done.1 = bf16[128,2,128,128]{3,2,1,0:T(8,128)(2,1)} async-done(((bf16[128,2,128,128]{3,2,1,0:T(8,128)(2,1)}), bf16[128,2,128,128]{3,2,1,0:T(8,128)(2,1)}, u32[]{:S(2)}, u32[]{:S(2)}) %all-to-all-start.1) | async-done | bytes 8388640 | tf_op jit(solution)/shard_map/all_to_all | solution.py:263
  137.4 17.1 %tile_and_sketch.1 = (bf16[512,13312]{1,0:T(8,128)(2,1)}, f32[512,512]{1,0:T(8,128)S(1)}) custom-call(s32[257]{0:T(512)S(1)} %pad_add_fusion.code_ref, bf16[256,128,128]{2,1,0:T(8,128)(2,1)} %bitcast.4.got_hbm, bf16[13312,512]{1,0:T(8,128)(2,1)} %omega_hbm.1), custom_call_target="tpu_custom_call" | custom-call | flops 6979321856 | bytes 35651584 | tf_op jit(solution)/shard_map/tile_and_sketch/pallas_call | solution.py:103
  154.6 0.1 collective-permute-start.4
  154.7 18.4 %all_to_all.34 = f32[4,128,512]{2,1,0:T(8,128)S(1)} all-to-all(f32[4,128,512]{2,1,0:T(8,128)S(1)} %bitcast.31), channel_id=1, replica_groups=mesh['rows'=32,'cols'=4] {'cols'}, dimensions={0} | all-to-all | bytes 2097152 | tf_op jit(solution)/shard_map/all_to_all | solution.py:288
  173.1 0.1 reduce_sum.77
  173.2 0.1 copy.16
  173.3 1.0 fusion.7
  174.3 0.7 copy.18
  175.0 24.8 %all_to_all.35 = f32[128,4,512]{2,1,0:T(4,128)S(1)} all-to-all(f32[128,4,512]{2,1,0:T(4,128)S(1)} %copy.18), channel_id=1, replica_groups=mesh['rows'=32,'cols'=4] {'rows','cols'}, dimensions={0} | all-to-all | bytes 2097152 | tf_op jit(solution)/shard_map/all_to_all | solution.py:293
  199.8 0.2 reduce_sum.78
  200.0 1.2 collective-permute-start
  201.2 1.8 collective-permute-start.1
  203.0 0.0 collective-permute-start.2
  203.0 1.1 broadcast_in_dim.57
  204.1 6.7 %all-to-all-start.4 = ((f32[128,4,512]{2,1,0:T(4,128)}), f32[128,4,512]{2,1,0:T(4,128)S(1)}, u32[]{:S(2)}, u32[]{:S(2)}) async-start(f32[128,4,512]{2,1,0:T(4,128)} %broadcast_in_dim.57), calls=%async_computation.4 | async-start | bytes 2097152 | tf_op jit(solution)/shard_map/all_to_all | solution.py:297
  210.8 0.0 collective-permute-done
  210.8 1.2 collective-permute-done.1
  212.0 12.6 %collective-permute-done.2 = f32[128,512]{1,0:T(8,128)S(1)} collective-permute-done((f32[128,512]{1,0:T(8,128)S(1)}, f32[128,512]{1,0:T(8,128)S(1)}, u32[]{:S(2)}, u32[]{:S(2)}) %collective-permute-start.2) | collective-permute-done | bytes 262176 | tf_op jit(solution)/shard_map/ppermute | solution.py:301
  224.8 0.1 constant_dynamic-slice_fusion
  224.9 0.3 collective-permute-start.3
  225.2 4.5 %all-to-all-done.4 = f32[128,4,512]{2,1,0:T(4,128)S(1)} async-done(((f32[128,4,512]{2,1,0:T(4,128)}), f32[128,4,512]{2,1,0:T(4,128)S(1)}, u32[]{:S(2)}, u32[]{:S(2)}) %all-to-all-start.4) | async-done | bytes 1048608 | tf_op jit(solution)/shard_map/all_to_all | solution.py:297
  229.7 0.4 reshape.100.gram_ref
  230.0 20.8 %inverse_factor.1 = f32[512,512]{1,0:T(8,128)S(1)} custom-call(f32[512,512]{1,0:T(8,128)S(1)} %reshape.100.gram_ref), custom_call_target="tpu_custom_call" | custom-call | flops 34359738368 | bytes 2097152 | tf_op jit(solution)/shard_map/inverse_factor/pallas_call | solution.py:200
  251.0 1.7 convolution_convert_fusion
  252.6 0.0 collective-permute-done.3
  252.6 3.9 %fusion.4.left_ref = bf16[256,1024]{1,0:T(8,128)(2,1)} fusion(f32[256,512]{1,0:T(8,128)S(1)} %bitcast.39, f32[512,512]{1,0:T(8,128)} %collective-permute-done.3, f32[512,512]{1,0:T(8,128)S(1)} %bitcast.37), kind=kOutput, calls=%fused_computation.5 | convolution fusion | flops 1611399168 | bytes 3145728 | tf_op jit(solution)/shard_map/dot_general | solution.py:317
  256.6 0.0 collective-permute-done.4.other_ref
  256.6 14.6 %product.1 = bf16[256,13312]{1,0:T(8,128)(2,1)} custom-call(bf16[256,1024]{1,0:T(8,128)(2,1)} %fusion.4.left_ref, bf16[512,13312]{1,0:T(8,128)(2,1)} %get-tuple-element.11.own_ref, bf16[512,13312]{1,0:T(8,128)(2,1)} %collective-permute-done.4.other_ref), custom_call_target="tpu_custom_call" | custom-call | flops 6979321856 | bytes 34078720 | tf_op jit(solution)/shard_map/product/pallas_call | solution.py:225
  271.2 83.2 %all_to_all.36 = bf16[16,16,13312]{2,1,0:T(8,128)(2,1)S(1)} all-to-all(bf16[16,16,13312]{2,1,0:T(8,128)(2,1)} %bitcast.34), channel_id=1, replica_groups={{0,8,16,24,32,40,48,56,64,72,80,88,96,104,112,120},{4,12,20,28,36,44,52..., dimensions={0} | all-to-all | bytes 13631488 | tf_op jit(solution)/shard_map/all_to_all | solution.py:331
  354.4 1.0 convert_reduce_fusion
  355.4 1.0 broadcast_multiply_fusion
  (11 shorter events, 0.2 us)
Async XLA Ops:
  2.2 12.0 %copy-start = (s32[128]{0:T(128)}, s32[128]{0:T(128)S(1)}, u32[]{:S(2)}) copy-start(s32[128]{0:T(128)S(1)} %get-tuple-element.16.place_ref) | copy-start | bytes 1540
  3.1 20.1 %all-to-all-start = ((s32[128,1,2]{2,1,0:T(1,128)}), s32[128,1,2]{2,1,0:T(1,128)S(1)}, u32[]{:S(2)}, u32[]{:S(2)}) async-start(s32[128,1,2]{2,1,0:T(1,128)} %bitcast.1), calls=%async_computation | async-start | bytes 131072 | tf_op jit(solution)/shard_map/all_to_all | solution.py:266
  23.2 114.2 %all-to-all-start.1 = ((bf16[128,2,128,128]{3,2,1,0:T(8,128)(2,1)}), bf16[128,2,128,128]{3,2,1,0:T(8,128)(2,1)}, u32[]{:S(2)}, u32[]{:S(2)}) async-start(bf16[128,2,128,128]{3,2,1,0:T(8,128)(2,1)} %bitcast.33), calls=%async_computation.1 | async-start | bytes 16777216 | tf_op jit(solution)/shard_map/all_to_all | solution.py:263
  154.6 102.0 %collective-permute-start.4 = (bf16[512,13312]{1,0:T(8,128)(2,1)}, bf16[512,13312]{1,0:T(8,128)(2,1)}, u32[]{:S(2)}, u32[]{:S(2)}) collective-permute-start(bf16[512,13312]{1,0:T(8,128)(2,1)} %get-tuple-element.11.own_ref), channel_id=1, source_target_pairs={{0,4},{4,0},{8,12},{12,8},{16,20},{20,16},{24,28},{28,24},{32,36},... | collective-permute-start | bytes 40894472 | tf_op jit(solution)/shard_map/ppermute | solution.py:285
  200.0 10.7 %collective-permute-start = (f32[128,512]{1,0:T(8,128)S(1)}, f32[128,512]{1,0:T(8,128)S(1)}, u32[]{:S(2)}, u32[]{:S(2)}) collective-permute-start(f32[128,512]{1,0:T(8,128)S(1)} %reduce_sum.77), channel_id=1, source_target_pairs={{0,3},{1,0},{2,1},{3,2},{4,7},{5,4},{6,5},{7,6},{8,11},{9,8},{10,9... | collective-permute-start | bytes 786440 | tf_op jit(solution)/shard_map/ppermute | solution.py:301
  201.2 10.8 %collective-permute-start.1 = (f32[128,512]{1,0:T(8,128)S(1)}, f32[128,512]{1,0:T(8,128)S(1)}, u32[]{:S(2)}, u32[]{:S(2)}) collective-permute-start(f32[128,512]{1,0:T(8,128)S(1)} %reduce_sum.77), channel_id=1, source_target_pairs={{0,2},{1,3},{2,0},{3,1},{4,6},{5,7},{6,4},{7,5},{8,10},{9,11},{10,... | collective-permute-start | bytes 786440 | tf_op jit(solution)/shard_map/ppermute | solution.py:301
  203.0 21.7 %collective-permute-start.2 = (f32[128,512]{1,0:T(8,128)S(1)}, f32[128,512]{1,0:T(8,128)S(1)}, u32[]{:S(2)}, u32[]{:S(2)}) collective-permute-start(f32[128,512]{1,0:T(8,128)S(1)} %reduce_sum.77), channel_id=1, source_target_pairs={{0,1},{1,2},{2,3},{3,0},{4,5},{5,6},{6,7},{7,4},{8,9},{9,10},{10,1... | collective-permute-start | bytes 786440 | tf_op jit(solution)/shard_map/ppermute | solution.py:301
  204.1 25.6 %all-to-all-start.4 = ((f32[128,4,512]{2,1,0:T(4,128)}), f32[128,4,512]{2,1,0:T(4,128)S(1)}, u32[]{:S(2)}, u32[]{:S(2)}) async-start(f32[128,4,512]{2,1,0:T(4,128)} %broadcast_in_dim.57), calls=%async_computation.4 | async-start | bytes 2097152 | tf_op jit(solution)/shard_map/all_to_all | solution.py:297
  224.9 27.7 %collective-permute-start.3 = (f32[512,512]{1,0:T(8,128)S(1)}, f32[512,512]{1,0:T(8,128)}, u32[]{:S(2)}, u32[]{:S(2)}) collective-permute-start(f32[512,512]{1,0:T(8,128)S(1)} %bitcast.35), channel_id=1, source_target_pairs={{0,4},{4,0},{8,12},{12,8},{16,20},{20,16},{24,28},{28,24},{32,36},... | collective-permute-start | bytes 3145736 | tf_op jit(solution)/shard_map/ppermute | solution.py:307

commit v5 on v4

--- a/solution.py
+++ b/solution.py
@@ -211,27 +211,97 @@
     )(gram)
 
 
-def product_kernel(left_ref, own_ref, other_ref, out_ref):
+FAR = 2
+FORWARD = ((2, 0), (2, 1)) + tuple((1, e) for e in range(4))
+BACKWARD = ((2, 2), (2, 3)) + tuple((3, e) for e in range(4))
+STAY = tuple((0, e) for e in range(4))
+PIECES = FORWARD + BACKWARD + STAY
+
+
+def basis_kernel(at_ref, inverse_ref, own_ref, other_ref, left_ref, turned_ref, basis_ref, chosen):
+    pieces = len(PIECES)
+    size = chosen.shape[0] // pieces
+    panel = own_ref.shape[0]
+    for k in range(pieces):
+        chosen[k * size : (k + 1) * size, :] = inverse_ref[
+            pl.ds(pl.multiple_of(at_ref[k], size), size), :
+        ]
+    contract = (((1,), (1,)), ((), ()))
+    for i, sketch_ref in enumerate((own_ref, other_ref)):
+        left = lax.dot_general(
+            chosen[...], sketch_ref[...], contract, precision=HIGHEST, preferred_element_type=jnp.float32
+        ).astype(left_ref.dtype)
+        left_ref[:, i * panel : (i + 1) * panel] = left
+        turned_ref[:, i * panel : (i + 1) * panel] = jnp.concatenate(
+            [left[PIECES.index((b, a)) * size :][:size] for a, b in PIECES], axis=0
+        )
+    width = basis_ref.shape[1]
+    basis_ref[...] = lax.dot_general(
+        own_ref[...],
+        inverse_ref[pl.ds(pl.multiple_of(at_ref[pieces], width), width), :],
+        contract,
+        precision=HIGHEST,
+        preferred_element_type=jnp.float32,
+    ).astype(basis_ref.dtype)
+
+
+def basis_parts(at, inverse, own, other, half, width):
+    panel, rank = own.shape
+    whole = pl.BlockSpec(memory_space=pltpu.VMEM)
+    return pl.pallas_call(
+        basis_kernel,
+        grid_spec=pltpu.PrefetchScalarGridSpec(
+            num_scalar_prefetch=1,
+            grid=(),
+            in_specs=[whole] * 3,
+            out_specs=[whole] * 3,
+            scratch_shapes=[pltpu.VMEM((half, rank), jnp.float32)],
+        ),
+        out_shape=[
+            jax.ShapeDtypeStruct((half, 2 * panel), jnp.bfloat16),
+            jax.ShapeDtypeStruct((half, 2 * panel), jnp.bfloat16),
+            jax.ShapeDtypeStruct((panel, width), jnp.bfloat16),
+        ],
+        compiler_params=pltpu.CompilerParams(vmem_limit_bytes=32 * MIB),
+        cost_estimate=pl.CostEstimate(
+            flops=12 * rank * panel * (2 * half + width), bytes_accessed=6 * rank * panel, transcendentals=0
+        ),
+        name="basis_parts",
+    )(at, inverse, own, other)
+
+
+def product_kernel(scale, left_ref, own_ref, other_ref, *out_refs):
     rows = own_ref.shape[0]
     total = jnp.dot(left_ref[:, :rows], own_ref[...], preferred_element_type=jnp.float32)
     total += jnp.dot(left_ref[:, rows:], other_ref[...], preferred_element_type=jnp.float32)
-    out_ref[...] = total.astype(out_ref.dtype)
-
-
-def product(left, own, other, width):
+    total *= scale
+    start = 0
+    for out_ref in out_refs:
+        end = start + out_ref.shape[0]
+        out_ref[...] = total[start:end].astype(out_ref.dtype)
+        start = end
+
+
+def product(left, own, other, part, parts, width, scale):
     rows, cols = own.shape
     half = left.shape[0]
-    spec = pl.BlockSpec((rows, width), lambda k: (0, k))
+    steps = cols // parts // width
+    size = half // len(PIECES)
+    heights = [size * len(g) for g in (FORWARD, BACKWARD, STAY)]
+    spec = pl.BlockSpec((rows, width), lambda k: (0, part * steps + k))
     return pl.pallas_call(
-        product_kernel,
-        grid=(cols // width,),
+        functools.partial(product_kernel, scale),
+        grid=(steps,),
         in_specs=[pl.BlockSpec((half, 2 * rows), lambda k: (0, 0)), spec, spec],
-        out_specs=pl.BlockSpec((half, width), lambda k: (0, k)),
-        out_shape=jax.ShapeDtypeStruct((half, cols), jnp.bfloat16),
-        compiler_params=pltpu.CompilerParams(vmem_limit_bytes=56 * MIB),
+        out_specs=[pl.BlockSpec((height, width), lambda k: (0, k)) for height in heights],
+        out_shape=[
+            jax.ShapeDtypeStruct((height, cols // parts), jnp.float32 if i == 2 else jnp.bfloat16)
+            for i, height in enumerate(heights)
+        ],
+        compiler_params=pltpu.CompilerParams(vmem_limit_bytes=40 * MIB),
         cost_estimate=pl.CostEstimate(
-            flops=2 * half * 2 * rows * cols,
-            bytes_accessed=4 * rows * cols + 2 * half * cols,
+            flops=4 * half * rows * cols // parts,
+            bytes_accessed=(4 * rows * cols + 2 * half * cols) // parts,
             transcendentals=0,
         ),
         name="product",
@@ -308,29 +378,41 @@
     inverse = inverse_factor(gram, 1.0 / total_rows)
 
     ranks = rank // row_devices
-    half = rank // 2
     chips = row_devices // 2
-    both = jnp.concatenate([sketch, other_sketch], axis=0)
-    my_ranks = lax.dynamic_index_in_dim(
-        inverse.reshape(chips, 2, ranks, rank), core, 1, keepdims=False
-    ).reshape(half, rank)
-    left = lax.dot_general(
-        my_ranks, both, (((1,), (1,)), ((), ())), precision=HIGHEST, preferred_element_type=jnp.float32
-    ).astype(jnp.bfloat16)
-
-    slice_width = rank // col_devices
-    my_rows = lax.dynamic_slice_in_dim(inverse, lax.axis_index("cols") * slice_width, slice_width, 0)
-    basis = lax.dot_general(
-        sketch, my_rows, (((1,), (1,)), ((), ())), precision=HIGHEST, preferred_element_type=jnp.float32
-    ).astype(jnp.bfloat16)
-
-    groups = [[2 * i + c for i in range(chips)] for c in range(2)]
-    scaling = 1.0 / math.sqrt(total_rows)
-    terms = product(left, tile, other_tile, cols // 4).reshape(chips, ranks, cols)
-    terms, basis = lax.optimization_barrier((terms, basis))
-    terms = lax.all_to_all(terms, "rows", 0, 0, axis_index_groups=groups, tiled=True)
-    coefficients = jnp.sum(terms.astype(jnp.float32), axis=0) * scaling
-
+    along = math.isqrt(chips)
+    chip = lax.axis_index("rows") // 2
+    x, y = chip // along, chip % along
+    at = [(((x + a) % along * along + (y + b) % along) * 2 + core) * ranks for a, b in PIECES]
+    width = rank // col_devices
+    at.append(lax.axis_index("cols") * width)
+    left, turned, basis = basis_parts(
+        jnp.stack(at).astype(jnp.int32), inverse, sketch, other_sketch, rank // 2, width
+    )
+
+    def shift(over_x, steps):
+        moves = []
+        for i in range(row_devices):
+            a, b = i // 2 // along, i // 2 % along
+            a, b = ((a + steps) % along, b) if over_x else (a, (b + steps) % along)
+            moves.append((i, (a * along + b) * 2 + i % 2))
+        return functools.partial(lax.ppermute, axis_name="rows", perm=moves)
+
+    def scatter(part, factor, x_first):
+        ahead, behind, total = product(
+            factor, tile, other_tile, part, 2, cols // 4, 1.0 / math.sqrt(total_rows)
+        )
+        forward, backward = shift(x_first, 1), shift(x_first, -1)
+        ahead, behind = forward(ahead), backward(behind)
+        far, back_far = forward(ahead[: FAR * ranks]), backward(behind[: FAR * ranks])
+        total += ahead[FAR * ranks :].astype(jnp.float32) + behind[FAR * ranks :].astype(jnp.float32)
+        total += jnp.concatenate([far, back_far], axis=0).astype(jnp.float32)
+        terms = [total[i * ranks : (i + 1) * ranks] for i in range(along)]
+        result = terms[0]
+        for i in range(1, along):
+            result += shift(not x_first, i)(terms[i].astype(jnp.bfloat16)).astype(jnp.float32)
+        return result
+
+    coefficients = jnp.concatenate([scatter(0, left, True), scatter(1, turned, False)], axis=1)
     return basis, coefficients
 
 

time: 359 us -> 338 us (0.942)
  blocking collectives: 126 us -> 46.1 us
  waiting for transfers between devices: 128 us -> 171 us
  starting transfers between devices: 27.2 us -> 47 us
  matrix products: 6.58 us -> 0.98 us
  Pallas kernels: 57.3 us -> 61.3 us
    all_to_all x1 -> x0, blocking collectives: 83.2 us -> none  [on_device(): lax.all_to_all(terms, 'rows', 0, 0, axis_index_groups=groups, tiled=True)]
    ppermute x0 -> x14, waiting for transfers between devices: none -> 43.4 us  [the longest x4 24.1 us: scatter(): ahead, behind = (forward(ahead), backward(behind))]
    ppermute x0 -> x14, starting transfers between devices: none -> 19 us  [the longest x4 6.83 us: scatter(): ahead, behind = (forward(ahead), backward(behind))]
    dot_general x2 -> x0, matrix products: 5.6 us -> none  [the longest x1 3.94 us: on_device(): lax.dot_general(my_ranks, both, (((1,), (1,)), ((), ())), precision=HIGHE...]
    pallas_call x1 -> x3, Pallas kernels: 14.6 us -> 18.4 us  [the longest x2 14.4 us: product(): pl.pallas_call(functools.partial(product_kernel, scale), grid=(steps,), i...]
  transfers between devices with their start and end apart: 8 -> 22, of which waited for: 5 -> 10; matrix products, arithmetic and copies ran while one was open for 3% -> 2% of each run, Pallas kernels for 7% -> 11%
where the time goes in v5:
time: 338 us
  waiting for transfers between devices  171 us (51%)
  Pallas kernels  61.3 us (18%)
  starting transfers between devices  47 us (14%)
  blocking collectives  46.1 us (14%)
  other arithmetic  6.03 us (2%)
  local copies, waits for them, and re-layouts  4.96 us (1%)
    all_to_all x1, waiting for transfers between devices, on_device(): lax.all_to_all(send_blocks.reshape(devices_all, capacity, BLK, BLK), ever...  106 us
    all_to_all x1, blocking collectives, on_device(): lax.all_to_all(local_gram.reshape(devices_all, rank // devices_all, rank)...  26.8 us
    ppermute x4, waiting for transfers between devices, scatter(): ahead, behind = (forward(ahead), backward(behind))  24.1 us
    pallas_call x1, Pallas kernels, inverse_factor(): pl.pallas_call(functools.partial(factor_kernel, scale), in_specs=[pl.Bloc...  20.8 us
    all_to_all x1, blocking collectives, on_device(): lax.all_to_all(part.reshape(col_devices, share, rank), 'cols', 0, 0, tile...  19.3 us
    pallas_call x1, Pallas kernels, tile_and_sketch(): pl.pallas_call(tile_kernel, grid_spec=pltpu.PrefetchScalarGridSpec(num_sc...  17.1 us
    pallas_call x2, Pallas kernels, product(): pl.pallas_call(functools.partial(product_kernel, scale), grid=(steps,), i...  14.4 us
    ppermute x3, waiting for transfers between devices, on_device(): lax.ppermute(late_share, 'cols', [(i, (i + d) % col_devices) for i in ran...  13.1 us
  transfers between devices with their start and end apart: 22, of which 10 were waited for; matrix products, arithmetic and copies ran while one was open for 2% of the time, Pallas kernels for 11%

profile of v5, /device:TPU:0, one launch (start us, length us, event | category | flops | bytes accessed | tf_op | source)
XLA Modules:
  0.0 338.4 jit_solution(7580071732586656658)
XLA Ops:
  0.6 0.9 convert_reduce_fusion.1
  1.5 0.7 multiply_add_fusion
  2.2 0.1 select_reduce_fusion.1
  2.3 0.8 all_to_all.18
  3.1 11.1 %all-to-all-start = ((s32[128,1,2]{2,1,0:T(1,128)}), s32[128,1,2]{2,1,0:T(1,128)S(1)}, u32[]{:S(2)}, u32[]{:S(2)}) async-start(s32[128,1,2]{2,1,0:T(1,128)} %bitcast.18), calls=%async_computation | async-start | bytes 131072 | tf_op jit(solution)/shard_map/all_to_all | solution.py:336
  14.3 5.0 %bucket.1 = bf16[256,128,128]{2,1,0:T(8,128)(2,1)} custom-call(s32[128]{0:T(128)} %copy-done, bf16[128,128,128]{2,1,0:T(8,128)(2,1)} %blocks_ref.1), custom_call_target="tpu_custom_call" | custom-call | bytes 8388608 | tf_op jit(solution)/shard_map/bucket/pallas_call | solution.py:30
  19.2 4.0 %all-to-all-done = s32[128,1,2]{2,1,0:T(1,128)S(1)} async-done(((s32[128,1,2]{2,1,0:T(1,128)}), s32[128,1,2]{2,1,0:T(1,128)S(1)}, u32[]{:S(2)}, u32[]{:S(2)}) %all-to-all-start) | async-done | bytes 1056 | tf_op jit(solution)/shard_map/all_to_all | solution.py:336
  23.2 6.3 %all-to-all-start.1 = ((bf16[128,2,128,128]{3,2,1,0:T(8,128)(2,1)}), bf16[128,2,128,128]{3,2,1,0:T(8,128)(2,1)}, u32[]{:S(2)}, u32[]{:S(2)}) async-start(bf16[128,2,128,128]{3,2,1,0:T(8,128)(2,1)} %bitcast.46), calls=%async_computation.1 | async-start | bytes 16777216 | tf_op jit(solution)/shard_map/all_to_all | solution.py:333
  29.5 0.9 fusion.16
  30.4 0.1 select_n.161
  30.6 0.2 convert_reduce_fusion
  30.8 0.1 select_reduce_fusion
  30.9 0.1 slice_compare_fusion
  31.0 0.1 add_convert_fusion
  31.1 0.1 fusion.15
  31.1 0.7 pad_add_fusion.code_ref
  31.8 105.8 %all-to-all-done.1 = bf16[128,2,128,128]{3,2,1,0:T(8,128)(2,1)} async-done(((bf16[128,2,128,128]{3,2,1,0:T(8,128)(2,1)}), bf16[128,2,128,128]{3,2,1,0:T(8,128)(2,1)}, u32[]{:S(2)}, u32[]{:S(2)}) %all-to-all-start.1) | async-done | bytes 8388640 | tf_op jit(solution)/shard_map/all_to_all | solution.py:333
  137.6 17.1 %tile_and_sketch.1 = (bf16[512,13312]{1,0:T(8,128)(2,1)}, f32[512,512]{1,0:T(8,128)S(1)}) custom-call(s32[257]{0:T(512)S(1)} %pad_add_fusion.code_ref, bf16[256,128,128]{2,1,0:T(8,128)(2,1)} %bitcast.21.got_hbm, bf16[13312,512]{1,0:T(8,128)(2,1)} %omega_hbm.1), custom_call_target="tpu_custom_call" | custom-call | flops 6979321856 | bytes 35651584 | tf_op jit(solution)/shard_map/tile_and_sketch/pallas_call | solution.py:103
  154.7 0.1 collective-permute-start.4
  154.8 19.3 %all_to_all.29 = f32[4,128,512]{2,1,0:T(8,128)S(1)} all-to-all(f32[4,128,512]{2,1,0:T(8,128)S(1)} %bitcast.45), channel_id=1, replica_groups=mesh['rows'=32,'cols'=4] {'cols'}, dimensions={0} | all-to-all | bytes 2097152 | tf_op jit(solution)/shard_map/all_to_all | solution.py:358
  174.1 0.1 reduce_sum.68
  174.2 0.1 copy.14
  174.3 1.0 fusion.4
  175.3 0.7 copy.16
  176.0 26.8 %all_to_all.30 = f32[128,4,512]{2,1,0:T(4,128)S(1)} all-to-all(f32[128,4,512]{2,1,0:T(4,128)S(1)} %copy.16), channel_id=1, replica_groups=mesh['rows'=32,'cols'=4] {'rows','cols'}, dimensions={0} | all-to-all | bytes 2097152 | tf_op jit(solution)/shard_map/all_to_all | solution.py:363
  202.8 0.2 reduce_sum.69
  203.0 1.2 collective-permute-start
  204.2 1.8 collective-permute-start.1
  205.9 0.1 stack.90.at_ref
  206.0 0.1 collective-permute-start.2
  206.1 1.1 broadcast_in_dim.57
  207.2 7.2 %all-to-all-start.4 = ((f32[128,4,512]{2,1,0:T(4,128)}), f32[128,4,512]{2,1,0:T(4,128)}, u32[]{:S(2)}, u32[]{:S(2)}) async-start(f32[128,4,512]{2,1,0:T(4,128)} %broadcast_in_dim.57), calls=%async_computation.4 | async-start | bytes 2097152 | tf_op jit(solution)/shard_map/all_to_all | solution.py:367
  214.5 0.5 collective-permute-done.1
  215.0 12.5 %collective-permute-done.2 = f32[128,512]{1,0:T(8,128)S(1)} collective-permute-done((f32[128,512]{1,0:T(8,128)S(1)}, f32[128,512]{1,0:T(8,128)S(1)}, u32[]{:S(2)}, u32[]{:S(2)}) %collective-permute-start.2) | collective-permute-done | bytes 262176 | tf_op jit(solution)/shard_map/ppermute | solution.py:371
  227.7 0.1 constant_dynamic-slice_fusion
  227.8 0.3 collective-permute-start.3
  228.0 4.9 %all-to-all-done.4 = f32[128,4,512]{2,1,0:T(4,128)} async-done(((f32[128,4,512]{2,1,0:T(4,128)}), f32[128,4,512]{2,1,0:T(4,128)}, u32[]{:S(2)}, u32[]{:S(2)}) %all-to-all-start.4) | async-done | bytes 1048608 | tf_op jit(solution)/shard_map/all_to_all | solution.py:367
  232.9 1.6 reshape.90.gram_ref
  234.5 20.8 %inverse_factor.1.inverse_ref = f32[512,512]{1,0:T(8,128)S(1)} custom-call(f32[512,512]{1,0:T(8,128)S(1)} %reshape.90.gram_ref), custom_call_target="tpu_custom_call" | custom-call | flops 34359738368 | bytes 2097152 | tf_op jit(solution)/shard_map/inverse_factor/pallas_call | solution.py:200
  255.4 4.0 %basis_parts.1 = (bf16[256,1024]{1,0:T(8,128)(2,1)S(1)}, bf16[256,1024]{1,0:T(8,128)(2,1)S(1)}, bf16[512,128]{1,0:T(8,128)(2,1)}) custom-call(s32[17]{0:T(128)S(1)} %stack.90.at_ref, f32[512,512]{1,0:T(8,128)S(1)} %inverse_factor.1.inverse_ref, f32[512,512]{1,0:T(8,128)S(1)} %bitcast.44, f32[512,512]{1,0:T(8,128)S(1)} %collective-permute-done.3.other_ref), custom_call_target="tpu_custom_call" | custom-call | flops 2013265920 | bytes 1572864 | tf_op jit(solution)/shard_map/basis_parts/pallas_call | solution.py:251
  259.3 7.2 %product.2 = (bf16[96,6656]{1,0:T(8,128)(2,1)S(1)}, bf16[96,6656]{1,0:T(8,128)(2,1)S(1)}, f32[64,6656]{1,0:T(8,128)S(1)}) custom-call(bf16[256,1024]{1,0:T(8,128)(2,1)S(1)} %get-tuple-element.19.left_ref, bf16[512,13312]{1,0:T(8,128)(2,1)} %get-tuple-element.20.own_ref, bf16[512,13312]{1,0:T(8,128)(2,1)} %collective-permute-done.4.other_ref), custom_call_target="tpu_custom_call" | custom-call | flops 3489660928 | bytes 17039360 | tf_op jit(solution)/shard_map/product/pallas_call | solution.py:292
  266.6 0.6 collective-permute-start.5
  267.2 2.7 collective-permute-start.6
  269.9 7.2 %product.3 = (bf16[96,6656]{1,0:T(8,128)(2,1)S(1)}, bf16[96,6656]{1,0:T(8,128)(2,1)S(1)}, f32[64,6656]{1,0:T(8,128)S(1)}) custom-call(bf16[256,1024]{1,0:T(8,128)(2,1)S(1)} %get-tuple-element.24.left_ref, bf16[512,13312]{1,0:T(8,128)(2,1)} %get-tuple-element.20.own_ref, bf16[512,13312]{1,0:T(8,128)(2,1)} %collective-permute-done.4.other_ref), custom_call_target="tpu_custom_call" | custom-call | flops 3489660928 | bytes 17039360 | tf_op jit(solution)/shard_map/product/pallas_call | solution.py:292
  277.1 0.8 collective-permute-start.12
  277.8 2.8 collective-permute-start.13
  280.6 17.3 %collective-permute-done.5 = bf16[96,6656]{1,0:T(8,128)(2,1)S(1)} collective-permute-done((bf16[96,6656]{1,0:T(8,128)(2,1)S(1)}, bf16[96,6656]{1,0:T(8,128)(2,1)S(1)}, u32[]{:S(2)}, u32[]{:S(2)}) %collective-permute-start.5) | collective-permute-done | bytes 1277984 | tf_op jit(solution)/shard_map/ppermute | solution.py:405
  298.0 0.1 collective-permute-start.7
  298.1 3.3 collective-permute-start.8
  301.4 6.7 %collective-permute-done.12 = bf16[96,6656]{1,0:T(8,128)(2,1)S(1)} collective-permute-done((bf16[96,6656]{1,0:T(8,128)(2,1)S(1)}, bf16[96,6656]{1,0:T(8,128)(2,1)S(1)}, u32[]{:S(2)}, u32[]{:S(2)}) %collective-permute-start.12) | collective-permute-done | bytes 1277984 | tf_op jit(solution)/shard_map/ppermute | solution.py:405
  308.3 3.3 collective-permute-start.15
  311.6 0.4 fusion.17
  312.0 0.1 collective-permute-start.10
  312.1 1.5 collective-permute-start.11
  313.5 0.6 collective-permute-start.9
  314.2 12.5 %collective-permute-done.14 = bf16[32,6656]{1,0:T(8,128)(2,1)S(1)} collective-permute-done((bf16[32,6656]{1,0:T(8,128)(2,1)S(1)}, bf16[32,6656]{1,0:T(8,128)(2,1)S(1)}, u32[]{:S(2)}, u32[]{:S(2)}) %collective-permute-start.14) | collective-permute-done | bytes 426016 | tf_op jit(solution)/shard_map/ppermute | solution.py:406
  326.6 0.4 fusion.18
  327.2 1.8 collective-permute-start.17
  329.0 1.4 collective-permute-start.18
  330.4 0.1 fusion.3
  330.5 6.0 %collective-permute-done.16 = bf16[16,6656]{1,0:T(8,128)(2,1)S(1)} collective-permute-done((bf16[16,6656]{1,0:T(8,128)(2,1)S(1)}, bf16[16,6656]{1,0:T(8,128)(2,1)S(1)}, u32[]{:S(2)}, u32[]{:S(2)}) %collective-permute-start.16) | collective-permute-done | bytes 213024 | tf_op jit(solution)/shard_map/ppermute | solution.py:412
  336.5 0.9 collective-permute-done.18
  337.4 0.1 fusion.1
  337.5 1.0 pad_maximum_fusion
  (32 shorter events, 0.6 us)
Async XLA Ops:
  2.2 12.0 %copy-start = (s32[128]{0:T(128)}, s32[128]{0:T(128)S(1)}, u32[]{:S(2)}) copy-start(s32[128]{0:T(128)S(1)} %get-tuple-element.40.place_ref) | copy-start | bytes 1540
  3.1 20.1 %all-to-all-start = ((s32[128,1,2]{2,1,0:T(1,128)}), s32[128,1,2]{2,1,0:T(1,128)S(1)}, u32[]{:S(2)}, u32[]{:S(2)}) async-start(s32[128,1,2]{2,1,0:T(1,128)} %bitcast.18), calls=%async_computation | async-start | bytes 131072 | tf_op jit(solution)/shard_map/all_to_all | solution.py:336
  23.2 114.3 %all-to-all-start.1 = ((bf16[128,2,128,128]{3,2,1,0:T(8,128)(2,1)}), bf16[128,2,128,128]{3,2,1,0:T(8,128)(2,1)}, u32[]{:S(2)}, u32[]{:S(2)}) async-start(bf16[128,2,128,128]{3,2,1,0:T(8,128)(2,1)} %bitcast.46), calls=%async_computation.1 | async-start | bytes 16777216 | tf_op jit(solution)/shard_map/all_to_all | solution.py:333
  154.7 104.6 %collective-permute-start.4 = (bf16[512,13312]{1,0:T(8,128)(2,1)}, bf16[512,13312]{1,0:T(8,128)(2,1)}, u32[]{:S(2)}, u32[]{:S(2)}) collective-permute-start(bf16[512,13312]{1,0:T(8,128)(2,1)} %get-tuple-element.20.own_ref), channel_id=1, source_target_pairs={{0,4},{4,0},{8,12},{12,8},{16,20},{20,16},{24,28},{28,24},{32,36},... | collective-permute-start | bytes 40894472 | tf_op jit(solution)/shard_map/ppermute | solution.py:355
  203.0 11.5 %collective-permute-start = (f32[128,512]{1,0:T(8,128)S(1)}, f32[128,512]{1,0:T(8,128)S(1)}, u32[]{:S(2)}, u32[]{:S(2)}) collective-permute-start(f32[128,512]{1,0:T(8,128)S(1)} %reduce_sum.68), channel_id=1, source_target_pairs={{0,3},{1,0},{2,1},{3,2},{4,7},{5,4},{6,5},{7,6},{8,11},{9,8},{10,9... | collective-permute-start | bytes 786440 | tf_op jit(solution)/shard_map/ppermute | solution.py:371
  204.2 10.8 %collective-permute-start.1 = (f32[128,512]{1,0:T(8,128)S(1)}, f32[128,512]{1,0:T(8,128)S(1)}, u32[]{:S(2)}, u32[]{:S(2)}) collective-permute-start(f32[128,512]{1,0:T(8,128)S(1)} %reduce_sum.68), channel_id=1, source_target_pairs={{0,2},{1,3},{2,0},{3,1},{4,6},{5,7},{6,4},{7,5},{8,10},{9,11},{10,... | collective-permute-start | bytes 786440 | tf_op jit(solution)/shard_map/ppermute | solution.py:371
  206.0 21.5 %collective-permute-start.2 = (f32[128,512]{1,0:T(8,128)S(1)}, f32[128,512]{1,0:T(8,128)S(1)}, u32[]{:S(2)}, u32[]{:S(2)}) collective-permute-start(f32[128,512]{1,0:T(8,128)S(1)} %reduce_sum.68), channel_id=1, source_target_pairs={{0,1},{1,2},{2,3},{3,0},{4,5},{5,6},{6,7},{7,4},{8,9},{9,10},{10,1... | collective-permute-start | bytes 786440 | tf_op jit(solution)/shard_map/ppermute | solution.py:371
  207.2 25.7 %all-to-all-start.4 = ((f32[128,4,512]{2,1,0:T(4,128)}), f32[128,4,512]{2,1,0:T(4,128)}, u32[]{:S(2)}, u32[]{:S(2)}) async-start(f32[128,4,512]{2,1,0:T(4,128)} %broadcast_in_dim.57), calls=%async_computation.4 | async-start | bytes 2097152 | tf_op jit(solution)/shard_map/all_to_all | solution.py:367
  227.8 27.6 %collective-permute-start.3 = (f32[512,512]{1,0:T(8,128)S(1)}, f32[512,512]{1,0:T(8,128)S(1)}, u32[]{:S(2)}, u32[]{:S(2)}) collective-permute-start(f32[512,512]{1,0:T(8,128)S(1)} %bitcast.43), channel_id=1, source_target_pairs={{0,4},{4,0},{8,12},{12,8},{16,20},{20,16},{24,28},{28,24},{32,36},... | collective-permute-start | bytes 3145736 | tf_op jit(solution)/shard_map/ppermute | solution.py:377
  266.6 31.4 %collective-permute-start.5 = (bf16[96,6656]{1,0:T(8,128)(2,1)S(1)}, bf16[96,6656]{1,0:T(8,128)(2,1)S(1)}, u32[]{:S(2)}, u32[]{:S(2)}) collective-permute-start(bf16[96,6656]{1,0:T(8,128)(2,1)S(1)} %get-tuple-element.22), channel_id=1, source_target_pairs={{0,32},{4,36},{8,40},{12,44},{16,48},{20,52},{24,56},{28,60},{32,6... | collective-permute-start | bytes 3833864 | tf_op jit(solution)/shard_map/ppermute | solution.py:405
  267.2 30.8 %collective-permute-start.6 = (bf16[96,6656]{1,0:T(8,128)(2,1)S(1)}, bf16[96,6656]{1,0:T(8,128)(2,1)S(1)}, u32[]{:S(2)}, u32[]{:S(2)}) collective-permute-start(bf16[96,6656]{1,0:T(8,128)(2,1)S(1)} %get-tuple-element.23), channel_id=1, source_target_pairs={{0,96},{4,100},{8,104},{12,108},{16,112},{20,116},{24,120},{28,124... | collective-permute-start | bytes 3833864 | tf_op jit(solution)/shard_map/ppermute | solution.py:405
  277.1 31.0 %collective-permute-start.12 = (bf16[96,6656]{1,0:T(8,128)(2,1)S(1)}, bf16[96,6656]{1,0:T(8,128)(2,1)S(1)}, u32[]{:S(2)}, u32[]{:S(2)}) collective-permute-start(bf16[96,6656]{1,0:T(8,128)(2,1)S(1)} %get-tuple-element.26), channel_id=1, source_target_pairs={{0,8},{4,12},{8,16},{12,20},{16,24},{20,28},{24,0},{28,4},{32,40},... | collective-permute-start | bytes 3833864 | tf_op jit(solution)/shard_map/ppermute | solution.py:405
  277.8 30.4 %collective-permute-start.13 = (bf16[96,6656]{1,0:T(8,128)(2,1)S(1)}, bf16[96,6656]{1,0:T(8,128)(2,1)S(1)}, u32[]{:S(2)}, u32[]{:S(2)}) collective-permute-start(bf16[96,6656]{1,0:T(8,128)(2,1)S(1)} %get-tuple-element.27), channel_id=1, source_target_pairs={{0,24},{4,28},{8,0},{12,4},{16,8},{20,12},{24,16},{28,20},{32,56},... | collective-permute-start | bytes 3833864 | tf_op jit(solution)/shard_map/ppermute | solution.py:405
  298.0 13.6 %collective-permute-start.7 = (bf16[32,6656]{1,0:T(8,128)(2,1)S(1)}, bf16[32,6656]{1,0:T(8,128)(2,1)S(1)}, u32[]{:S(2)}, u32[]{:S(2)}) collective-permute-start(bf16[32,6656]{1,0:T(8,128)(2,1)S(1)} %slice.84), channel_id=1, source_target_pairs={{0,32},{4,36},{8,40},{12,44},{16,48},{20,52},{24,56},{28,60},{32,6... | collective-permute-start | bytes 1277960 | tf_op jit(solution)/shard_map/ppermute | solution.py:406
  298.1 13.5 %collective-permute-start.8 = (bf16[32,6656]{1,0:T(8,128)(2,1)S(1)}, bf16[32,6656]{1,0:T(8,128)(2,1)S(1)}, u32[]{:S(2)}, u32[]{:S(2)}) collective-permute-start(bf16[32,6656]{1,0:T(8,128)(2,1)S(1)} %slice.85), channel_id=1, source_target_pairs={{0,96},{4,100},{8,104},{12,108},{16,112},{20,116},{24,120},{28,124... | collective-permute-start | bytes 1277960 | tf_op jit(solution)/shard_map/ppermute | solution.py:406
  308.1 18.5 %collective-permute-start.14 = (bf16[32,6656]{1,0:T(8,128)(2,1)S(1)}, bf16[32,6656]{1,0:T(8,128)(2,1)S(1)}, u32[]{:S(2)}, u32[]{:S(2)}) collective-permute-start(bf16[32,6656]{1,0:T(8,128)(2,1)S(1)} %slice.92), channel_id=1, source_target_pairs={{0,8},{4,12},{8,16},{12,20},{16,24},{20,28},{24,0},{28,4},{32,40},... | collective-permute-start | bytes 1277960 | tf_op jit(solution)/shard_map/ppermute | solution.py:406
  308.3 18.4 %collective-permute-start.15 = (bf16[32,6656]{1,0:T(8,128)(2,1)S(1)}, bf16[32,6656]{1,0:T(8,128)(2,1)S(1)}, u32[]{:S(2)}, u32[]{:S(2)}) collective-permute-start(bf16[32,6656]{1,0:T(8,128)(2,1)S(1)} %slice.93), channel_id=1, source_target_pairs={{0,24},{4,28},{8,0},{12,4},{16,8},{20,12},{24,16},{28,20},{32,56},... | collective-permute-start | bytes 1277960 | tf_op jit(solution)/shard_map/ppermute | solution.py:406
  312.0 17.0 %collective-permute-start.10 = (bf16[16,6656]{1,0:T(8,128)(2,1)S(1)}, bf16[16,6656]{1,0:T(8,128)(2,1)S(1)}, u32[]{:S(2)}, u32[]{:S(2)}) collective-permute-start(bf16[16,6656]{1,0:T(8,128)(2,1)S(1)} %get-tuple-element.36), channel_id=1, source_target_pairs={{0,16},{4,20},{8,24},{12,28},{16,0},{20,4},{24,8},{28,12},{32,48},... | collective-permute-start | bytes 638984 | tf_op jit(solution)/shard_map/ppermute | solution.py:412
  312.1 18.3 %collective-permute-start.11 = (bf16[16,6656]{1,0:T(8,128)(2,1)S(1)}, bf16[16,6656]{1,0:T(8,128)(2,1)S(1)}, u32[]{:S(2)}, u32[]{:S(2)}) collective-permute-start(bf16[16,6656]{1,0:T(8,128)(2,1)S(1)} %get-tuple-element.35), channel_id=1, source_target_pairs={{0,24},{4,28},{8,0},{12,4},{16,8},{20,12},{24,16},{28,20},{32,56},... | collective-permute-start | bytes 638984 | tf_op jit(solution)/shard_map/ppermute | solution.py:412
  313.5 16.9 %collective-permute-start.9 = (bf16[16,6656]{1,0:T(8,128)(2,1)S(1)}, bf16[16,6656]{1,0:T(8,128)(2,1)S(1)}, u32[]{:S(2)}, u32[]{:S(2)}) collective-permute-start(bf16[16,6656]{1,0:T(8,128)(2,1)S(1)} %get-tuple-element.34), channel_id=1, source_target_pairs={{0,8},{4,12},{8,16},{12,20},{16,24},{20,28},{24,0},{28,4},{32,40},... | collective-permute-start | bytes 638984 | tf_op jit(solution)/shard_map/ppermute | solution.py:412
  327.1 9.4 %collective-permute-start.16 = (bf16[16,6656]{1,0:T(8,128)(2,1)S(1)}, bf16[16,6656]{1,0:T(8,128)(2,1)S(1)}, u32[]{:S(2)}, u32[]{:S(2)}) collective-permute-start(bf16[16,6656]{1,0:T(8,128)(2,1)S(1)} %get-tuple-element.37), channel_id=1, source_target_pairs={{0,32},{4,36},{8,40},{12,44},{16,48},{20,52},{24,56},{28,60},{32,6... | collective-permute-start | bytes 638984 | tf_op jit(solution)/shard_map/ppermute | solution.py:412
  327.2 9.3 %collective-permute-start.17 = (bf16[16,6656]{1,0:T(8,128)(2,1)S(1)}, bf16[16,6656]{1,0:T(8,128)(2,1)S(1)}, u32[]{:S(2)}, u32[]{:S(2)}) collective-permute-start(bf16[16,6656]{1,0:T(8,128)(2,1)S(1)} %get-tuple-element.39), channel_id=1, source_target_pairs={{0,64},{4,68},{8,72},{12,76},{16,80},{20,84},{24,88},{28,92},{32,9... | collective-permute-start | bytes 638984 | tf_op jit(solution)/shard_map/ppermute | solution.py:412
  329.0 8.4 %collective-permute-start.18 = (bf16[16,6656]{1,0:T(8,128)(2,1)S(1)}, bf16[16,6656]{1,0:T(8,128)(2,1)S(1)}, u32[]{:S(2)}, u32[]{:S(2)}) collective-permute-start(bf16[16,6656]{1,0:T(8,128)(2,1)S(1)} %get-tuple-element.38), channel_id=1, source_target_pairs={{0,96},{4,100},{8,104},{12,108},{16,112},{20,116},{24,120},{28,124... | collective-permute-start | bytes 638984 | tf_op jit(solution)/shard_map/ppermute | solution.py:412

commit v6 on v5

--- a/solution.py
+++ b/solution.py
@@ -132,9 +132,53 @@
     )(code, got, omega)
 
 
+def upper_rows(n):
+    start = 0
+    for at in range(0, n, BLK):
+        yield at, start, n - at
+        start += n - at
+
+
+def gram_kernel(parts_ref, share_ref, packed_ref):
+    share = parts_ref[0]
+    for i in range(1, parts_ref.shape[0]):
+        share += parts_ref[i]
+    share_ref[...] = share
+    for at, start, width in upper_rows(share.shape[1]):
+        packed_ref[:, start : start + width] = lax.dot_general(
+            share[:, at : at + BLK],
+            share[:, at:],
+            (((0,), (0,)), ((), ())),
+            precision=HIGHEST,
+            preferred_element_type=jnp.float32,
+        )
+
+
+def share_and_gram(parts):
+    _, share, rank = parts.shape
+    packed = sum(width for _, _, width in upper_rows(rank))
+    whole = pl.BlockSpec(memory_space=pltpu.VMEM)
+    return pl.pallas_call(
+        gram_kernel,
+        in_specs=[whole],
+        out_specs=[whole] * 2,
+        out_shape=[
+            jax.ShapeDtypeStruct((share, rank), jnp.float32),
+            jax.ShapeDtypeStruct((BLK, packed), jnp.float32),
+        ],
+        compiler_params=pltpu.CompilerParams(vmem_limit_bytes=24 * MIB),
+        cost_estimate=pl.CostEstimate(
+            flops=12 * share * rank * rank, bytes_accessed=8 * parts.size, transcendentals=0
+        ),
+        name="share_and_gram",
+    )(parts)
+
+
 def factor_kernel(scale, gram_ref, out_ref, work):
-    n = gram_ref.shape[0]
-    work[...] = gram_ref[...] * scale
+    n = work.shape[0]
+    work[...] = jnp.zeros_like(work)
+    for at, start, width in upper_rows(n):
+        work[at : at + BLK, at:] = gram_ref[:, start : start + width] * scale
     row = lax.broadcasted_iota(jnp.int32, (n, n), 0)
     lane = lax.broadcasted_iota(jnp.int32, (n, n), 1)
     out_ref[...] = jnp.where(row == lane, 1.0, 0.0)
@@ -195,8 +239,7 @@
     lax.fori_loop(0, n // BLK, block, 0)
 
 
-def inverse_factor(gram, scale):
-    n = gram.shape[0]
+def inverse_factor(gram, n, scale):
     return pl.pallas_call(
         functools.partial(factor_kernel, scale),
         in_specs=[pl.BlockSpec(memory_space=pltpu.VMEM)],
@@ -282,26 +325,28 @@
         start = end
 
 
-def product(left, own, other, part, parts, width, scale):
-    rows, cols = own.shape
+def product(left, own, other, first, width, steps, scale):
+    rows = own.shape[0]
     half = left.shape[0]
-    steps = cols // parts // width
+    count = width * steps
     size = half // len(PIECES)
     heights = [size * len(g) for g in (FORWARD, BACKWARD, STAY)]
-    spec = pl.BlockSpec((rows, width), lambda k: (0, part * steps + k))
+    spec = pl.BlockSpec(
+        (pl.Element(rows), pl.Element(width)), lambda k: (0, pl.multiple_of(first + k * width, BLK))
+    )
     return pl.pallas_call(
         functools.partial(product_kernel, scale),
         grid=(steps,),
         in_specs=[pl.BlockSpec((half, 2 * rows), lambda k: (0, 0)), spec, spec],
         out_specs=[pl.BlockSpec((height, width), lambda k: (0, k)) for height in heights],
         out_shape=[
-            jax.ShapeDtypeStruct((height, cols // parts), jnp.float32 if i == 2 else jnp.bfloat16)
+            jax.ShapeDtypeStruct((height, count), jnp.float32 if i == 2 else jnp.bfloat16)
             for i, height in enumerate(heights)
         ],
         compiler_params=pltpu.CompilerParams(vmem_limit_bytes=40 * MIB),
         cost_estimate=pl.CostEstimate(
-            flops=4 * half * rows * cols // parts,
-            bytes_accessed=(4 * rows * cols + 2 * half * cols) // parts,
+            flops=4 * half * rows * count,
+            bytes_accessed=(4 * rows + 2 * half) * count,
             transcendentals=0,
         ),
         name="product",
@@ -356,17 +401,14 @@
 
     share = panel // col_devices
     parts = lax.all_to_all(part.reshape(col_devices, share, rank), "cols", 0, 0, tiled=True)
-    own_share = jnp.sum(parts, axis=0)
-    local_gram = lax.dot_general(
-        own_share, own_share, (((0,), (0,)), ((), ())), precision=HIGHEST, preferred_element_type=jnp.float32
-    )
-    grams = lax.all_to_all(
-        local_gram.reshape(devices_all, rank // devices_all, rank), everywhere, 0, 0, tiled=True
-    )
-    gram_rows, late_share = lax.optimization_barrier((jnp.sum(grams, axis=0), own_share))
+    own_share, local_gram = share_and_gram(parts)
+    packed = local_gram.shape[1]
+    gram_rows = (devices_all, BLK // devices_all, packed)
+    grams = lax.all_to_all(local_gram.reshape(gram_rows), everywhere, 0, 0, tiled=True)
+    gram, late_share = lax.optimization_barrier((jnp.sum(grams, axis=0), own_share))
     gram = lax.all_to_all(
-        jnp.broadcast_to(gram_rows[None], (devices_all,) + gram_rows.shape), everywhere, 0, 0, tiled=True
-    ).reshape(rank, rank)
+        jnp.broadcast_to(gram[None], gram_rows), everywhere, 0, 0, tiled=True
+    ).reshape(BLK, packed)
     shares = [late_share] + [
         lax.ppermute(late_share, "cols", [(i, (i + d) % col_devices) for i in range(col_devices)])
         for d in range(1, col_devices)
@@ -375,7 +417,7 @@
     start = col_devices - 1 - lax.axis_index("cols")
     sketch = lax.dynamic_slice_in_dim(back, start, col_devices, 0).reshape(panel, rank)
     other_sketch = lax.ppermute(sketch, "rows", swap)
-    inverse = inverse_factor(gram, 1.0 / total_rows)
+    inverse = inverse_factor(gram, rank, 1.0 / total_rows)
 
     ranks = rank // row_devices
     chips = row_devices // 2
@@ -397,9 +439,9 @@
             moves.append((i, (a * along + b) * 2 + i % 2))
         return functools.partial(lax.ppermute, axis_name="rows", perm=moves)
 
-    def scatter(part, factor, x_first):
+    def scatter(first, count, factor, x_first):
         ahead, behind, total = product(
-            factor, tile, other_tile, part, 2, cols // 4, 1.0 / math.sqrt(total_rows)
+            factor, tile, other_tile, first, count // 2, 2, 1.0 / math.sqrt(total_rows)
         )
         forward, backward = shift(x_first, 1), shift(x_first, -1)
         ahead, behind = forward(ahead), backward(behind)
@@ -412,7 +454,10 @@
             result += shift(not x_first, i)(terms[i].astype(jnp.bfloat16)).astype(jnp.float32)
         return result
 
-    coefficients = jnp.concatenate([scatter(0, left, True), scatter(1, turned, False)], axis=1)
+    cut = TBC * 7 // 13 * BLK
+    coefficients = jnp.concatenate(
+        [scatter(0, cut, left, True), scatter(cut, cols - cut, turned, False)], axis=1
+    )
     return basis, coefficients
 
 

time: 338 us -> 331 us (0.979)
  blocking collectives: 46.1 us -> 41 us
  starting transfers between devices: 47 us -> 42.7 us
    ppermute x2, waiting for transfers between devices: 0.01 us -> 6.97 us  [scatter(): backward(behind[:FAR * ranks])]
    ppermute x2, waiting for transfers between devices: 12.5 us -> 6.64 us  [scatter(): forward(ahead[:FAR * ranks])]
    all_to_all x1, blocking collectives: 26.8 us -> 22.5 us  [on_device(): lax.all_to_all(local_gram.reshape(gram_rows), everywhere, 0, 0, tiled=True)]
    ppermute x3, waiting for transfers between devices: 13.1 us -> 9.49 us  [on_device(): lax.ppermute(late_share, 'cols', [(i, (i + d) % col_devices) for i in ran...]
  transfers between devices with their start and end apart: 22 -> 22, of which waited for: 10 -> 12; matrix products, arithmetic and copies ran while one was open for 2% -> 2% of each run, Pallas kernels for 11% -> 12%
where the time goes in v6:
time: 331 us; the launch traced here: 330 us
  waiting for transfers between devices  174 us (53%)
  Pallas kernels  61.9 us (19%)
  starting transfers between devices  42.7 us (13%)
  blocking collectives  41 us (12%)
  other arithmetic  6.21 us (2%)
  local copies, waits for them, and re-layouts  3.34 us (1%)
    all_to_all x1, waiting for transfers between devices, on_device(): lax.all_to_all(send_blocks.reshape(devices_all, capacity, BLK, BLK), ever...  106 us
    ppermute x4, waiting for transfers between devices, scatter(): ahead, behind = (forward(ahead), backward(behind))  27.4 us
    all_to_all x1, blocking collectives, on_device(): lax.all_to_all(local_gram.reshape(gram_rows), everywhere, 0, 0, tiled=True)  22.5 us
    pallas_call x1, Pallas kernels, inverse_factor(): pl.pallas_call(functools.partial(factor_kernel, scale), in_specs=[pl.Bloc...  20.8 us
    all_to_all x1, blocking collectives, on_device(): lax.all_to_all(part.reshape(col_devices, share, rank), 'cols', 0, 0, tile...  18.4 us
    pallas_call x1, Pallas kernels, tile_and_sketch(): pl.pallas_call(tile_kernel, grid_spec=pltpu.PrefetchScalarGridSpec(num_sc...  17.1 us
    pallas_call x2, Pallas kernels, product(): pl.pallas_call(functools.partial(product_kernel, scale), grid=(steps,), i...  14.4 us
    all_to_all x1, starting transfers between devices, on_device(): lax.all_to_all(send_where.reshape(devices_all, capacity), everywhere, 0,...  11.1 us
  transfers between devices with their start and end apart: 22, of which 12 were waited for; matrix products, arithmetic and copies ran while one was open for 2% of the time, Pallas kernels for 12%

profile of v6, /device:TPU:0, one launch (start us, length us, event | category | flops | bytes accessed | tf_op | source)
XLA Modules:
  0.0 330.0 jit_solution(8111945183538387007)
XLA Ops:
  0.6 0.9 convert_reduce_fusion.1
  1.5 0.7 multiply_add_fusion
  2.2 0.1 select_reduce_fusion.1
  2.3 0.8 all_to_all.18
  3.1 11.1 %all-to-all-start = ((s32[128,1,2]{2,1,0:T(1,128)}), s32[128,1,2]{2,1,0:T(1,128)S(1)}, u32[]{:S(2)}, u32[]{:S(2)}) async-start(s32[128,1,2]{2,1,0:T(1,128)} %bitcast.18), calls=%async_computation | async-start | bytes 131072 | tf_op jit(solution)/shard_map/all_to_all | solution.py:381
  14.3 4.8 %bucket.1 = bf16[256,128,128]{2,1,0:T(8,128)(2,1)} custom-call(s32[128]{0:T(128)} %copy-done, bf16[128,128,128]{2,1,0:T(8,128)(2,1)} %blocks_ref.1), custom_call_target="tpu_custom_call" | custom-call | bytes 8388608 | tf_op jit(solution)/shard_map/bucket/pallas_call | solution.py:30
  19.1 4.2 %all-to-all-done = s32[128,1,2]{2,1,0:T(1,128)S(1)} async-done(((s32[128,1,2]{2,1,0:T(1,128)}), s32[128,1,2]{2,1,0:T(1,128)S(1)}, u32[]{:S(2)}, u32[]{:S(2)}) %all-to-all-start) | async-done | bytes 1056 | tf_op jit(solution)/shard_map/all_to_all | solution.py:381
  23.2 6.1 %all-to-all-start.1 = ((bf16[128,2,128,128]{3,2,1,0:T(8,128)(2,1)}), bf16[128,2,128,128]{3,2,1,0:T(8,128)(2,1)}, u32[]{:S(2)}, u32[]{:S(2)}) async-start(bf16[128,2,128,128]{3,2,1,0:T(8,128)(2,1)} %bitcast.47), calls=%async_computation.1 | async-start | bytes 16777216 | tf_op jit(solution)/shard_map/all_to_all | solution.py:378
  29.4 0.9 fusion.13
  30.3 0.1 select_n.161
  30.4 0.2 convert_reduce_fusion
  30.6 0.1 select_reduce_fusion
  30.8 0.1 slice_compare_fusion
  30.8 0.1 add_convert_fusion
  30.9 0.1 fusion.12
  31.0 0.7 pad_add_fusion.code_ref
  31.7 105.8 %all-to-all-done.1 = bf16[128,2,128,128]{3,2,1,0:T(8,128)(2,1)} async-done(((bf16[128,2,128,128]{3,2,1,0:T(8,128)(2,1)}), bf16[128,2,128,128]{3,2,1,0:T(8,128)(2,1)}, u32[]{:S(2)}, u32[]{:S(2)}) %all-to-all-start.1) | async-done | bytes 8388640 | tf_op jit(solution)/shard_map/all_to_all | solution.py:378
  137.4 17.1 %tile_and_sketch.1 = (bf16[512,13312]{1,0:T(8,128)(2,1)}, f32[512,512]{1,0:T(8,128)S(1)}) custom-call(s32[257]{0:T(512)S(1)} %pad_add_fusion.code_ref, bf16[256,128,128]{2,1,0:T(8,128)(2,1)} %bitcast.21.got_hbm, bf16[13312,512]{1,0:T(8,128)(2,1)} %omega_hbm.1), custom_call_target="tpu_custom_call" | custom-call | flops 6979321856 | bytes 35651584 | tf_op jit(solution)/shard_map/tile_and_sketch/pallas_call | solution.py:103
  154.6 0.1 collective-permute-start.4
  154.7 18.4 %all_to_all.29.parts_ref = f32[4,128,512]{2,1,0:T(8,128)S(1)} all-to-all(f32[4,128,512]{2,1,0:T(8,128)S(1)} %bitcast.44), channel_id=1, replica_groups=mesh['rows'=32,'cols'=4] {'cols'}, dimensions={0} | all-to-all | bytes 2097152 | tf_op jit(solution)/shard_map/all_to_all | solution.py:403
  173.1 0.8 share_and_gram.1
  173.9 0.7 copy.9
  174.6 22.5 %all_to_all.30 = f32[128,1,1280]{2,1,0:T(1,128)S(1)} all-to-all(f32[128,1,1280]{2,1,0:T(1,128)S(1)} %copy.9), channel_id=1, replica_groups=mesh['rows'=32,'cols'=4] {'rows','cols'}, dimensions={0} | all-to-all | bytes 1310720 | tf_op jit(solution)/shard_map/all_to_all | solution.py:407
  197.1 0.4 reduce_sum.61
  197.5 1.2 collective-permute-start
  198.7 1.7 collective-permute-start.1
  200.4 0.1 stack.90.at_ref
  200.5 0.1 collective-permute-start.2
  200.7 1.2 broadcast_in_dim.60
  201.8 6.7 %all-to-all-start.4 = ((f32[128,1,1280]{2,1,0:T(1,128)}), f32[128,1,1280]{2,1,0:T(1,128)S(1)}, u32[]{:S(2)}, u32[]{:S(2)}) async-start(f32[128,1,1280]{2,1,0:T(1,128)} %broadcast_in_dim.60), calls=%async_computation.4 | async-start | bytes 1310720 | tf_op jit(solution)/shard_map/all_to_all | solution.py:409
  208.6 0.9 collective-permute-done.1
  209.5 8.6 %collective-permute-done.2 = f32[128,512]{1,0:T(8,128)S(1)} collective-permute-done((f32[128,512]{1,0:T(8,128)S(1)}, f32[128,512]{1,0:T(8,128)S(1)}, u32[]{:S(2)}, u32[]{:S(2)}) %collective-permute-start.2) | collective-permute-done | bytes 262176 | tf_op jit(solution)/shard_map/ppermute | solution.py:413
  218.3 0.1 constant_dynamic-slice_fusion
  218.4 0.3 collective-permute-start.3
  218.6 4.7 %all-to-all-done.4 = f32[128,1,1280]{2,1,0:T(1,128)S(1)} async-done(((f32[128,1,1280]{2,1,0:T(1,128)}), f32[128,1,1280]{2,1,0:T(1,128)S(1)}, u32[]{:S(2)}, u32[]{:S(2)}) %all-to-all-start.4) | async-done | bytes 655392 | tf_op jit(solution)/shard_map/all_to_all | solution.py:409
  223.4 20.8 %inverse_factor.1.inverse_ref = f32[512,512]{1,0:T(8,128)S(1)} custom-call(f32[128,1280]{1,0:T(8,128)S(1)} %bitcast.46), custom_call_target="tpu_custom_call" | custom-call | flops 34359738368 | bytes 2097152 | tf_op jit(solution)/shard_map/inverse_factor/pallas_call | solution.py:243
  244.2 4.0 %basis_parts.1 = (bf16[256,1024]{1,0:T(8,128)(2,1)S(1)}, bf16[256,1024]{1,0:T(8,128)(2,1)S(1)}, bf16[512,128]{1,0:T(8,128)(2,1)}) custom-call(s32[17]{0:T(128)S(1)} %stack.90.at_ref, f32[512,512]{1,0:T(8,128)S(1)} %inverse_factor.1.inverse_ref, f32[512,512]{1,0:T(8,128)S(1)} %bitcast.43, f32[512,512]{1,0:T(8,128)S(1)} %collective-permute-done.3.other_ref), custom_call_target="tpu_custom_call" | custom-call | flops 2013265920 | bytes 1572864 | tf_op jit(solution)/shard_map/basis_parts/pallas_call | solution.py:294
  248.2 6.8 %product.3 = (bf16[96,6144]{1,0:T(8,128)(2,1)S(1)}, bf16[96,6144]{1,0:T(8,128)(2,1)S(1)}, f32[64,6144]{1,0:T(8,128)S(1)}) custom-call(bf16[256,1024]{1,0:T(8,128)(2,1)S(1)} %get-tuple-element.28.left_ref, bf16[512,13312]{1,0:T(8,128)(2,1)} %get-tuple-element.24.own_ref, bf16[512,13312]{1,0:T(8,128)(2,1)} %collective-permute-done.4.other_ref), custom_call_target="tpu_custom_call" | custom-call | flops 3221225472 | bytes 15728640 | tf_op jit(solution)/shard_map/product/pallas_call | solution.py:337
  255.0 0.9 collective-permute-start.13
  255.8 1.2 collective-permute-start.12
  257.1 7.6 %product.2 = (bf16[96,7168]{1,0:T(8,128)(2,1)S(1)}, bf16[96,7168]{1,0:T(8,128)(2,1)S(1)}, f32[64,7168]{1,0:T(8,128)S(1)}) custom-call(bf16[256,1024]{1,0:T(8,128)(2,1)S(1)} %get-tuple-element.23.left_ref, bf16[512,13312]{1,0:T(8,128)(2,1)} %get-tuple-element.24.own_ref, bf16[512,13312]{1,0:T(8,128)(2,1)} %collective-permute-done.4.other_ref), custom_call_target="tpu_custom_call" | custom-call | flops 3758096384 | bytes 18350080 | tf_op jit(solution)/shard_map/product/pallas_call | solution.py:337
  264.7 1.2 collective-permute-start.6
  265.9 0.9 collective-permute-start.5
  266.8 16.2 %collective-permute-done.13 = bf16[96,6144]{1,0:T(8,128)(2,1)S(1)} collective-permute-done((bf16[96,6144]{1,0:T(8,128)(2,1)S(1)}, bf16[96,6144]{1,0:T(8,128)(2,1)S(1)}, u32[]{:S(2)}, u32[]{:S(2)}) %collective-permute-start.13) | collective-permute-done | bytes 1179680 | tf_op jit(solution)/shard_map/ppermute | solution.py:447
  283.0 1.9 collective-permute-start.15
  284.9 0.3 collective-permute-start.14
  285.2 11.2 %collective-permute-done.6 = bf16[96,7168]{1,0:T(8,128)(2,1)S(1)} collective-permute-done((bf16[96,7168]{1,0:T(8,128)(2,1)S(1)}, bf16[96,7168]{1,0:T(8,128)(2,1)S(1)}, u32[]{:S(2)}, u32[]{:S(2)}) %collective-permute-start.6) | collective-permute-done | bytes 1376288 | tf_op jit(solution)/shard_map/ppermute | solution.py:447
  296.4 2.4 collective-permute-start.8
  298.9 0.1 collective-permute-start.7
  299.0 0.4 fusion.15
  299.4 3.3 collective-permute-start.18
  302.7 0.9 collective-permute-start.16
  303.6 7.0 %collective-permute-done.8 = bf16[32,7168]{1,0:T(8,128)(2,1)S(1)} collective-permute-done((bf16[32,7168]{1,0:T(8,128)(2,1)S(1)}, bf16[32,7168]{1,0:T(8,128)(2,1)S(1)}, u32[]{:S(2)}, u32[]{:S(2)}) %collective-permute-start.8) | collective-permute-done | bytes 458784 | tf_op jit(solution)/shard_map/ppermute | solution.py:448
  310.6 6.6 %collective-permute-done.7 = bf16[32,7168]{1,0:T(8,128)(2,1)S(1)} collective-permute-done((bf16[32,7168]{1,0:T(8,128)(2,1)S(1)}, bf16[32,7168]{1,0:T(8,128)(2,1)S(1)}, u32[]{:S(2)}, u32[]{:S(2)}) %collective-permute-start.7) | collective-permute-done | bytes 458784 | tf_op jit(solution)/shard_map/ppermute | solution.py:448
  317.2 0.4 fusion.14
  317.7 1.3 collective-permute-start.11
  319.0 0.8 collective-permute-start.10
  319.8 0.1 collective-permute-start.9
  320.0 0.1 fusion.3
  320.1 3.8 %collective-permute-done.11 = bf16[16,7168]{1,0:T(8,128)(2,1)S(1)} collective-permute-done((bf16[16,7168]{1,0:T(8,128)(2,1)S(1)}, bf16[16,7168]{1,0:T(8,128)(2,1)S(1)}, u32[]{:S(2)}, u32[]{:S(2)}) %collective-permute-start.11) | collective-permute-done | bytes 229408 | tf_op jit(solution)/shard_map/ppermute | solution.py:454
  323.8 2.8 collective-permute-done.10
  326.6 2.4 collective-permute-done.9
  329.0 0.1 fusion.1
  329.1 1.0 pad_maximum_fusion
  (32 shorter events, 0.5 us)
Async XLA Ops:
  2.2 12.0 %copy-start = (s32[128]{0:T(128)}, s32[128]{0:T(128)S(1)}, u32[]{:S(2)}) copy-start(s32[128]{0:T(128)S(1)} %get-tuple-element.44.place_ref) | copy-start | bytes 1540
  3.1 20.1 %all-to-all-start = ((s32[128,1,2]{2,1,0:T(1,128)}), s32[128,1,2]{2,1,0:T(1,128)S(1)}, u32[]{:S(2)}, u32[]{:S(2)}) async-start(s32[128,1,2]{2,1,0:T(1,128)} %bitcast.18), calls=%async_computation | async-start | bytes 131072 | tf_op jit(solution)/shard_map/all_to_all | solution.py:381
  23.2 114.2 %all-to-all-start.1 = ((bf16[128,2,128,128]{3,2,1,0:T(8,128)(2,1)}), bf16[128,2,128,128]{3,2,1,0:T(8,128)(2,1)}, u32[]{:S(2)}, u32[]{:S(2)}) async-start(bf16[128,2,128,128]{3,2,1,0:T(8,128)(2,1)} %bitcast.47), calls=%async_computation.1 | async-start | bytes 16777216 | tf_op jit(solution)/shard_map/all_to_all | solution.py:378
  154.6 93.6 %collective-permute-start.4 = (bf16[512,13312]{1,0:T(8,128)(2,1)}, bf16[512,13312]{1,0:T(8,128)(2,1)}, u32[]{:S(2)}, u32[]{:S(2)}) collective-permute-start(bf16[512,13312]{1,0:T(8,128)(2,1)} %get-tuple-element.24.own_ref), channel_id=1, source_target_pairs={{0,4},{4,0},{8,12},{12,8},{16,20},{20,16},{24,28},{28,24},{32,36},... | collective-permute-start | bytes 40894472 | tf_op jit(solution)/shard_map/ppermute | solution.py:400
  197.5 11.1 %collective-permute-start = (f32[128,512]{1,0:T(8,128)S(1)}, f32[128,512]{1,0:T(8,128)S(1)}, u32[]{:S(2)}, u32[]{:S(2)}) collective-permute-start(f32[128,512]{1,0:T(8,128)S(1)} %get-tuple-element.21), channel_id=1, source_target_pairs={{0,3},{1,0},{2,1},{3,2},{4,7},{5,4},{6,5},{7,6},{8,11},{9,8},{10,9... | collective-permute-start | bytes 786440 | tf_op jit(solution)/shard_map/ppermute | solution.py:413
  198.7 10.8 %collective-permute-start.1 = (f32[128,512]{1,0:T(8,128)S(1)}, f32[128,512]{1,0:T(8,128)S(1)}, u32[]{:S(2)}, u32[]{:S(2)}) collective-permute-start(f32[128,512]{1,0:T(8,128)S(1)} %get-tuple-element.21), channel_id=1, source_target_pairs={{0,2},{1,3},{2,0},{3,1},{4,6},{5,7},{6,4},{7,5},{8,10},{9,11},{10,... | collective-permute-start | bytes 786440 | tf_op jit(solution)/shard_map/ppermute | solution.py:413
  200.5 17.6 %collective-permute-start.2 = (f32[128,512]{1,0:T(8,128)S(1)}, f32[128,512]{1,0:T(8,128)S(1)}, u32[]{:S(2)}, u32[]{:S(2)}) collective-permute-start(f32[128,512]{1,0:T(8,128)S(1)} %get-tuple-element.21), channel_id=1, source_target_pairs={{0,1},{1,2},{2,3},{3,0},{4,5},{5,6},{6,7},{7,4},{8,9},{9,10},{10,1... | collective-permute-start | bytes 786440 | tf_op jit(solution)/shard_map/ppermute | solution.py:413
  201.8 21.5 %all-to-all-start.4 = ((f32[128,1,1280]{2,1,0:T(1,128)}), f32[128,1,1280]{2,1,0:T(1,128)S(1)}, u32[]{:S(2)}, u32[]{:S(2)}) async-start(f32[128,1,1280]{2,1,0:T(1,128)} %broadcast_in_dim.60), calls=%async_computation.4 | async-start | bytes 1310720 | tf_op jit(solution)/shard_map/all_to_all | solution.py:409
  218.4 25.9 %collective-permute-start.3 = (f32[512,512]{1,0:T(8,128)S(1)}, f32[512,512]{1,0:T(8,128)S(1)}, u32[]{:S(2)}, u32[]{:S(2)}) collective-permute-start(f32[512,512]{1,0:T(8,128)S(1)} %bitcast.42), channel_id=1, source_target_pairs={{0,4},{4,0},{8,12},{12,8},{16,20},{20,16},{24,28},{28,24},{32,36},... | collective-permute-start | bytes 3145736 | tf_op jit(solution)/shard_map/ppermute | solution.py:419
  255.0 28.0 %collective-permute-start.13 = (bf16[96,6144]{1,0:T(8,128)(2,1)S(1)}, bf16[96,6144]{1,0:T(8,128)(2,1)S(1)}, u32[]{:S(2)}, u32[]{:S(2)}) collective-permute-start(bf16[96,6144]{1,0:T(8,128)(2,1)S(1)} %get-tuple-element.31), channel_id=1, source_target_pairs={{0,24},{4,28},{8,0},{12,4},{16,8},{20,12},{24,16},{28,20},{32,56},... | collective-permute-start | bytes 3538952 | tf_op jit(solution)/shard_map/ppermute | solution.py:447
  255.8 29.0 %collective-permute-start.12 = (bf16[96,6144]{1,0:T(8,128)(2,1)S(1)}, bf16[96,6144]{1,0:T(8,128)(2,1)S(1)}, u32[]{:S(2)}, u32[]{:S(2)}) collective-permute-start(bf16[96,6144]{1,0:T(8,128)(2,1)S(1)} %get-tuple-element.30), channel_id=1, source_target_pairs={{0,8},{4,12},{8,16},{12,20},{16,24},{20,28},{24,0},{28,4},{32,40},... | collective-permute-start | bytes 3538952 | tf_op jit(solution)/shard_map/ppermute | solution.py:447
  264.7 31.7 %collective-permute-start.6 = (bf16[96,7168]{1,0:T(8,128)(2,1)S(1)}, bf16[96,7168]{1,0:T(8,128)(2,1)S(1)}, u32[]{:S(2)}, u32[]{:S(2)}) collective-permute-start(bf16[96,7168]{1,0:T(8,128)(2,1)S(1)} %get-tuple-element.27), channel_id=1, source_target_pairs={{0,96},{4,100},{8,104},{12,108},{16,112},{20,116},{24,120},{28,124... | collective-permute-start | bytes 4128776 | tf_op jit(solution)/shard_map/ppermute | solution.py:447
  265.9 32.9 %collective-permute-start.5 = (bf16[96,7168]{1,0:T(8,128)(2,1)S(1)}, bf16[96,7168]{1,0:T(8,128)(2,1)S(1)}, u32[]{:S(2)}, u32[]{:S(2)}) collective-permute-start(bf16[96,7168]{1,0:T(8,128)(2,1)S(1)} %get-tuple-element.26), channel_id=1, source_target_pairs={{0,32},{4,36},{8,40},{12,44},{16,48},{20,52},{24,56},{28,60},{32,6... | collective-permute-start | bytes 4128776 | tf_op jit(solution)/shard_map/ppermute | solution.py:447
  283.0 16.0 %collective-permute-start.15 = (bf16[32,6144]{1,0:T(8,128)(2,1)S(1)}, bf16[32,6144]{1,0:T(8,128)(2,1)S(1)}, u32[]{:S(2)}, u32[]{:S(2)}) collective-permute-start(bf16[32,6144]{1,0:T(8,128)(2,1)S(1)} %slice.93), channel_id=1, source_target_pairs={{0,24},{4,28},{8,0},{12,4},{16,8},{20,12},{24,16},{28,20},{32,56},... | collective-permute-start | bytes 1179656 | tf_op jit(solution)/shard_map/ppermute | solution.py:448
  284.9 14.1 %collective-permute-start.14 = (bf16[32,6144]{1,0:T(8,128)(2,1)S(1)}, bf16[32,6144]{1,0:T(8,128)(2,1)S(1)}, u32[]{:S(2)}, u32[]{:S(2)}) collective-permute-start(bf16[32,6144]{1,0:T(8,128)(2,1)S(1)} %slice.92), channel_id=1, source_target_pairs={{0,8},{4,12},{8,16},{12,20},{16,24},{20,28},{24,0},{28,4},{32,40},... | collective-permute-start | bytes 1179656 | tf_op jit(solution)/shard_map/ppermute | solution.py:448
  296.4 14.2 %collective-permute-start.8 = (bf16[32,7168]{1,0:T(8,128)(2,1)S(1)}, bf16[32,7168]{1,0:T(8,128)(2,1)S(1)}, u32[]{:S(2)}, u32[]{:S(2)}) collective-permute-start(bf16[32,7168]{1,0:T(8,128)(2,1)S(1)} %slice.85), channel_id=1, source_target_pairs={{0,96},{4,100},{8,104},{12,108},{16,112},{20,116},{24,120},{28,124... | collective-permute-start | bytes 1376264 | tf_op jit(solution)/shard_map/ppermute | solution.py:448
  298.9 18.4 %collective-permute-start.7 = (bf16[32,7168]{1,0:T(8,128)(2,1)S(1)}, bf16[32,7168]{1,0:T(8,128)(2,1)S(1)}, u32[]{:S(2)}, u32[]{:S(2)}) collective-permute-start(bf16[32,7168]{1,0:T(8,128)(2,1)S(1)} %slice.84), channel_id=1, source_target_pairs={{0,32},{4,36},{8,40},{12,44},{16,48},{20,52},{24,56},{28,60},{32,6... | collective-permute-start | bytes 1376264 | tf_op jit(solution)/shard_map/ppermute | solution.py:448
  299.4 20.4 %collective-permute-start.18 = (bf16[16,6144]{1,0:T(8,128)(2,1)S(1)}, bf16[16,6144]{1,0:T(8,128)(2,1)S(1)}, u32[]{:S(2)}, u32[]{:S(2)}) collective-permute-start(bf16[16,6144]{1,0:T(8,128)(2,1)S(1)} %get-tuple-element.42), channel_id=1, source_target_pairs={{0,96},{4,100},{8,104},{12,108},{16,112},{20,116},{24,120},{28,124... | collective-permute-start | bytes 589832 | tf_op jit(solution)/shard_map/ppermute | solution.py:454
  302.7 17.3 %collective-permute-start.17 = (bf16[16,6144]{1,0:T(8,128)(2,1)S(1)}, bf16[16,6144]{1,0:T(8,128)(2,1)S(1)}, u32[]{:S(2)}, u32[]{:S(2)}) collective-permute-start(bf16[16,6144]{1,0:T(8,128)(2,1)S(1)} %get-tuple-element.43), channel_id=1, source_target_pairs={{0,64},{4,68},{8,72},{12,76},{16,80},{20,84},{24,88},{28,92},{32,9... | collective-permute-start | bytes 589832 | tf_op jit(solution)/shard_map/ppermute | solution.py:454
  302.7 17.3 %collective-permute-start.16 = (bf16[16,6144]{1,0:T(8,128)(2,1)S(1)}, bf16[16,6144]{1,0:T(8,128)(2,1)S(1)}, u32[]{:S(2)}, u32[]{:S(2)}) collective-permute-start(bf16[16,6144]{1,0:T(8,128)(2,1)S(1)} %get-tuple-element.41), channel_id=1, source_target_pairs={{0,32},{4,36},{8,40},{12,44},{16,48},{20,52},{24,56},{28,60},{32,6... | collective-permute-start | bytes 589832 | tf_op jit(solution)/shard_map/ppermute | solution.py:454
  317.7 6.1 %collective-permute-start.11 = (bf16[16,7168]{1,0:T(8,128)(2,1)S(1)}, bf16[16,7168]{1,0:T(8,128)(2,1)S(1)}, u32[]{:S(2)}, u32[]{:S(2)}) collective-permute-start(bf16[16,7168]{1,0:T(8,128)(2,1)S(1)} %get-tuple-element.39), channel_id=1, source_target_pairs={{0,24},{4,28},{8,0},{12,4},{16,8},{20,12},{24,16},{28,20},{32,56},... | collective-permute-start | bytes 688136 | tf_op jit(solution)/shard_map/ppermute | solution.py:454
  319.0 7.6 %collective-permute-start.10 = (bf16[16,7168]{1,0:T(8,128)(2,1)S(1)}, bf16[16,7168]{1,0:T(8,128)(2,1)S(1)}, u32[]{:S(2)}, u32[]{:S(2)}) collective-permute-start(bf16[16,7168]{1,0:T(8,128)(2,1)S(1)} %get-tuple-element.40), channel_id=1, source_target_pairs={{0,16},{4,20},{8,24},{12,28},{16,0},{20,4},{24,8},{28,12},{32,48},... | collective-permute-start | bytes 688136 | tf_op jit(solution)/shard_map/ppermute | solution.py:454
  319.8 9.2 %collective-permute-start.9 = (bf16[16,7168]{1,0:T(8,128)(2,1)S(1)}, bf16[16,7168]{1,0:T(8,128)(2,1)S(1)}, u32[]{:S(2)}, u32[]{:S(2)}) collective-permute-start(bf16[16,7168]{1,0:T(8,128)(2,1)S(1)} %get-tuple-element.38), channel_id=1, source_target_pairs={{0,8},{4,12},{8,16},{12,20},{16,24},{20,28},{24,0},{28,4},{32,40},... | collective-permute-start | bytes 688136 | tf_op jit(solution)/shard_map/ppermute | solution.py:454

commit v7 on v6

--- a/solution.py
+++ b/solution.py
@@ -139,46 +139,58 @@
         start += n - at
 
 
-def gram_kernel(parts_ref, share_ref, packed_ref):
+def gram_kernel(core_ref, parts_ref, share_ref, keep_ref, send_ref, packed):
     share = parts_ref[0]
     for i in range(1, parts_ref.shape[0]):
         share += parts_ref[i]
     share_ref[...] = share
     for at, start, width in upper_rows(share.shape[1]):
-        packed_ref[:, start : start + width] = lax.dot_general(
+        packed[:, start : start + width] = lax.dot_general(
             share[:, at : at + BLK],
             share[:, at:],
             (((0,), (0,)), ((), ())),
             precision=HIGHEST,
             preferred_element_type=jnp.float32,
         )
-
-
-def share_and_gram(parts):
+    half = keep_ref.shape[0]
+    keep_ref[...] = packed[pl.ds(pl.multiple_of(core_ref[0] * half, half), half), :]
+    send_ref[...] = packed[pl.ds(pl.multiple_of((1 - core_ref[0]) * half, half), half), :]
+
+
+def share_and_gram(core, parts):
     _, share, rank = parts.shape
     packed = sum(width for _, _, width in upper_rows(rank))
     whole = pl.BlockSpec(memory_space=pltpu.VMEM)
     return pl.pallas_call(
         gram_kernel,
-        in_specs=[whole],
-        out_specs=[whole] * 2,
+        grid_spec=pltpu.PrefetchScalarGridSpec(
+            num_scalar_prefetch=1,
+            grid=(),
+            in_specs=[whole],
+            out_specs=[whole] * 3,
+            scratch_shapes=[pltpu.VMEM((BLK, packed), jnp.float32)],
+        ),
         out_shape=[
             jax.ShapeDtypeStruct((share, rank), jnp.float32),
-            jax.ShapeDtypeStruct((BLK, packed), jnp.float32),
+            jax.ShapeDtypeStruct((BLK // 2, packed), jnp.float32),
+            jax.ShapeDtypeStruct((BLK // 2, packed), jnp.float32),
         ],
         compiler_params=pltpu.CompilerParams(vmem_limit_bytes=24 * MIB),
         cost_estimate=pl.CostEstimate(
             flops=12 * share * rank * rank, bytes_accessed=8 * parts.size, transcendentals=0
         ),
         name="share_and_gram",
-    )(parts)
-
-
-def factor_kernel(scale, gram_ref, out_ref, work):
+    )(core, parts)
+
+
+def factor_kernel(scale, core_ref, mine_ref, other_ref, out_ref, work):
     n = work.shape[0]
     work[...] = jnp.zeros_like(work)
     for at, start, width in upper_rows(n):
-        work[at : at + BLK, at:] = gram_ref[:, start : start + width] * scale
+        for core, rows_ref in ((core_ref[0], mine_ref), (1 - core_ref[0], other_ref)):
+            half = rows_ref.shape[0]
+            rows = pl.ds(pl.multiple_of(at + core * half, half), half)
+            work[rows, at:] = rows_ref[:, start : start + width] * scale
     row = lax.broadcasted_iota(jnp.int32, (n, n), 0)
     lane = lax.broadcasted_iota(jnp.int32, (n, n), 1)
     out_ref[...] = jnp.where(row == lane, 1.0, 0.0)
@@ -239,19 +251,24 @@
     lax.fori_loop(0, n // BLK, block, 0)
 
 
-def inverse_factor(gram, n, scale):
+def inverse_factor(core, mine, other, n, scale):
+    whole = pl.BlockSpec(memory_space=pltpu.VMEM)
     return pl.pallas_call(
         functools.partial(factor_kernel, scale),
-        in_specs=[pl.BlockSpec(memory_space=pltpu.VMEM)],
-        out_specs=pl.BlockSpec(memory_space=pltpu.VMEM),
+        grid_spec=pltpu.PrefetchScalarGridSpec(
+            num_scalar_prefetch=1,
+            grid=(),
+            in_specs=[whole] * 2,
+            out_specs=whole,
+            scratch_shapes=[pltpu.VMEM((n, n), jnp.float32)],
+        ),
         out_shape=jax.ShapeDtypeStruct((n, n), jnp.float32),
-        scratch_shapes=[pltpu.VMEM((n, n), jnp.float32)],
         compiler_params=pltpu.CompilerParams(vmem_limit_bytes=24 * MIB),
         cost_estimate=pl.CostEstimate(
             flops=1 << 35, bytes_accessed=2 * n * n * 4, transcendentals=0
         ),
         name="inverse_factor",
-    )(gram)
+    )(core, mine, other)
 
 
 FAR = 2
@@ -356,16 +373,17 @@
 def on_device(blocks, owner, block_pos, omega):
     slot_count = blocks.shape[0]
     rank = omega.shape[1]
-    row_devices = lax.axis_size("rows")
+    chips = lax.axis_size("chips")
+    row_devices = 2 * chips
     col_devices = lax.axis_size("cols")
     devices_all = row_devices * col_devices
-    everywhere = ("rows", "cols")
+    everywhere = ("chips", "core", "cols")
     capacity = max(2, 2 * slot_count // devices_all)
     slots = devices_all * capacity
     panel, cols = PBR * BLK, TBC * BLK
     total_rows = panel * row_devices
-    core = lax.axis_index("rows") % 2
-    swap = [(i, i ^ 1) for i in range(row_devices)]
+    core = lax.axis_index("core")
+    swap = functools.partial(lax.ppermute, axis_name="core", perm=[(0, 1), (1, 0)])
 
     target = owner[:, 0]
     numbers = jnp.arange(slot_count, dtype=jnp.int32)
@@ -397,18 +415,20 @@
     code = jnp.concatenate([code, filled[None]])
 
     tile, part = tile_and_sketch(code, got_blocks, omega, panel, cols)
-    other_tile = lax.ppermute(tile, "rows", swap)
+    other_tile = swap(tile)
 
     share = panel // col_devices
     parts = lax.all_to_all(part.reshape(col_devices, share, rank), "cols", 0, 0, tiled=True)
-    own_share, local_gram = share_and_gram(parts)
-    packed = local_gram.shape[1]
-    gram_rows = (devices_all, BLK // devices_all, packed)
-    grams = lax.all_to_all(local_gram.reshape(gram_rows), everywhere, 0, 0, tiled=True)
-    gram, late_share = lax.optimization_barrier((jnp.sum(grams, axis=0), own_share))
-    gram = lax.all_to_all(
-        jnp.broadcast_to(gram[None], gram_rows), everywhere, 0, 0, tiled=True
-    ).reshape(BLK, packed)
+    which = core.astype(jnp.int32)[None]
+    own_share, keep, send = share_and_gram(which, parts)
+    same_core = ("chips", "cols")
+    gram_rows = (chips * col_devices, BLK // devices_all, keep.shape[1])
+    grams = lax.all_to_all((keep + swap(send)).reshape(gram_rows), same_core, 0, 0, tiled=True)
+    gram, late_share = lax.optimization_barrier(
+        (jnp.broadcast_to(jnp.sum(grams, axis=0)[None], gram_rows), own_share)
+    )
+    gram = lax.all_to_all(gram, same_core, 0, 0, tiled=True).reshape(keep.shape)
+    other_gram = swap(gram)
     shares = [late_share] + [
         lax.ppermute(late_share, "cols", [(i, (i + d) % col_devices) for i in range(col_devices)])
         for d in range(1, col_devices)
@@ -416,13 +436,12 @@
     back = jnp.stack(shares[::-1] * 2)
     start = col_devices - 1 - lax.axis_index("cols")
     sketch = lax.dynamic_slice_in_dim(back, start, col_devices, 0).reshape(panel, rank)
-    other_sketch = lax.ppermute(sketch, "rows", swap)
-    inverse = inverse_factor(gram, rank, 1.0 / total_rows)
+    other_sketch = swap(sketch)
+    inverse = inverse_factor(which, gram, other_gram, rank, 1.0 / total_rows)
 
     ranks = rank // row_devices
-    chips = row_devices // 2
     along = math.isqrt(chips)
-    chip = lax.axis_index("rows") // 2
+    chip = lax.axis_index("chips")
     x, y = chip // along, chip % along
     at = [(((x + a) % along * along + (y + b) % along) * 2 + core) * ranks for a, b in PIECES]
     width = rank // col_devices
@@ -433,16 +452,16 @@
 
     def shift(over_x, steps):
         moves = []
-        for i in range(row_devices):
-            a, b = i // 2 // along, i // 2 % along
+        for i in range(chips):
+            a, b = divmod(i, along)
             a, b = ((a + steps) % along, b) if over_x else (a, (b + steps) % along)
-            moves.append((i, (a * along + b) * 2 + i % 2))
-        return functools.partial(lax.ppermute, axis_name="rows", perm=moves)
-
-    def scatter(first, count, factor, x_first):
-        ahead, behind, total = product(
-            factor, tile, other_tile, first, count // 2, 2, 1.0 / math.sqrt(total_rows)
-        )
+            moves.append((i, a * along + b))
+        return functools.partial(lax.ppermute, axis_name="chips", perm=moves)
+
+    def multiply(first, count, factor):
+        return product(factor, tile, other_tile, first, count // 2, 2, 1.0 / math.sqrt(total_rows))
+
+    def scatter(ahead, behind, total, x_first):
         forward, backward = shift(x_first, 1), shift(x_first, -1)
         ahead, behind = forward(ahead), backward(behind)
         far, back_far = forward(ahead[: FAR * ranks]), backward(behind[: FAR * ranks])
@@ -454,21 +473,19 @@
             result += shift(not x_first, i)(terms[i].astype(jnp.bfloat16)).astype(jnp.float32)
         return result
 
-    cut = TBC * 7 // 13 * BLK
-    coefficients = jnp.concatenate(
-        [scatter(0, cut, left, True), scatter(cut, cols - cut, turned, False)], axis=1
-    )
+    cut = TBC // 2 * BLK
+    one = multiply(0, cut, left)
+    two = multiply(cut, cols - cut, turned)
+    coefficients = jnp.concatenate([scatter(*one, True), scatter(*two, False)], axis=1)
     return basis, coefficients
 
 
 def solution(mesh):
-    in_specs = (
-        P(("rows", "cols"), None, None),
-        P(("rows", "cols"), None),
-        P(("rows", "cols")),
-        P("cols", None),
-    )
-    out_specs = (P("rows", "cols"), P("rows", "cols"))
+    rows, cols = mesh.devices.shape
+    mesh = jax.sharding.Mesh(mesh.devices.reshape(rows // 2, 2, cols), ("chips", "core", "cols"))
+    everywhere = ("chips", "core", "cols")
+    in_specs = (P(everywhere, None, None), P(everywhere, None), P(everywhere), P("cols", None))
+    out_specs = (P(("chips", "core"), "cols"), P(("chips", "core"), "cols"))
     return jax.shard_map(
         on_device, mesh=mesh, in_specs=in_specs, out_specs=out_specs, check_vma=False
     )

time: 331 us -> 325 us (0.982)
  blocking collectives: 41 us -> 21.2 us
  starting transfers between devices: 42.7 us -> 51.3 us
  waiting for transfers between devices: 174 us -> 180 us
    all_to_all x2 -> x1, blocking collectives: 41 us -> 21.2 us  [on_device(): lax.all_to_all((keep + swap(send)).reshape(gram_rows), same_core, 0, 0, t...]
    all_to_all x1 -> x2, waiting for transfers between devices: 4.68 us -> 19.9 us  [the longest x1 16 us: on_device(): lax.all_to_all(part.reshape(col_devices, share, rank), 'cols', 0, 0, tile...]
    ppermute x2, waiting for transfers between devices: 6.97 us -> 1.65 us  [scatter(): backward(behind[:FAR * ranks])]
    all_to_all x1 -> x2, starting transfers between devices: 6.73 us -> 10.7 us  [the longest x1 7.14 us: on_device(): gram = lax.all_to_all(gram, same_core, 0, 0, tiled=True).reshape(keep.shape)]
    ppermute x6, waiting for transfers between devices: 8.93 us -> 5.47 us  [scatter(): shift(not x_first, i)(terms[i].astype(jnp.bfloat16)).astype(jnp.float32)]
  transfers between devices with their start and end apart: 22 -> 25, of which waited for: 12 -> 16; matrix products, arithmetic and copies ran while one was open for 2% -> 2% of each run, Pallas kernels for 12% -> 12%
where the time goes in v7:
time: 325 us
  waiting for transfers between devices  180 us (55%)
  Pallas kernels  63 us (19%)
  starting transfers between devices  51.3 us (16%)
  blocking collectives  21.2 us (7%)
  other arithmetic  5.98 us (2%)
    all_to_all x1, waiting for transfers between devices, on_device(): lax.all_to_all(send_blocks.reshape(devices_all, capacity, BLK, BLK), ever...  106 us
    ppermute x4, waiting for transfers between devices, scatter(): ahead, behind = (forward(ahead), backward(behind))  25.1 us
    all_to_all x1, blocking collectives, on_device(): lax.all_to_all((keep + swap(send)).reshape(gram_rows), same_core, 0, 0, t...  21.2 us
    pallas_call x1, Pallas kernels, inverse_factor(): pl.pallas_call(functools.partial(factor_kernel, scale), grid_spec=pltpu.P...  20.9 us
    pallas_call x1, Pallas kernels, tile_and_sketch(): pl.pallas_call(tile_kernel, grid_spec=pltpu.PrefetchScalarGridSpec(num_sc...  18.1 us
    all_to_all x1, waiting for transfers between devices, on_device(): lax.all_to_all(part.reshape(col_devices, share, rank), 'cols', 0, 0, tile...  16 us
    pallas_call x2, Pallas kernels, product(): pl.pallas_call(functools.partial(product_kernel, scale), grid=(steps,), i...  14.4 us
    all_to_all x1, starting transfers between devices, on_device(): lax.all_to_all(send_where.reshape(devices_all, capacity), everywhere, 0,...  11.1 us
  transfers between devices with their start and end apart: 25, of which 16 were waited for; matrix products, arithmetic and copies ran while one was open for 2% of the time, Pallas kernels for 12%

profile of v7, /device:TPU:0, one launch (start us, length us, event | category | flops | bytes accessed | tf_op | source)
XLA Modules:
  0.0 324.9 jit_solution(10286495531300006595)
XLA Ops:
  0.6 0.9 convert_reduce_fusion.1
  1.5 0.7 multiply_add_fusion
  2.2 0.1 select_reduce_fusion.1
  2.3 0.8 all_to_all.18
  3.1 11.1 %all-to-all-start = ((s32[128,1,2]{2,1,0:T(1,128)}), s32[128,1,2]{2,1,0:T(1,128)S(1)}, u32[]{:S(2)}, u32[]{:S(2)}) async-start(s32[128,1,2]{2,1,0:T(1,128)} %bitcast.19), calls=%async_computation | async-start | bytes 131072 | tf_op jit(solution)/shard_map/all_to_all | solution.py:399
  14.3 4.9 %bucket.1 = bf16[256,128,128]{2,1,0:T(8,128)(2,1)} custom-call(s32[128]{0:T(128)} %copy-done, bf16[128,128,128]{2,1,0:T(8,128)(2,1)} %blocks_ref.1), custom_call_target="tpu_custom_call" | custom-call | bytes 8388608 | tf_op jit(solution)/shard_map/bucket/pallas_call | solution.py:30
  19.2 4.0 %all-to-all-done = s32[128,1,2]{2,1,0:T(1,128)S(1)} async-done(((s32[128,1,2]{2,1,0:T(1,128)}), s32[128,1,2]{2,1,0:T(1,128)S(1)}, u32[]{:S(2)}, u32[]{:S(2)}) %all-to-all-start) | async-done | bytes 1056 | tf_op jit(solution)/shard_map/all_to_all | solution.py:399
  23.2 6.2 %all-to-all-start.1 = ((bf16[128,2,128,128]{3,2,1,0:T(8,128)(2,1)}), bf16[128,2,128,128]{3,2,1,0:T(8,128)(2,1)}, u32[]{:S(2)}, u32[]{:S(2)}) async-start(bf16[128,2,128,128]{3,2,1,0:T(8,128)(2,1)} %bitcast.48), calls=%async_computation.1 | async-start | bytes 16777216 | tf_op jit(solution)/shard_map/all_to_all | solution.py:396
  29.5 0.9 fusion.13
  30.4 0.1 select_n.152
  30.6 0.2 convert_reduce_fusion
  30.8 0.1 select_reduce_fusion
  31.1 0.7 pad_add_fusion.code_ref
  31.8 105.8 %all-to-all-done.1 = bf16[128,2,128,128]{3,2,1,0:T(8,128)(2,1)} async-done(((bf16[128,2,128,128]{3,2,1,0:T(8,128)(2,1)}), bf16[128,2,128,128]{3,2,1,0:T(8,128)(2,1)}, u32[]{:S(2)}, u32[]{:S(2)}) %all-to-all-start.1) | async-done | bytes 8388640 | tf_op jit(solution)/shard_map/all_to_all | solution.py:396
  137.6 18.1 %tile_and_sketch.1 = (bf16[512,13312]{1,0:T(8,128)(2,1)}, f32[512,512]{1,0:T(8,128)}) custom-call(s32[257]{0:T(512)S(1)} %pad_add_fusion.code_ref, bf16[256,128,128]{2,1,0:T(8,128)(2,1)} %bitcast.22.got_hbm, bf16[13312,512]{1,0:T(8,128)(2,1)} %omega_hbm.1), custom_call_target="tpu_custom_call" | custom-call | flops 6979321856 | bytes 35651584 | tf_op jit(solution)/shard_map/tile_and_sketch/pallas_call | solution.py:103
  155.7 0.1 collective-permute-start.6
  155.8 3.5 %all-to-all-start.2 = ((f32[4,128,512]{2,1,0:T(8,128)}), f32[4,128,512]{2,1,0:T(8,128)S(1)}, u32[]{:S(2)}, u32[]{:S(2)}) async-start(f32[4,128,512]{2,1,0:T(8,128)} %bitcast.23), calls=%async_computation.2 | async-start | bytes 2097152 | tf_op jit(solution)/shard_map/all_to_all | solution.py:421
  159.3 16.0 %all-to-all-done.2.parts_ref = f32[4,128,512]{2,1,0:T(8,128)S(1)} async-done(((f32[4,128,512]{2,1,0:T(8,128)}), f32[4,128,512]{2,1,0:T(8,128)S(1)}, u32[]{:S(2)}, u32[]{:S(2)}) %all-to-all-start.2) | async-done | bytes 1048608 | tf_op jit(solution)/shard_map/all_to_all | solution.py:421
  175.3 0.8 share_and_gram.1
  176.2 1.6 collective-permute-done
  177.8 0.3 copy.9
  178.2 21.2 %all_to_all.29 = f32[64,1,1280]{2,1,0:T(1,128)S(1)} all-to-all(f32[64,1,1280]{2,1,0:T(1,128)S(1)} %copy.9), channel_id=1, replica_groups=mesh['chips'=16,'core'=2,'cols'=4] {'chips','cols'}, dimensions={0} | all-to-all | bytes 655360 | tf_op jit(solution)/shard_map/all_to_all | solution.py:426
  199.4 0.2 reduce_sum.59
  199.6 0.9 broadcast_in_dim.61
  200.5 1.0 collective-permute-start.2
  201.5 1.7 collective-permute-start.3
  203.2 0.1 stack.90.at_ref
  203.3 0.1 collective-permute-start.4
  203.4 7.1 %all-to-all-start.4 = ((f32[64,1,1280]{2,1,0:T(1,128)}), f32[64,1,1280]{2,1,0:T(1,128)S(1)}, u32[]{:S(2)}, u32[]{:S(2)}) async-start(f32[64,1,1280]{2,1,0:T(1,128)} %broadcast_in_dim.61), calls=%async_computation.4 | async-start | bytes 655360 | tf_op jit(solution)/shard_map/all_to_all | solution.py:430
  210.6 1.7 collective-permute-done.3
  212.3 4.9 %collective-permute-done.4 = f32[128,512]{1,0:T(8,128)S(1)} collective-permute-done((f32[128,512]{1,0:T(8,128)S(1)}, f32[128,512]{1,0:T(8,128)S(1)}, u32[]{:S(2)}, u32[]{:S(2)}) %collective-permute-start.4) | collective-permute-done | bytes 262176 | tf_op jit(solution)/shard_map/ppermute | solution.py:433
  217.3 4.0 %all-to-all-done.4 = f32[64,1,1280]{2,1,0:T(1,128)S(1)} async-done(((f32[64,1,1280]{2,1,0:T(1,128)}), f32[64,1,1280]{2,1,0:T(1,128)S(1)}, u32[]{:S(2)}, u32[]{:S(2)}) %all-to-all-start.4) | async-done | bytes 327712 | tf_op jit(solution)/shard_map/all_to_all | solution.py:430
  221.4 0.1 constant_dynamic-slice_fusion
  221.5 0.8 collective-permute-start.5
  222.3 0.7 collective-permute-done.1.other_ref
  223.0 20.9 %inverse_factor.1.inverse_ref = f32[512,512]{1,0:T(8,128)S(1)} custom-call(s32[1]{0:T(128)} %bitcast.17.core_ref, f32[64,1280]{1,0:T(8,128)S(1)} %bitcast.47, f32[64,1280]{1,0:T(8,128)S(1)} %collective-permute-done.1.other_ref), custom_call_target="tpu_custom_call" | custom-call | flops 34359738368 | bytes 2097152 | tf_op jit(solution)/shard_map/inverse_factor/pallas_call | solution.py:256
  243.9 3.9 %basis_parts.1 = (bf16[256,1024]{1,0:T(8,128)(2,1)S(1)}, bf16[256,1024]{1,0:T(8,128)(2,1)S(1)}, bf16[512,128]{1,0:T(8,128)(2,1)}) custom-call(s32[17]{0:T(128)S(1)} %stack.90.at_ref, f32[512,512]{1,0:T(8,128)S(1)} %inverse_factor.1.inverse_ref, f32[512,512]{1,0:T(8,128)S(1)} %bitcast.45, f32[512,512]{1,0:T(8,128)S(1)} %collective-permute-done.5.other_ref), custom_call_target="tpu_custom_call" | custom-call | flops 2013265920 | bytes 1572864 | tf_op jit(solution)/shard_map/basis_parts/pallas_call | solution.py:311
  247.8 7.2 %product.2 = (bf16[96,6656]{1,0:T(8,128)(2,1)S(1)}, bf16[96,6656]{1,0:T(8,128)(2,1)S(1)}, f32[64,6656]{1,0:T(8,128)S(1)}) custom-call(bf16[256,1024]{1,0:T(8,128)(2,1)S(1)} %get-tuple-element.25.left_ref, bf16[512,13312]{1,0:T(8,128)(2,1)} %get-tuple-element.26.own_ref, bf16[512,13312]{1,0:T(8,128)(2,1)} %collective-permute-done.6.other_ref), custom_call_target="tpu_custom_call" | custom-call | flops 3489660928 | bytes 17039360 | tf_op jit(solution)/shard_map/product/pallas_call | solution.py:354
  255.0 1.1 collective-permute-start.8
  256.1 1.0 collective-permute-start.7
  257.1 7.2 %product.3 = (bf16[96,6656]{1,0:T(8,128)(2,1)S(1)}, bf16[96,6656]{1,0:T(8,128)(2,1)S(1)}, f32[64,6656]{1,0:T(8,128)S(1)}) custom-call(bf16[256,1024]{1,0:T(8,128)(2,1)S(1)} %get-tuple-element.30.left_ref, bf16[512,13312]{1,0:T(8,128)(2,1)} %get-tuple-element.26.own_ref, bf16[512,13312]{1,0:T(8,128)(2,1)} %collective-permute-done.6.other_ref), custom_call_target="tpu_custom_call" | custom-call | flops 3489660928 | bytes 17039360 | tf_op jit(solution)/shard_map/product/pallas_call | solution.py:354
  264.3 0.7 collective-permute-start.14
  265.0 2.7 collective-permute-start.15
  267.7 17.6 %collective-permute-done.8 = bf16[96,6656]{1,0:T(8,128)(2,1)S(1)} collective-permute-done((bf16[96,6656]{1,0:T(8,128)(2,1)S(1)}, bf16[96,6656]{1,0:T(8,128)(2,1)S(1)}, u32[]{:S(2)}, u32[]{:S(2)}) %collective-permute-start.8) | collective-permute-done | bytes 1277984 | tf_op jit(solution)/shard_map/ppermute | solution.py:466
  285.3 2.3 collective-permute-start.10
  287.7 7.5 %collective-permute-done.14 = bf16[96,6656]{1,0:T(8,128)(2,1)S(1)} collective-permute-done((bf16[96,6656]{1,0:T(8,128)(2,1)S(1)}, bf16[96,6656]{1,0:T(8,128)(2,1)S(1)}, u32[]{:S(2)}, u32[]{:S(2)}) %collective-permute-start.14) | collective-permute-done | bytes 1277984 | tf_op jit(solution)/shard_map/ppermute | solution.py:466
  295.3 3.3 %collective-permute-start.17 = (bf16[32,6656]{1,0:T(8,128)(2,1)S(1)}, bf16[32,6656]{1,0:T(8,128)(2,1)S(1)}, u32[]{:S(2)}, u32[]{:S(2)}) collective-permute-start(bf16[32,6656]{1,0:T(8,128)(2,1)S(1)} %slice.93), channel_id=1, source_target_pairs={{0,24},{8,0},{16,8},{24,16},{32,56},{40,32},{48,40},{56,48},{64,88... | collective-permute-start | bytes 1277960 | tf_op jit(solution)/shard_map/ppermute | solution.py:467
  298.6 1.0 collective-permute-done.9
  299.6 0.4 fusion.14
  300.0 0.5 collective-permute-start.11
  300.6 1.5 collective-permute-start.12
  302.1 1.5 collective-permute-start.13
  303.7 7.8 %collective-permute-done.16 = bf16[32,6656]{1,0:T(8,128)(2,1)S(1)} collective-permute-done((bf16[32,6656]{1,0:T(8,128)(2,1)S(1)}, bf16[32,6656]{1,0:T(8,128)(2,1)S(1)}, u32[]{:S(2)}, u32[]{:S(2)}) %collective-permute-start.16) | collective-permute-done | bytes 426016 | tf_op jit(solution)/shard_map/ppermute | solution.py:467
  311.5 1.7 collective-permute-done.17
  313.1 0.4 fusion.15
  313.6 0.7 collective-permute-start.18
  314.3 3.1 collective-permute-start.19
  317.3 0.9 collective-permute-start.20
  318.3 0.1 fusion.3
  318.4 2.3 collective-permute-done.18
  320.7 2.7 collective-permute-done.19
  323.4 0.4 collective-permute-done.20
  323.8 0.1 fusion.1
  323.9 1.0 pad_maximum_fusion
  (36 shorter events, 1.0 us)
Async XLA Ops:
  2.2 12.0 %copy-start = (s32[128]{0:T(128)}, s32[128]{0:T(128)S(1)}, u32[]{:S(2)}) copy-start(s32[128]{0:T(128)S(1)} %get-tuple-element.46.place_ref) | copy-start | bytes 1540
  3.1 20.1 %all-to-all-start = ((s32[128,1,2]{2,1,0:T(1,128)}), s32[128,1,2]{2,1,0:T(1,128)S(1)}, u32[]{:S(2)}, u32[]{:S(2)}) async-start(s32[128,1,2]{2,1,0:T(1,128)} %bitcast.19), calls=%async_computation | async-start | bytes 131072 | tf_op jit(solution)/shard_map/all_to_all | solution.py:399
  23.2 114.3 %all-to-all-start.1 = ((bf16[128,2,128,128]{3,2,1,0:T(8,128)(2,1)}), bf16[128,2,128,128]{3,2,1,0:T(8,128)(2,1)}, u32[]{:S(2)}, u32[]{:S(2)}) async-start(bf16[128,2,128,128]{3,2,1,0:T(8,128)(2,1)} %bitcast.48), calls=%async_computation.1 | async-start | bytes 16777216 | tf_op jit(solution)/shard_map/all_to_all | solution.py:396
  155.7 92.2 %collective-permute-start.6 = (bf16[512,13312]{1,0:T(8,128)(2,1)}, bf16[512,13312]{1,0:T(8,128)(2,1)}, u32[]{:S(2)}, u32[]{:S(2)}) collective-permute-start(bf16[512,13312]{1,0:T(8,128)(2,1)} %get-tuple-element.26.own_ref), channel_id=1, source_target_pairs={{0,4},{4,0},{1,5},{5,1},{2,6},{6,2},{3,7},{7,3},{8,12},{12,8},{9,1... | collective-permute-start | bytes 40894472 | tf_op jit(solution)/shard_map/ppermute | solution.py:418
  155.8 19.5 %all-to-all-start.2 = ((f32[4,128,512]{2,1,0:T(8,128)}), f32[4,128,512]{2,1,0:T(8,128)S(1)}, u32[]{:S(2)}, u32[]{:S(2)}) async-start(f32[4,128,512]{2,1,0:T(8,128)} %bitcast.23), calls=%async_computation.2 | async-start | bytes 2097152 | tf_op jit(solution)/shard_map/all_to_all | solution.py:421
  176.1 1.7 collective-permute-start
  200.5 10.0 %collective-permute-start.2 = (f32[128,512]{1,0:T(8,128)S(1)}, f32[128,512]{1,0:T(8,128)S(1)}, u32[]{:S(2)}, u32[]{:S(2)}) collective-permute-start(f32[128,512]{1,0:T(8,128)S(1)} %get-tuple-element.23), channel_id=1, source_target_pairs={{0,3},{1,0},{2,1},{3,2},{4,7},{5,4},{6,5},{7,6},{8,11},{9,8},{10,9... | collective-permute-start | bytes 786440 | tf_op jit(solution)/shard_map/ppermute | solution.py:433
  201.5 10.8 %collective-permute-start.3 = (f32[128,512]{1,0:T(8,128)S(1)}, f32[128,512]{1,0:T(8,128)S(1)}, u32[]{:S(2)}, u32[]{:S(2)}) collective-permute-start(f32[128,512]{1,0:T(8,128)S(1)} %get-tuple-element.23), channel_id=1, source_target_pairs={{0,2},{1,3},{2,0},{3,1},{4,6},{5,7},{6,4},{7,5},{8,10},{9,11},{10,... | collective-permute-start | bytes 786440 | tf_op jit(solution)/shard_map/ppermute | solution.py:433
  203.3 13.9 %collective-permute-start.4 = (f32[128,512]{1,0:T(8,128)S(1)}, f32[128,512]{1,0:T(8,128)S(1)}, u32[]{:S(2)}, u32[]{:S(2)}) collective-permute-start(f32[128,512]{1,0:T(8,128)S(1)} %get-tuple-element.23), channel_id=1, source_target_pairs={{0,1},{1,2},{2,3},{3,0},{4,5},{5,6},{6,7},{7,4},{8,9},{9,10},{10,1... | collective-permute-start | bytes 786440 | tf_op jit(solution)/shard_map/ppermute | solution.py:433
  203.4 17.9 %all-to-all-start.4 = ((f32[64,1,1280]{2,1,0:T(1,128)}), f32[64,1,1280]{2,1,0:T(1,128)S(1)}, u32[]{:S(2)}, u32[]{:S(2)}) async-start(f32[64,1,1280]{2,1,0:T(1,128)} %broadcast_in_dim.61), calls=%async_computation.4 | async-start | bytes 655360 | tf_op jit(solution)/shard_map/all_to_all | solution.py:430
  221.3 1.7 collective-permute-start.1
  221.5 22.4 %collective-permute-start.5 = (f32[512,512]{1,0:T(8,128)S(1)}, f32[512,512]{1,0:T(8,128)S(1)}, u32[]{:S(2)}, u32[]{:S(2)}) collective-permute-start(f32[512,512]{1,0:T(8,128)S(1)} %bitcast.44), channel_id=1, source_target_pairs={{0,4},{4,0},{1,5},{5,1},{2,6},{6,2},{3,7},{7,3},{8,12},{12,8},{9,1... | collective-permute-start | bytes 3145736 | tf_op jit(solution)/shard_map/ppermute | solution.py:439
  255.0 30.2 %collective-permute-start.8 = (bf16[96,6656]{1,0:T(8,128)(2,1)S(1)}, bf16[96,6656]{1,0:T(8,128)(2,1)S(1)}, u32[]{:S(2)}, u32[]{:S(2)}) collective-permute-start(bf16[96,6656]{1,0:T(8,128)(2,1)S(1)} %get-tuple-element.29), channel_id=1, source_target_pairs={{0,96},{8,104},{16,112},{24,120},{32,0},{40,8},{48,16},{56,24},{64... | collective-permute-start | bytes 3833864 | tf_op jit(solution)/shard_map/ppermute | solution.py:466
  256.1 31.4 %collective-permute-start.7 = (bf16[96,6656]{1,0:T(8,128)(2,1)S(1)}, bf16[96,6656]{1,0:T(8,128)(2,1)S(1)}, u32[]{:S(2)}, u32[]{:S(2)}) collective-permute-start(bf16[96,6656]{1,0:T(8,128)(2,1)S(1)} %get-tuple-element.28), channel_id=1, source_target_pairs={{0,32},{8,40},{16,48},{24,56},{32,64},{40,72},{48,80},{56,88},{64,... | collective-permute-start | bytes 3833864 | tf_op jit(solution)/shard_map/ppermute | solution.py:466
  264.3 30.8 %collective-permute-start.14 = (bf16[96,6656]{1,0:T(8,128)(2,1)S(1)}, bf16[96,6656]{1,0:T(8,128)(2,1)S(1)}, u32[]{:S(2)}, u32[]{:S(2)}) collective-permute-start(bf16[96,6656]{1,0:T(8,128)(2,1)S(1)} %get-tuple-element.32), channel_id=1, source_target_pairs={{0,8},{8,16},{16,24},{24,0},{32,40},{40,48},{48,56},{56,32},{64,72... | collective-permute-start | bytes 3833864 | tf_op jit(solution)/shard_map/ppermute | solution.py:466
  265.0 30.3 %collective-permute-start.15 = (bf16[96,6656]{1,0:T(8,128)(2,1)S(1)}, bf16[96,6656]{1,0:T(8,128)(2,1)S(1)}, u32[]{:S(2)}, u32[]{:S(2)}) collective-permute-start(bf16[96,6656]{1,0:T(8,128)(2,1)S(1)} %get-tuple-element.33), channel_id=1, source_target_pairs={{0,24},{8,0},{16,8},{24,16},{32,56},{40,32},{48,40},{56,48},{64,88... | collective-permute-start | bytes 3833864 | tf_op jit(solution)/shard_map/ppermute | solution.py:466
  285.3 13.4 %collective-permute-start.10 = (bf16[32,6656]{1,0:T(8,128)(2,1)S(1)}, bf16[32,6656]{1,0:T(8,128)(2,1)S(1)}, u32[]{:S(2)}, u32[]{:S(2)}) collective-permute-start(bf16[32,6656]{1,0:T(8,128)(2,1)S(1)} %slice.85), channel_id=1, source_target_pairs={{0,96},{8,104},{16,112},{24,120},{32,0},{40,8},{48,16},{56,24},{64... | collective-permute-start | bytes 1277960 | tf_op jit(solution)/shard_map/ppermute | solution.py:467
  287.6 12.0 %collective-permute-start.9 = (bf16[32,6656]{1,0:T(8,128)(2,1)S(1)}, bf16[32,6656]{1,0:T(8,128)(2,1)S(1)}, u32[]{:S(2)}, u32[]{:S(2)}) collective-permute-start(bf16[32,6656]{1,0:T(8,128)(2,1)S(1)} %slice.84), channel_id=1, source_target_pairs={{0,32},{8,40},{16,48},{24,56},{32,64},{40,72},{48,80},{56,88},{64,... | collective-permute-start | bytes 1277960 | tf_op jit(solution)/shard_map/ppermute | solution.py:467
  295.2 16.2 %collective-permute-start.16 = (bf16[32,6656]{1,0:T(8,128)(2,1)S(1)}, bf16[32,6656]{1,0:T(8,128)(2,1)S(1)}, u32[]{:S(2)}, u32[]{:S(2)}) collective-permute-start(bf16[32,6656]{1,0:T(8,128)(2,1)S(1)} %slice.92), channel_id=1, source_target_pairs={{0,8},{8,16},{16,24},{24,0},{32,40},{40,48},{48,56},{56,32},{64,72... | collective-permute-start | bytes 1277960 | tf_op jit(solution)/shard_map/ppermute | solution.py:467
  295.3 17.8 %collective-permute-start.17 = (bf16[32,6656]{1,0:T(8,128)(2,1)S(1)}, bf16[32,6656]{1,0:T(8,128)(2,1)S(1)}, u32[]{:S(2)}, u32[]{:S(2)}) collective-permute-start(bf16[32,6656]{1,0:T(8,128)(2,1)S(1)} %slice.93), channel_id=1, source_target_pairs={{0,24},{8,0},{16,8},{24,16},{32,56},{40,32},{48,40},{56,48},{64,88... | collective-permute-start | bytes 1277960 | tf_op jit(solution)/shard_map/ppermute | solution.py:467
  300.0 17.3 %collective-permute-start.11 = (bf16[16,6656]{1,0:T(8,128)(2,1)S(1)}, bf16[16,6656]{1,0:T(8,128)(2,1)S(1)}, u32[]{:S(2)}, u32[]{:S(2)}) collective-permute-start(bf16[16,6656]{1,0:T(8,128)(2,1)S(1)} %get-tuple-element.40), channel_id=1, source_target_pairs={{0,8},{8,16},{16,24},{24,0},{32,40},{40,48},{48,56},{56,32},{64,72... | collective-permute-start | bytes 638984 | tf_op jit(solution)/shard_map/ppermute | solution.py:473
  300.6 17.7 %collective-permute-start.12 = (bf16[16,6656]{1,0:T(8,128)(2,1)S(1)}, bf16[16,6656]{1,0:T(8,128)(2,1)S(1)}, u32[]{:S(2)}, u32[]{:S(2)}) collective-permute-start(bf16[16,6656]{1,0:T(8,128)(2,1)S(1)} %get-tuple-element.42), channel_id=1, source_target_pairs={{0,16},{8,24},{16,0},{24,8},{32,48},{40,56},{48,32},{56,40},{64,80... | collective-permute-start | bytes 638984 | tf_op jit(solution)/shard_map/ppermute | solution.py:473
  302.1 16.1 %collective-permute-start.13 = (bf16[16,6656]{1,0:T(8,128)(2,1)S(1)}, bf16[16,6656]{1,0:T(8,128)(2,1)S(1)}, u32[]{:S(2)}, u32[]{:S(2)}) collective-permute-start(bf16[16,6656]{1,0:T(8,128)(2,1)S(1)} %get-tuple-element.41), channel_id=1, source_target_pairs={{0,24},{8,0},{16,8},{24,16},{32,56},{40,32},{48,40},{56,48},{64,88... | collective-permute-start | bytes 638984 | tf_op jit(solution)/shard_map/ppermute | solution.py:473
  313.6 7.1 %collective-permute-start.18 = (bf16[16,6656]{1,0:T(8,128)(2,1)S(1)}, bf16[16,6656]{1,0:T(8,128)(2,1)S(1)}, u32[]{:S(2)}, u32[]{:S(2)}) collective-permute-start(bf16[16,6656]{1,0:T(8,128)(2,1)S(1)} %get-tuple-element.43), channel_id=1, source_target_pairs={{0,32},{8,40},{16,48},{24,56},{32,64},{40,72},{48,80},{56,88},{64,... | collective-permute-start | bytes 638984 | tf_op jit(solution)/shard_map/ppermute | solution.py:473
  314.3 9.2 %collective-permute-start.19 = (bf16[16,6656]{1,0:T(8,128)(2,1)S(1)}, bf16[16,6656]{1,0:T(8,128)(2,1)S(1)}, u32[]{:S(2)}, u32[]{:S(2)}) collective-permute-start(bf16[16,6656]{1,0:T(8,128)(2,1)S(1)} %get-tuple-element.45), channel_id=1, source_target_pairs={{0,64},{8,72},{16,80},{24,88},{32,96},{40,104},{48,112},{56,120},{... | collective-permute-start | bytes 638984 | tf_op jit(solution)/shard_map/ppermute | solution.py:473
  317.3 6.5 %collective-permute-start.20 = (bf16[16,6656]{1,0:T(8,128)(2,1)S(1)}, bf16[16,6656]{1,0:T(8,128)(2,1)S(1)}, u32[]{:S(2)}, u32[]{:S(2)}) collective-permute-start(bf16[16,6656]{1,0:T(8,128)(2,1)S(1)} %get-tuple-element.44), channel_id=1, source_target_pairs={{0,96},{8,104},{16,112},{24,120},{32,0},{40,8},{48,16},{56,24},{64... | collective-permute-start | bytes 638984 | tf_op jit(solution)/shard_map/ppermute | solution.py:473

commit v8 on v7

--- a/solution.py
+++ b/solution.py
@@ -3,6 +3,7 @@
 
 import jax
 import jax.numpy as jnp
+import numpy as np
 from jax import lax
 from jax.experimental import pallas as pl
 from jax.experimental.pallas import tpu as pltpu
@@ -377,7 +378,7 @@
     row_devices = 2 * chips
     col_devices = lax.axis_size("cols")
     devices_all = row_devices * col_devices
-    everywhere = ("chips", "core", "cols")
+    everywhere, same_core = ("chips", "core", "cols"), ("chips", "cols")
     capacity = max(2, 2 * slot_count // devices_all)
     slots = devices_all * capacity
     panel, cols = PBR * BLK, TBC * BLK
@@ -390,14 +391,26 @@
     same = (target[:, None] == target[None, :]) & (numbers[None, :] < numbers[:, None])
     place = target * capacity + jnp.sum(same.astype(jnp.int32), axis=1)
     spots = jnp.arange(slots, dtype=jnp.int32)
-    hit = place[None, :] == spots[:, None]
+    by_core = np.arange(slots, dtype=np.int32).reshape(chips, 2, col_devices, capacity)
+    by_core = jnp.asarray(by_core.transpose(0, 2, 1, 3).reshape(slots))
+    hit = place[None, :] == by_core[:, None]
     send_where = jnp.sum(jnp.where(hit, block_pos[None, :] + 1, 0), axis=1)
     send_blocks = bucket(place, blocks, slots)
     got_blocks = lax.all_to_all(
         send_blocks.reshape(devices_all, capacity, BLK, BLK), everywhere, 0, 0, tiled=True
     ).reshape(slots, BLK, BLK)
     got_where = lax.all_to_all(
-        send_where.reshape(devices_all, capacity), everywhere, 0, 0, tiled=True
+        send_where.reshape(devices_all // 2, 2 * capacity), same_core, 0, 0, tiled=True
+    ).reshape(devices_all // 2, 2, capacity)
+    first, second = got_where[:, 0], got_where[:, 1]
+    kept = jnp.where(core == 0, first, second)
+    come = swap(jnp.where(core == 0, second, first))
+    got_where = jnp.stack(
+        [
+            jnp.where(core == 0, part, other).reshape(chips, col_devices, capacity)
+            for part, other in ((kept, come), (come, kept))
+        ],
+        axis=1,
     ).reshape(slots)
 
     key = jnp.where(got_where == 0, PBR * TBC, got_where - 1)
@@ -421,7 +434,6 @@
     parts = lax.all_to_all(part.reshape(col_devices, share, rank), "cols", 0, 0, tiled=True)
     which = core.astype(jnp.int32)[None]
     own_share, keep, send = share_and_gram(which, parts)
-    same_core = ("chips", "cols")
     gram_rows = (chips * col_devices, BLK // devices_all, keep.shape[1])
     grams = lax.all_to_all((keep + swap(send)).reshape(gram_rows), same_core, 0, 0, tiled=True)
     gram, late_share = lax.optimization_barrier(

time: 325 us -> 324 us (level)
  waiting for transfers between devices: 180 us -> 165 us
  blocking collectives: 21.2 us -> 35 us
  starting transfers between devices: 51.3 us -> 48 us
    all_to_all x0 -> x1, blocking collectives: none -> 18.4 us  [on_device(): lax.all_to_all(part.reshape(col_devices, share, rank), 'cols', 0, 0, tile...]
    all_to_all x2 -> x1, waiting for transfers between devices: 20 us -> 4.62 us  [on_device(): lax.all_to_all(send_where.reshape(devices_all // 2, 2 * capacity), same_c...]
    all_to_all x1, blocking collectives: 21.2 us -> 16.5 us  [on_device(): lax.all_to_all((keep + swap(send)).reshape(gram_rows), same_core, 0, 0, t...]
    all_to_all x2 -> x1, starting transfers between devices: 14.7 us -> 11.5 us  [on_device(): lax.all_to_all(send_where.reshape(devices_all // 2, 2 * capacity), same_c...]
  transfers between devices with their start and end apart: 25 -> 25, of which waited for: 16 -> 15; matrix products, arithmetic and copies ran while one was open for 2% -> 2% of each run, Pallas kernels for 12% -> 12%
where the time goes in v8:
time: 324 us
  waiting for transfers between devices  165 us (51%)
  Pallas kernels  65.6 us (20%)
  starting transfers between devices  48 us (15%)
  blocking collectives  35 us (11%)
  other arithmetic  6.48 us (2%)
    all_to_all x1, waiting for transfers between devices, on_device(): lax.all_to_all(send_blocks.reshape(devices_all, capacity, BLK, BLK), ever...  104 us
    ppermute x4, waiting for transfers between devices, scatter(): ahead, behind = (forward(ahead), backward(behind))  24.1 us
    pallas_call x1, Pallas kernels, inverse_factor(): pl.pallas_call(functools.partial(factor_kernel, scale), grid_spec=pltpu.P...  20.9 us
    pallas_call x1, Pallas kernels, tile_and_sketch(): pl.pallas_call(tile_kernel, grid_spec=pltpu.PrefetchScalarGridSpec(num_sc...  20.8 us
    all_to_all x1, blocking collectives, on_device(): lax.all_to_all(part.reshape(col_devices, share, rank), 'cols', 0, 0, tile...  18.4 us
    all_to_all x1, blocking collectives, on_device(): lax.all_to_all((keep + swap(send)).reshape(gram_rows), same_core, 0, 0, t...  16.5 us
    pallas_call x2, Pallas kernels, product(): pl.pallas_call(functools.partial(product_kernel, scale), grid=(steps,), i...  14.4 us
    all_to_all x1, starting transfers between devices, on_device(): lax.all_to_all(send_where.reshape(devices_all // 2, 2 * capacity), same_c...  11.5 us
  transfers between devices with their start and end apart: 25, of which 15 were waited for; matrix products, arithmetic and copies ran while one was open for 2% of the time, Pallas kernels for 12%

profile of v8, /device:TPU:0, one launch (start us, length us, event | category | flops | bytes accessed | tf_op | source)
XLA Modules:
  0.0 324.4 jit_solution(1151864675516773715)
XLA Ops:
  0.6 0.9 convert_reduce_fusion.1
  1.5 0.7 multiply_add_fusion
  2.2 0.9 select_reduce_fusion.1
  3.1 0.7 all_to_all.18
  3.8 11.5 %all-to-all-start = ((s32[64,1,4]{2,1,0:T(1,128)}), s32[64,1,4]{2,1,0:T(1,128)S(1)}, u32[]{:S(2)}, u32[]{:S(2)}) async-start(s32[64,1,4]{2,1,0:T(1,128)} %bitcast.19), calls=%async_computation | async-start | bytes 65536 | tf_op jit(solution)/shard_map/all_to_all | solution.py:402
  15.3 4.8 %bucket.1 = bf16[256,128,128]{2,1,0:T(8,128)(2,1)} custom-call(s32[128]{0:T(128)} %copy-done, bf16[128,128,128]{2,1,0:T(8,128)(2,1)} %blocks_ref.1), custom_call_target="tpu_custom_call" | custom-call | bytes 8388608 | tf_op jit(solution)/shard_map/bucket/pallas_call | solution.py:31
  20.2 4.6 %all-to-all-done = s32[64,1,4]{2,1,0:T(1,128)S(1)} async-done(((s32[64,1,4]{2,1,0:T(1,128)}), s32[64,1,4]{2,1,0:T(1,128)S(1)}, u32[]{:S(2)}, u32[]{:S(2)}) %all-to-all-start) | async-done | bytes 1056 | tf_op jit(solution)/shard_map/all_to_all | solution.py:402
  24.8 5.9 %all-to-all-start.1 = ((bf16[128,2,128,128]{3,2,1,0:T(8,128)(2,1)}), bf16[128,2,128,128]{3,2,1,0:T(8,128)(2,1)}, u32[]{:S(2)}, u32[]{:S(2)}) async-start(bf16[128,2,128,128]{3,2,1,0:T(8,128)(2,1)} %bitcast.59), calls=%async_computation.1 | async-start | bytes 16777216 | tf_op jit(solution)/shard_map/all_to_all | solution.py:399
  30.8 1.1 collective-permute-done
  32.1 0.1 copy.20
  32.2 0.1 copy.21
  32.3 0.7 convert_reduce_fusion.2
  33.0 0.1 copy.22
  33.1 0.1 select_n.187
  33.3 0.2 convert_reduce_fusion
  33.5 0.1 select_reduce_fusion
  33.8 0.7 pad_add_fusion.1.code_ref
  34.5 104.3 %all-to-all-done.1 = bf16[128,2,128,128]{3,2,1,0:T(8,128)(2,1)} async-done(((bf16[128,2,128,128]{3,2,1,0:T(8,128)(2,1)}), bf16[128,2,128,128]{3,2,1,0:T(8,128)(2,1)}, u32[]{:S(2)}, u32[]{:S(2)}) %all-to-all-start.1) | async-done | bytes 8388640 | tf_op jit(solution)/shard_map/all_to_all | solution.py:399
  138.8 20.8 %tile_and_sketch.1 = (bf16[512,13312]{1,0:T(8,128)(2,1)}, f32[512,512]{1,0:T(8,128)S(1)}) custom-call(s32[257]{0:T(512)S(1)} %pad_add_fusion.1.code_ref, bf16[256,128,128]{2,1,0:T(8,128)(2,1)} %bitcast.25.got_hbm, bf16[13312,512]{1,0:T(8,128)(2,1)} %omega_hbm.1), custom_call_target="tpu_custom_call" | custom-call | flops 6979321856 | bytes 35651584 | tf_op jit(solution)/shard_map/tile_and_sketch/pallas_call | solution.py:104
  159.6 0.1 collective-permute-start.7
  159.7 18.4 %all_to_all.29.parts_ref = f32[4,128,512]{2,1,0:T(8,128)S(1)} all-to-all(f32[4,128,512]{2,1,0:T(8,128)S(1)} %bitcast.56), channel_id=1, replica_groups=mesh['chips'=16,'core'=2,'cols'=4] {'cols'}, dimensions={0} | all-to-all | bytes 2097152 | tf_op jit(solution)/shard_map/all_to_all | solution.py:434
  178.1 0.8 share_and_gram.1
  179.0 1.8 collective-permute-done.1
  180.8 0.3 copy.23
  181.2 16.5 %all_to_all.30 = f32[64,1,1280]{2,1,0:T(1,128)S(1)} all-to-all(f32[64,1,1280]{2,1,0:T(1,128)S(1)} %copy.23), channel_id=1, replica_groups=mesh['chips'=16,'core'=2,'cols'=4] {'chips','cols'}, dimensions={0} | all-to-all | bytes 655360 | tf_op jit(solution)/shard_map/all_to_all | solution.py:438
  197.7 0.2 reduce_sum.59
  197.9 0.9 broadcast_in_dim.61
  198.8 1.0 collective-permute-start.3
  199.8 1.7 collective-permute-start.4
  201.5 0.1 stack.93.at_ref
  201.6 0.1 collective-permute-start.5
  201.7 7.1 %all-to-all-start.4 = ((f32[64,1,1280]{2,1,0:T(1,128)}), f32[64,1,1280]{2,1,0:T(1,128)S(1)}, u32[]{:S(2)}, u32[]{:S(2)}) async-start(f32[64,1,1280]{2,1,0:T(1,128)} %broadcast_in_dim.61), calls=%async_computation.4 | async-start | bytes 655360 | tf_op jit(solution)/shard_map/all_to_all | solution.py:442
  208.9 1.7 collective-permute-done.4
  210.6 5.6 %collective-permute-done.5 = f32[128,512]{1,0:T(8,128)S(1)} collective-permute-done((f32[128,512]{1,0:T(8,128)S(1)}, f32[128,512]{1,0:T(8,128)S(1)}, u32[]{:S(2)}, u32[]{:S(2)}) %collective-permute-start.5) | collective-permute-done | bytes 262176 | tf_op jit(solution)/shard_map/ppermute | solution.py:445
  216.3 3.2 all-to-all-done.4
  219.7 0.1 constant_dynamic-slice_fusion
  219.8 0.8 collective-permute-start.6
  220.6 0.7 collective-permute-done.2.other_ref
  221.3 20.9 %inverse_factor.1.inverse_ref = f32[512,512]{1,0:T(8,128)S(1)} custom-call(s32[1]{0:T(128)} %bitcast.17.core_ref, f32[64,1280]{1,0:T(8,128)S(1)} %bitcast.58, f32[64,1280]{1,0:T(8,128)S(1)} %collective-permute-done.2.other_ref), custom_call_target="tpu_custom_call" | custom-call | flops 34359738368 | bytes 2097152 | tf_op jit(solution)/shard_map/inverse_factor/pallas_call | solution.py:257
  242.2 3.9 %basis_parts.1 = (bf16[256,1024]{1,0:T(8,128)(2,1)S(1)}, bf16[256,1024]{1,0:T(8,128)(2,1)S(1)}, bf16[512,128]{1,0:T(8,128)(2,1)}) custom-call(s32[17]{0:T(128)S(1)} %stack.93.at_ref, f32[512,512]{1,0:T(8,128)S(1)} %inverse_factor.1.inverse_ref, f32[512,512]{1,0:T(8,128)S(1)} %bitcast.55, f32[512,512]{1,0:T(8,128)S(1)} %collective-permute-done.6.other_ref), custom_call_target="tpu_custom_call" | custom-call | flops 2013265920 | bytes 1572864 | tf_op jit(solution)/shard_map/basis_parts/pallas_call | solution.py:312
  246.1 7.2 %product.2 = (bf16[96,6656]{1,0:T(8,128)(2,1)S(1)}, bf16[96,6656]{1,0:T(8,128)(2,1)S(1)}, f32[64,6656]{1,0:T(8,128)S(1)}) custom-call(bf16[256,1024]{1,0:T(8,128)(2,1)S(1)} %get-tuple-element.25.left_ref, bf16[512,13312]{1,0:T(8,128)(2,1)} %get-tuple-element.26.own_ref, bf16[512,13312]{1,0:T(8,128)(2,1)} %collective-permute-done.7.other_ref), custom_call_target="tpu_custom_call" | custom-call | flops 3489660928 | bytes 17039360 | tf_op jit(solution)/shard_map/product/pallas_call | solution.py:355
  253.3 0.7 collective-permute-start.8
  254.0 2.6 collective-permute-start.9
  256.6 7.2 %product.3 = (bf16[96,6656]{1,0:T(8,128)(2,1)S(1)}, bf16[96,6656]{1,0:T(8,128)(2,1)S(1)}, f32[64,6656]{1,0:T(8,128)S(1)}) custom-call(bf16[256,1024]{1,0:T(8,128)(2,1)S(1)} %get-tuple-element.30.left_ref, bf16[512,13312]{1,0:T(8,128)(2,1)} %get-tuple-element.26.own_ref, bf16[512,13312]{1,0:T(8,128)(2,1)} %collective-permute-done.7.other_ref), custom_call_target="tpu_custom_call" | custom-call | flops 3489660928 | bytes 17039360 | tf_op jit(solution)/shard_map/product/pallas_call | solution.py:355
  263.9 0.6 collective-permute-start.15
  264.5 2.7 collective-permute-start.16
  267.2 17.6 %collective-permute-done.8 = bf16[96,6656]{1,0:T(8,128)(2,1)S(1)} collective-permute-done((bf16[96,6656]{1,0:T(8,128)(2,1)S(1)}, bf16[96,6656]{1,0:T(8,128)(2,1)S(1)}, u32[]{:S(2)}, u32[]{:S(2)}) %collective-permute-start.8) | collective-permute-done | bytes 1277984 | tf_op jit(solution)/shard_map/ppermute | solution.py:478
  284.9 3.3 %collective-permute-start.11 = (bf16[32,6656]{1,0:T(8,128)(2,1)S(1)}, bf16[32,6656]{1,0:T(8,128)(2,1)S(1)}, u32[]{:S(2)}, u32[]{:S(2)}) collective-permute-start(bf16[32,6656]{1,0:T(8,128)(2,1)S(1)} %slice.95), channel_id=1, source_target_pairs={{0,96},{8,104},{16,112},{24,120},{32,0},{40,8},{48,16},{56,24},{64... | collective-permute-start | bytes 1277960 | tf_op jit(solution)/shard_map/ppermute | solution.py:479
  288.2 6.5 %collective-permute-done.15 = bf16[96,6656]{1,0:T(8,128)(2,1)S(1)} collective-permute-done((bf16[96,6656]{1,0:T(8,128)(2,1)S(1)}, bf16[96,6656]{1,0:T(8,128)(2,1)S(1)}, u32[]{:S(2)}, u32[]{:S(2)}) %collective-permute-start.15) | collective-permute-done | bytes 1277984 | tf_op jit(solution)/shard_map/ppermute | solution.py:478
  294.8 3.3 %collective-permute-start.18 = (bf16[32,6656]{1,0:T(8,128)(2,1)S(1)}, bf16[32,6656]{1,0:T(8,128)(2,1)S(1)}, u32[]{:S(2)}, u32[]{:S(2)}) collective-permute-start(bf16[32,6656]{1,0:T(8,128)(2,1)S(1)} %slice.103), channel_id=1, source_target_pairs={{0,24},{8,0},{16,8},{24,16},{32,56},{40,32},{48,40},{56,48},{64,88... | collective-permute-start | bytes 1277960 | tf_op jit(solution)/shard_map/ppermute | solution.py:479
  298.1 0.4 fusion.12
  298.6 1.5 collective-permute-start.13
  300.1 1.7 collective-permute-start.14
  301.9 9.1 %collective-permute-done.17 = bf16[32,6656]{1,0:T(8,128)(2,1)S(1)} collective-permute-done((bf16[32,6656]{1,0:T(8,128)(2,1)S(1)}, bf16[32,6656]{1,0:T(8,128)(2,1)S(1)}, u32[]{:S(2)}, u32[]{:S(2)}) %collective-permute-start.17) | collective-permute-done | bytes 426016 | tf_op jit(solution)/shard_map/ppermute | solution.py:479
  310.9 1.7 collective-permute-done.18
  312.6 0.4 fusion.13
  313.1 2.1 collective-permute-start.20
  315.2 0.3 collective-permute-done.12
  315.5 0.9 collective-permute-start.21
  316.4 0.1 fusion.3
  316.5 6.0 %collective-permute-done.19 = bf16[16,6656]{1,0:T(8,128)(2,1)S(1)} collective-permute-done((bf16[16,6656]{1,0:T(8,128)(2,1)S(1)}, bf16[16,6656]{1,0:T(8,128)(2,1)S(1)}, u32[]{:S(2)}, u32[]{:S(2)}) %collective-permute-start.19) | collective-permute-done | bytes 213024 | tf_op jit(solution)/shard_map/ppermute | solution.py:485
  322.5 0.9 collective-permute-done.21
  323.4 0.1 fusion.1
  323.5 1.0 pad_maximum_fusion
  (45 shorter events, 1.4 us)
Async XLA Ops:
  2.2 13.1 %copy-start = (s32[128]{0:T(128)}, s32[128]{0:T(128)S(1)}, u32[]{:S(2)}) copy-start(s32[128]{0:T(128)S(1)} %get-tuple-element.48.place_ref) | copy-start | bytes 1540
  3.8 21.0 %all-to-all-start = ((s32[64,1,4]{2,1,0:T(1,128)}), s32[64,1,4]{2,1,0:T(1,128)S(1)}, u32[]{:S(2)}, u32[]{:S(2)}) async-start(s32[64,1,4]{2,1,0:T(1,128)} %bitcast.19), calls=%async_computation | async-start | bytes 65536 | tf_op jit(solution)/shard_map/all_to_all | solution.py:402
  24.8 114.0 %all-to-all-start.1 = ((bf16[128,2,128,128]{3,2,1,0:T(8,128)(2,1)}), bf16[128,2,128,128]{3,2,1,0:T(8,128)(2,1)}, u32[]{:S(2)}, u32[]{:S(2)}) async-start(bf16[128,2,128,128]{3,2,1,0:T(8,128)(2,1)} %bitcast.59), calls=%async_computation.1 | async-start | bytes 16777216 | tf_op jit(solution)/shard_map/all_to_all | solution.py:399
  30.8 1.2 collective-permute-start
  159.6 86.6 %collective-permute-start.7 = (bf16[512,13312]{1,0:T(8,128)(2,1)}, bf16[512,13312]{1,0:T(8,128)(2,1)}, u32[]{:S(2)}, u32[]{:S(2)}) collective-permute-start(bf16[512,13312]{1,0:T(8,128)(2,1)} %get-tuple-element.26.own_ref), channel_id=1, source_target_pairs={{0,4},{4,0},{1,5},{5,1},{2,6},{6,2},{3,7},{7,3},{8,12},{12,8},{9,1... | collective-permute-start | bytes 40894472 | tf_op jit(solution)/shard_map/ppermute | solution.py:431
  178.9 1.9 collective-permute-start.1
  198.8 10.0 %collective-permute-start.3 = (f32[128,512]{1,0:T(8,128)S(1)}, f32[128,512]{1,0:T(8,128)S(1)}, u32[]{:S(2)}, u32[]{:S(2)}) collective-permute-start(f32[128,512]{1,0:T(8,128)S(1)} %get-tuple-element.23), channel_id=1, source_target_pairs={{0,3},{1,0},{2,1},{3,2},{4,7},{5,4},{6,5},{7,6},{8,11},{9,8},{10,9... | collective-permute-start | bytes 786440 | tf_op jit(solution)/shard_map/ppermute | solution.py:445
  199.8 10.8 %collective-permute-start.4 = (f32[128,512]{1,0:T(8,128)S(1)}, f32[128,512]{1,0:T(8,128)S(1)}, u32[]{:S(2)}, u32[]{:S(2)}) collective-permute-start(f32[128,512]{1,0:T(8,128)S(1)} %get-tuple-element.23), channel_id=1, source_target_pairs={{0,2},{1,3},{2,0},{3,1},{4,6},{5,7},{6,4},{7,5},{8,10},{9,11},{10,... | collective-permute-start | bytes 786440 | tf_op jit(solution)/shard_map/ppermute | solution.py:445
  201.6 14.6 %collective-permute-start.5 = (f32[128,512]{1,0:T(8,128)S(1)}, f32[128,512]{1,0:T(8,128)S(1)}, u32[]{:S(2)}, u32[]{:S(2)}) collective-permute-start(f32[128,512]{1,0:T(8,128)S(1)} %get-tuple-element.23), channel_id=1, source_target_pairs={{0,1},{1,2},{2,3},{3,0},{4,5},{5,6},{6,7},{7,4},{8,9},{9,10},{10,1... | collective-permute-start | bytes 786440 | tf_op jit(solution)/shard_map/ppermute | solution.py:445
  201.7 17.9 %all-to-all-start.4 = ((f32[64,1,1280]{2,1,0:T(1,128)}), f32[64,1,1280]{2,1,0:T(1,128)S(1)}, u32[]{:S(2)}, u32[]{:S(2)}) async-start(f32[64,1,1280]{2,1,0:T(1,128)} %broadcast_in_dim.61), calls=%async_computation.4 | async-start | bytes 655360 | tf_op jit(solution)/shard_map/all_to_all | solution.py:442
  219.6 1.7 collective-permute-start.2
  219.8 22.4 %collective-permute-start.6 = (f32[512,512]{1,0:T(8,128)S(1)}, f32[512,512]{1,0:T(8,128)S(1)}, u32[]{:S(2)}, u32[]{:S(2)}) collective-permute-start(f32[512,512]{1,0:T(8,128)S(1)} %bitcast.54), channel_id=1, source_target_pairs={{0,4},{4,0},{1,5},{5,1},{2,6},{6,2},{3,7},{7,3},{8,12},{12,8},{9,1... | collective-permute-start | bytes 3145736 | tf_op jit(solution)/shard_map/ppermute | solution.py:451
  253.3 31.4 %collective-permute-start.8 = (bf16[96,6656]{1,0:T(8,128)(2,1)S(1)}, bf16[96,6656]{1,0:T(8,128)(2,1)S(1)}, u32[]{:S(2)}, u32[]{:S(2)}) collective-permute-start(bf16[96,6656]{1,0:T(8,128)(2,1)S(1)} %get-tuple-element.28), channel_id=1, source_target_pairs={{0,32},{8,40},{16,48},{24,56},{32,64},{40,72},{48,80},{56,88},{64,... | collective-permute-start | bytes 3833864 | tf_op jit(solution)/shard_map/ppermute | solution.py:478
  254.0 30.8 %collective-permute-start.9 = (bf16[96,6656]{1,0:T(8,128)(2,1)S(1)}, bf16[96,6656]{1,0:T(8,128)(2,1)S(1)}, u32[]{:S(2)}, u32[]{:S(2)}) collective-permute-start(bf16[96,6656]{1,0:T(8,128)(2,1)S(1)} %get-tuple-element.29), channel_id=1, source_target_pairs={{0,96},{8,104},{16,112},{24,120},{32,0},{40,8},{48,16},{56,24},{64... | collective-permute-start | bytes 3833864 | tf_op jit(solution)/shard_map/ppermute | solution.py:478
  263.9 30.8 %collective-permute-start.15 = (bf16[96,6656]{1,0:T(8,128)(2,1)S(1)}, bf16[96,6656]{1,0:T(8,128)(2,1)S(1)}, u32[]{:S(2)}, u32[]{:S(2)}) collective-permute-start(bf16[96,6656]{1,0:T(8,128)(2,1)S(1)} %get-tuple-element.32), channel_id=1, source_target_pairs={{0,8},{8,16},{16,24},{24,0},{32,40},{40,48},{48,56},{56,32},{64,72... | collective-permute-start | bytes 3833864 | tf_op jit(solution)/shard_map/ppermute | solution.py:478
  264.5 30.3 %collective-permute-start.16 = (bf16[96,6656]{1,0:T(8,128)(2,1)S(1)}, bf16[96,6656]{1,0:T(8,128)(2,1)S(1)}, u32[]{:S(2)}, u32[]{:S(2)}) collective-permute-start(bf16[96,6656]{1,0:T(8,128)(2,1)S(1)} %get-tuple-element.33), channel_id=1, source_target_pairs={{0,24},{8,0},{16,8},{24,16},{32,56},{40,32},{48,40},{56,48},{64,88... | collective-permute-start | bytes 3833864 | tf_op jit(solution)/shard_map/ppermute | solution.py:478
  284.8 13.4 %collective-permute-start.10 = (bf16[32,6656]{1,0:T(8,128)(2,1)S(1)}, bf16[32,6656]{1,0:T(8,128)(2,1)S(1)}, u32[]{:S(2)}, u32[]{:S(2)}) collective-permute-start(bf16[32,6656]{1,0:T(8,128)(2,1)S(1)} %slice.94), channel_id=1, source_target_pairs={{0,32},{8,40},{16,48},{24,56},{32,64},{40,72},{48,80},{56,88},{64,... | collective-permute-start | bytes 1277960 | tf_op jit(solution)/shard_map/ppermute | solution.py:479
  284.9 13.2 %collective-permute-start.11 = (bf16[32,6656]{1,0:T(8,128)(2,1)S(1)}, bf16[32,6656]{1,0:T(8,128)(2,1)S(1)}, u32[]{:S(2)}, u32[]{:S(2)}) collective-permute-start(bf16[32,6656]{1,0:T(8,128)(2,1)S(1)} %slice.95), channel_id=1, source_target_pairs={{0,96},{8,104},{16,112},{24,120},{32,0},{40,8},{48,16},{56,24},{64... | collective-permute-start | bytes 1277960 | tf_op jit(solution)/shard_map/ppermute | solution.py:479
  294.7 16.2 %collective-permute-start.17 = (bf16[32,6656]{1,0:T(8,128)(2,1)S(1)}, bf16[32,6656]{1,0:T(8,128)(2,1)S(1)}, u32[]{:S(2)}, u32[]{:S(2)}) collective-permute-start(bf16[32,6656]{1,0:T(8,128)(2,1)S(1)} %slice.102), channel_id=1, source_target_pairs={{0,8},{8,16},{16,24},{24,0},{32,40},{40,48},{48,56},{56,32},{64,72... | collective-permute-start | bytes 1277960 | tf_op jit(solution)/shard_map/ppermute | solution.py:479
  294.8 17.7 %collective-permute-start.18 = (bf16[32,6656]{1,0:T(8,128)(2,1)S(1)}, bf16[32,6656]{1,0:T(8,128)(2,1)S(1)}, u32[]{:S(2)}, u32[]{:S(2)}) collective-permute-start(bf16[32,6656]{1,0:T(8,128)(2,1)S(1)} %slice.103), channel_id=1, source_target_pairs={{0,24},{8,0},{16,8},{24,16},{32,56},{40,32},{48,40},{56,48},{64,88... | collective-permute-start | bytes 1277960 | tf_op jit(solution)/shard_map/ppermute | solution.py:479
  298.6 17.0 %collective-permute-start.12 = (bf16[16,6656]{1,0:T(8,128)(2,1)S(1)}, bf16[16,6656]{1,0:T(8,128)(2,1)S(1)}, u32[]{:S(2)}, u32[]{:S(2)}) collective-permute-start(bf16[16,6656]{1,0:T(8,128)(2,1)S(1)} %get-tuple-element.40), channel_id=1, source_target_pairs={{0,8},{8,16},{16,24},{24,0},{32,40},{40,48},{48,56},{56,32},{64,72... | collective-permute-start | bytes 638984 | tf_op jit(solution)/shard_map/ppermute | solution.py:485
  298.6 17.7 %collective-permute-start.13 = (bf16[16,6656]{1,0:T(8,128)(2,1)S(1)}, bf16[16,6656]{1,0:T(8,128)(2,1)S(1)}, u32[]{:S(2)}, u32[]{:S(2)}) collective-permute-start(bf16[16,6656]{1,0:T(8,128)(2,1)S(1)} %get-tuple-element.42), channel_id=1, source_target_pairs={{0,16},{8,24},{16,0},{24,8},{32,48},{40,56},{48,32},{56,40},{64,80... | collective-permute-start | bytes 638984 | tf_op jit(solution)/shard_map/ppermute | solution.py:485
  300.1 16.3 %collective-permute-start.14 = (bf16[16,6656]{1,0:T(8,128)(2,1)S(1)}, bf16[16,6656]{1,0:T(8,128)(2,1)S(1)}, u32[]{:S(2)}, u32[]{:S(2)}) collective-permute-start(bf16[16,6656]{1,0:T(8,128)(2,1)S(1)} %get-tuple-element.41), channel_id=1, source_target_pairs={{0,24},{8,0},{16,8},{24,16},{32,56},{40,32},{48,40},{56,48},{64,88... | collective-permute-start | bytes 638984 | tf_op jit(solution)/shard_map/ppermute | solution.py:485
  313.0 9.4 %collective-permute-start.19 = (bf16[16,6656]{1,0:T(8,128)(2,1)S(1)}, bf16[16,6656]{1,0:T(8,128)(2,1)S(1)}, u32[]{:S(2)}, u32[]{:S(2)}) collective-permute-start(bf16[16,6656]{1,0:T(8,128)(2,1)S(1)} %get-tuple-element.43), channel_id=1, source_target_pairs={{0,32},{8,40},{16,48},{24,56},{32,64},{40,72},{48,80},{56,88},{64,... | collective-permute-start | bytes 638984 | tf_op jit(solution)/shard_map/ppermute | solution.py:485
  313.1 9.3 %collective-permute-start.20 = (bf16[16,6656]{1,0:T(8,128)(2,1)S(1)}, bf16[16,6656]{1,0:T(8,128)(2,1)S(1)}, u32[]{:S(2)}, u32[]{:S(2)}) collective-permute-start(bf16[16,6656]{1,0:T(8,128)(2,1)S(1)} %get-tuple-element.45), channel_id=1, source_target_pairs={{0,64},{8,72},{16,80},{24,88},{32,96},{40,104},{48,112},{56,120},{... | collective-permute-start | bytes 638984 | tf_op jit(solution)/shard_map/ppermute | solution.py:485
  315.5 7.8 %collective-permute-start.21 = (bf16[16,6656]{1,0:T(8,128)(2,1)S(1)}, bf16[16,6656]{1,0:T(8,128)(2,1)S(1)}, u32[]{:S(2)}, u32[]{:S(2)}) collective-permute-start(bf16[16,6656]{1,0:T(8,128)(2,1)S(1)} %get-tuple-element.44), channel_id=1, source_target_pairs={{0,96},{8,104},{16,112},{24,120},{32,0},{40,8},{48,16},{56,24},{64... | collective-permute-start | bytes 638984 | tf_op jit(solution)/shard_map/ppermute | solution.py:485

commit v9 on v7

--- a/solution.py
+++ b/solution.py
@@ -473,10 +473,14 @@
             result += shift(not x_first, i)(terms[i].astype(jnp.bfloat16)).astype(jnp.float32)
         return result
 
-    cut = TBC // 2 * BLK
-    one = multiply(0, cut, left)
-    two = multiply(cut, cols - cut, turned)
-    coefficients = jnp.concatenate([scatter(*one, True), scatter(*two, False)], axis=1)
+    quarter = cols // 4
+    coefficients = jnp.concatenate(
+        [
+            scatter(*multiply(i * quarter, quarter, (left, turned)[i % 2]), i % 2 == 0)
+            for i in range(4)
+        ],
+        axis=1,
+    )
     return basis, coefficients
 
 

time: 325 us -> 325 us (level)
  waiting for transfers between devices: 180 us -> 164 us
  starting transfers between devices: 51.3 us -> 63.5 us
  Pallas kernels: 63 us -> 66.3 us
    ppermute x4 -> x8, waiting for transfers between devices: 25.1 us -> 13 us  [scatter(): ahead, behind = (forward(ahead), backward(behind))]
    ppermute x2 -> x4, waiting for transfers between devices: 8.79 us -> 4.1 us  [scatter(): forward(ahead[:FAR * ranks])]
    ppermute x4 -> x8, starting transfers between devices: 5.4 us -> 9.61 us  [scatter(): ahead, behind = (forward(ahead), backward(behind))]
    ppermute x6 -> x12, starting transfers between devices: 8.31 us -> 11.7 us  [scatter(): shift(not x_first, i)(terms[i].astype(jnp.bfloat16)).astype(jnp.float32)]
    pallas_call x2 -> x4, Pallas kernels: 14.4 us -> 17.6 us  [product(): pl.pallas_call(functools.partial(product_kernel, scale), grid=(steps,), i...]
    ppermute x6 -> x12, waiting for transfers between devices: 5.47 us -> 8.35 us  [scatter(): shift(not x_first, i)(terms[i].astype(jnp.bfloat16)).astype(jnp.float32)]
    ppermute x2 -> x4, starting transfers between devices: 5.58 us -> 8.11 us  [scatter(): backward(behind[:FAR * ranks])]
  transfers between devices with their start and end apart: 25 -> 39, of which waited for: 16 -> 18; matrix products, arithmetic and copies ran while one was open for 2% -> 2% of each run, Pallas kernels for 12% -> 13%
where the time goes in v9:
time: 325 us
  waiting for transfers between devices  164 us (50%)
  Pallas kernels  66.3 us (20%)
  starting transfers between devices  63.5 us (20%)
  blocking collectives  21.1 us (6%)
  other arithmetic  5.98 us (2%)
    all_to_all x1, waiting for transfers between devices, on_device(): lax.all_to_all(send_blocks.reshape(devices_all, capacity, BLK, BLK), ever...  106 us
    all_to_all x1, blocking collectives, on_device(): lax.all_to_all((keep + swap(send)).reshape(gram_rows), same_core, 0, 0, t...  21.1 us
    pallas_call x1, Pallas kernels, inverse_factor(): pl.pallas_call(functools.partial(factor_kernel, scale), grid_spec=pltpu.P...  20.9 us
    pallas_call x1, Pallas kernels, tile_and_sketch(): pl.pallas_call(tile_kernel, grid_spec=pltpu.PrefetchScalarGridSpec(num_sc...  18.1 us
    pallas_call x4, Pallas kernels, product(): pl.pallas_call(functools.partial(product_kernel, scale), grid=(steps,), i...  17.6 us
    all_to_all x1, waiting for transfers between devices, on_device(): lax.all_to_all(part.reshape(col_devices, share, rank), 'cols', 0, 0, tile...  15.9 us
    ppermute x8, waiting for transfers between devices, scatter(): ahead, behind = (forward(ahead), backward(behind))  13 us
    ppermute x12, starting transfers between devices, scatter(): shift(not x_first, i)(terms[i].astype(jnp.bfloat16)).astype(jnp.float32)  11.7 us
  transfers between devices with their start and end apart: 39, of which 18 were waited for; matrix products, arithmetic and copies ran while one was open for 2% of the time, Pallas kernels for 13%

profile of v9, /device:TPU:0, one launch (start us, length us, event | category | flops | bytes accessed | tf_op | source)
XLA Modules:
  0.0 325.0 jit_solution(9647226465294659086)
XLA Ops:
  0.6 0.9 convert_reduce_fusion.1
  1.5 0.7 multiply_add_fusion
  2.3 0.8 all_to_all.18
  3.1 11.1 %all-to-all-start = ((s32[128,1,2]{2,1,0:T(1,128)}), s32[128,1,2]{2,1,0:T(1,128)S(1)}, u32[]{:S(2)}, u32[]{:S(2)}) async-start(s32[128,1,2]{2,1,0:T(1,128)} %bitcast.19), calls=%async_computation | async-start | bytes 131072 | tf_op jit(solution)/shard_map/all_to_all | solution.py:399
  14.3 5.0 %bucket.1 = bf16[256,128,128]{2,1,0:T(8,128)(2,1)} custom-call(s32[128]{0:T(128)} %copy-done, bf16[128,128,128]{2,1,0:T(8,128)(2,1)} %blocks_ref.1), custom_call_target="tpu_custom_call" | custom-call | bytes 8388608 | tf_op jit(solution)/shard_map/bucket/pallas_call | solution.py:30
  19.3 4.0 %all-to-all-done = s32[128,1,2]{2,1,0:T(1,128)S(1)} async-done(((s32[128,1,2]{2,1,0:T(1,128)}), s32[128,1,2]{2,1,0:T(1,128)S(1)}, u32[]{:S(2)}, u32[]{:S(2)}) %all-to-all-start) | async-done | bytes 1056 | tf_op jit(solution)/shard_map/all_to_all | solution.py:399
  23.2 6.3 %all-to-all-start.1 = ((bf16[128,2,128,128]{3,2,1,0:T(8,128)(2,1)}), bf16[128,2,128,128]{3,2,1,0:T(8,128)(2,1)}, u32[]{:S(2)}, u32[]{:S(2)}) async-start(bf16[128,2,128,128]{3,2,1,0:T(8,128)(2,1)} %bitcast.48), calls=%async_computation.1 | async-start | bytes 16777216 | tf_op jit(solution)/shard_map/all_to_all | solution.py:396
  29.5 0.9 fusion.17
  31.1 0.7 pad_add_fusion.code_ref
  31.8 105.8 %all-to-all-done.1 = bf16[128,2,128,128]{3,2,1,0:T(8,128)(2,1)} async-done(((bf16[128,2,128,128]{3,2,1,0:T(8,128)(2,1)}), bf16[128,2,128,128]{3,2,1,0:T(8,128)(2,1)}, u32[]{:S(2)}, u32[]{:S(2)}) %all-to-all-start.1) | async-done | bytes 8388640 | tf_op jit(solution)/shard_map/all_to_all | solution.py:396
  137.6 18.1 %tile_and_sketch.1 = (bf16[512,13312]{1,0:T(8,128)(2,1)}, f32[512,512]{1,0:T(8,128)}) custom-call(s32[257]{0:T(512)S(1)} %pad_add_fusion.code_ref, bf16[256,128,128]{2,1,0:T(8,128)(2,1)} %bitcast.22.got_hbm, bf16[13312,512]{1,0:T(8,128)(2,1)} %omega_hbm.1), custom_call_target="tpu_custom_call" | custom-call | flops 6979321856 | bytes 35651584 | tf_op jit(solution)/shard_map/tile_and_sketch/pallas_call | solution.py:103
  155.8 3.6 %all-to-all-start.2 = ((f32[4,128,512]{2,1,0:T(8,128)}), f32[4,128,512]{2,1,0:T(8,128)S(1)}, u32[]{:S(2)}, u32[]{:S(2)}) async-start(f32[4,128,512]{2,1,0:T(8,128)} %bitcast.23), calls=%async_computation.2 | async-start | bytes 2097152 | tf_op jit(solution)/shard_map/all_to_all | solution.py:421
  159.4 15.9 %all-to-all-done.2.parts_ref = f32[4,128,512]{2,1,0:T(8,128)S(1)} async-done(((f32[4,128,512]{2,1,0:T(8,128)}), f32[4,128,512]{2,1,0:T(8,128)S(1)}, u32[]{:S(2)}, u32[]{:S(2)}) %all-to-all-start.2) | async-done | bytes 1048608 | tf_op jit(solution)/shard_map/all_to_all | solution.py:421
  175.3 0.8 share_and_gram.1
  176.2 1.6 collective-permute-done
  177.9 0.3 copy.9
  178.2 21.1 %all_to_all.29 = f32[64,1,1280]{2,1,0:T(1,128)S(1)} all-to-all(f32[64,1,1280]{2,1,0:T(1,128)S(1)} %copy.9), channel_id=1, replica_groups=mesh['chips'=16,'core'=2,'cols'=4] {'chips','cols'}, dimensions={0} | all-to-all | bytes 655360 | tf_op jit(solution)/shard_map/all_to_all | solution.py:426
  199.6 0.9 broadcast_in_dim.61
  200.5 1.0 collective-permute-start.2
  201.5 1.7 collective-permute-start.3
  203.4 7.1 %all-to-all-start.4 = ((f32[64,1,1280]{2,1,0:T(1,128)}), f32[64,1,1280]{2,1,0:T(1,128)S(1)}, u32[]{:S(2)}, u32[]{:S(2)}) async-start(f32[64,1,1280]{2,1,0:T(1,128)} %broadcast_in_dim.61), calls=%async_computation.4 | async-start | bytes 655360 | tf_op jit(solution)/shard_map/all_to_all | solution.py:430
  210.5 1.7 collective-permute-done.3
  212.3 4.9 %collective-permute-done.4 = f32[128,512]{1,0:T(8,128)S(1)} collective-permute-done((f32[128,512]{1,0:T(8,128)S(1)}, f32[128,512]{1,0:T(8,128)S(1)}, u32[]{:S(2)}, u32[]{:S(2)}) %collective-permute-start.4) | collective-permute-done | bytes 262176 | tf_op jit(solution)/shard_map/ppermute | solution.py:433
  217.3 4.0 %all-to-all-done.4 = f32[64,1,1280]{2,1,0:T(1,128)S(1)} async-done(((f32[64,1,1280]{2,1,0:T(1,128)}), f32[64,1,1280]{2,1,0:T(1,128)S(1)}, u32[]{:S(2)}, u32[]{:S(2)}) %all-to-all-start.4) | async-done | bytes 327712 | tf_op jit(solution)/shard_map/all_to_all | solution.py:430
  221.5 0.8 collective-permute-start.5
  222.2 0.7 collective-permute-done.1.other_ref
  223.0 20.9 %inverse_factor.1.inverse_ref = f32[512,512]{1,0:T(8,128)S(1)} custom-call(s32[1]{0:T(128)} %bitcast.17.core_ref, f32[64,1280]{1,0:T(8,128)S(1)} %bitcast.47, f32[64,1280]{1,0:T(8,128)S(1)} %collective-permute-done.1.other_ref), custom_call_target="tpu_custom_call" | custom-call | flops 34359738368 | bytes 2097152 | tf_op jit(solution)/shard_map/inverse_factor/pallas_call | solution.py:256
  243.9 3.9 %basis_parts.1 = (bf16[256,1024]{1,0:T(8,128)(2,1)S(1)}, bf16[256,1024]{1,0:T(8,128)(2,1)S(1)}, bf16[512,128]{1,0:T(8,128)(2,1)}) custom-call(s32[17]{0:T(128)S(1)} %stack.90.at_ref, f32[512,512]{1,0:T(8,128)S(1)} %inverse_factor.1.inverse_ref, f32[512,512]{1,0:T(8,128)S(1)} %bitcast.45, f32[512,512]{1,0:T(8,128)S(1)} %collective-permute-done.5.other_ref), custom_call_target="tpu_custom_call" | custom-call | flops 2013265920 | bytes 1572864 | tf_op jit(solution)/shard_map/basis_parts/pallas_call | solution.py:311
  247.8 4.4 %product.7 = (bf16[96,3328]{1,0:T(8,128)(2,1)S(1)}, bf16[96,3328]{1,0:T(8,128)(2,1)S(1)}, f32[64,3328]{1,0:T(8,128)S(1)}) custom-call(bf16[256,1024]{1,0:T(8,128)(2,1)S(1)} %get-tuple-element.36.left_ref, bf16[512,13312]{1,0:T(8,128)(2,1)} %get-tuple-element.32.own_ref, bf16[512,13312]{1,0:T(8,128)(2,1)} %collective-permute-done.6.other_ref), custom_call_target="tpu_custom_call" | custom-call | flops 1744830464 | bytes 8519680 | tf_op jit(solution)/shard_map/product/pallas_call | solution.py:354
  252.2 0.7 collective-permute-start.29
  252.9 1.4 collective-permute-start.28
  254.3 4.4 %product.6 = (bf16[96,3328]{1,0:T(8,128)(2,1)S(1)}, bf16[96,3328]{1,0:T(8,128)(2,1)S(1)}, f32[64,3328]{1,0:T(8,128)S(1)}) custom-call(bf16[256,1024]{1,0:T(8,128)(2,1)S(1)} %get-tuple-element.31.left_ref, bf16[512,13312]{1,0:T(8,128)(2,1)} %get-tuple-element.32.own_ref, bf16[512,13312]{1,0:T(8,128)(2,1)} %collective-permute-done.6.other_ref), custom_call_target="tpu_custom_call" | custom-call | flops 1744830464 | bytes 8519680 | tf_op jit(solution)/shard_map/product/pallas_call | solution.py:354
  258.7 1.1 collective-permute-start.22
  259.8 1.0 collective-permute-start.21
  260.8 4.4 %product.5 = (bf16[96,3328]{1,0:T(8,128)(2,1)S(1)}, bf16[96,3328]{1,0:T(8,128)(2,1)S(1)}, f32[64,3328]{1,0:T(8,128)S(1)}) custom-call(bf16[256,1024]{1,0:T(8,128)(2,1)S(1)} %get-tuple-element.36.left_ref, bf16[512,13312]{1,0:T(8,128)(2,1)} %get-tuple-element.32.own_ref, bf16[512,13312]{1,0:T(8,128)(2,1)} %collective-permute-done.6.other_ref), custom_call_target="tpu_custom_call" | custom-call | flops 1744830464 | bytes 8519680 | tf_op jit(solution)/shard_map/product/pallas_call | solution.py:354
  265.2 2.2 collective-permute-start.15
  267.4 4.4 %product.4 = (bf16[96,3328]{1,0:T(8,128)(2,1)S(1)}, bf16[96,3328]{1,0:T(8,128)(2,1)S(1)}, f32[64,3328]{1,0:T(8,128)S(1)}) custom-call(bf16[256,1024]{1,0:T(8,128)(2,1)S(1)} %get-tuple-element.31.left_ref, bf16[512,13312]{1,0:T(8,128)(2,1)} %get-tuple-element.32.own_ref, bf16[512,13312]{1,0:T(8,128)(2,1)} %collective-permute-done.6.other_ref), custom_call_target="tpu_custom_call" | custom-call | flops 1744830464 | bytes 8519680 | tf_op jit(solution)/shard_map/product/pallas_call | solution.py:354
  272.0 2.2 collective-permute-start.8
  274.2 1.7 collective-permute-done.22
  275.9 0.8 collective-permute-start.7
  276.8 1.6 collective-permute-start.31
  278.4 4.8 %collective-permute-done.15 = bf16[96,3328]{1,0:T(8,128)(2,1)S(1)} collective-permute-done((bf16[96,3328]{1,0:T(8,128)(2,1)S(1)}, bf16[96,3328]{1,0:T(8,128)(2,1)S(1)}, u32[]{:S(2)}, u32[]{:S(2)}) %collective-permute-start.15) | collective-permute-done | bytes 639008 | tf_op jit(solution)/shard_map/ppermute | solution.py:466
  283.2 0.6 collective-permute-start.30
  283.8 6.5 %collective-permute-done.14 = bf16[96,3328]{1,0:T(8,128)(2,1)S(1)} collective-permute-done((bf16[96,3328]{1,0:T(8,128)(2,1)S(1)}, bf16[96,3328]{1,0:T(8,128)(2,1)S(1)}, u32[]{:S(2)}, u32[]{:S(2)}) %collective-permute-start.14) | collective-permute-done | bytes 639008 | tf_op jit(solution)/shard_map/ppermute | solution.py:466
  290.4 2.1 collective-permute-start.24
  292.6 1.2 collective-permute-start.17
  293.8 1.0 collective-permute-start.16
  294.8 3.2 collective-permute-start.10
  298.5 0.5 collective-permute-start.9
  299.0 4.1 %collective-permute-done.23 = bf16[32,3328]{1,0:T(8,128)(2,1)S(1)} collective-permute-done((bf16[32,3328]{1,0:T(8,128)(2,1)S(1)}, bf16[32,3328]{1,0:T(8,128)(2,1)S(1)}, u32[]{:S(2)}, u32[]{:S(2)}) %collective-permute-start.23) | collective-permute-done | bytes 213024 | tf_op jit(solution)/shard_map/ppermute | solution.py:467
  303.3 0.4 collective-permute-start.33
  303.7 1.8 collective-permute-start.32
  305.8 0.9 collective-permute-start.26
  306.9 1.3 collective-permute-done.34
  308.2 2.5 collective-permute-done.33
  310.7 1.5 collective-permute-start.20
  312.2 1.4 collective-permute-start.19
  313.8 2.7 collective-permute-start.13
  316.5 1.4 collective-permute-start.12
  318.0 1.4 collective-permute-start.11
  319.4 0.3 collective-permute-done.18
  319.8 3.0 collective-permute-done.12
  322.8 1.2 collective-permute-done.11
  324.1 1.0 pad_maximum_fusion
  (76 shorter events, 3.7 us)
Async XLA Ops:
  2.2 12.0 %copy-start = (s32[128]{0:T(128)}, s32[128]{0:T(128)S(1)}, u32[]{:S(2)}) copy-start(s32[128]{0:T(128)S(1)} %get-tuple-element.68.place_ref) | copy-start | bytes 1540
  3.1 20.1 %all-to-all-start = ((s32[128,1,2]{2,1,0:T(1,128)}), s32[128,1,2]{2,1,0:T(1,128)S(1)}, u32[]{:S(2)}, u32[]{:S(2)}) async-start(s32[128,1,2]{2,1,0:T(1,128)} %bitcast.19), calls=%async_computation | async-start | bytes 131072 | tf_op jit(solution)/shard_map/all_to_all | solution.py:399
  23.2 114.3 %all-to-all-start.1 = ((bf16[128,2,128,128]{3,2,1,0:T(8,128)(2,1)}), bf16[128,2,128,128]{3,2,1,0:T(8,128)(2,1)}, u32[]{:S(2)}, u32[]{:S(2)}) async-start(bf16[128,2,128,128]{3,2,1,0:T(8,128)(2,1)} %bitcast.48), calls=%async_computation.1 | async-start | bytes 16777216 | tf_op jit(solution)/shard_map/all_to_all | solution.py:396
  155.7 92.1 %collective-permute-start.6 = (bf16[512,13312]{1,0:T(8,128)(2,1)}, bf16[512,13312]{1,0:T(8,128)(2,1)}, u32[]{:S(2)}, u32[]{:S(2)}) collective-permute-start(bf16[512,13312]{1,0:T(8,128)(2,1)} %get-tuple-element.32.own_ref), channel_id=1, source_target_pairs={{0,4},{4,0},{1,5},{5,1},{2,6},{6,2},{3,7},{7,3},{8,12},{12,8},{9,1... | collective-permute-start | bytes 40894472 | tf_op jit(solution)/shard_map/ppermute | solution.py:418
  155.8 19.5 %all-to-all-start.2 = ((f32[4,128,512]{2,1,0:T(8,128)}), f32[4,128,512]{2,1,0:T(8,128)S(1)}, u32[]{:S(2)}, u32[]{:S(2)}) async-start(f32[4,128,512]{2,1,0:T(8,128)} %bitcast.23), calls=%async_computation.2 | async-start | bytes 2097152 | tf_op jit(solution)/shard_map/all_to_all | solution.py:421
  176.1 1.7 collective-permute-start
  200.5 10.0 %collective-permute-start.2 = (f32[128,512]{1,0:T(8,128)S(1)}, f32[128,512]{1,0:T(8,128)S(1)}, u32[]{:S(2)}, u32[]{:S(2)}) collective-permute-start(f32[128,512]{1,0:T(8,128)S(1)} %get-tuple-element.29), channel_id=1, source_target_pairs={{0,3},{1,0},{2,1},{3,2},{4,7},{5,4},{6,5},{7,6},{8,11},{9,8},{10,9... | collective-permute-start | bytes 786440 | tf_op jit(solution)/shard_map/ppermute | solution.py:433
  201.5 10.8 %collective-permute-start.3 = (f32[128,512]{1,0:T(8,128)S(1)}, f32[128,512]{1,0:T(8,128)S(1)}, u32[]{:S(2)}, u32[]{:S(2)}) collective-permute-start(f32[128,512]{1,0:T(8,128)S(1)} %get-tuple-element.29), channel_id=1, source_target_pairs={{0,2},{1,3},{2,0},{3,1},{4,6},{5,7},{6,4},{7,5},{8,10},{9,11},{10,... | collective-permute-start | bytes 786440 | tf_op jit(solution)/shard_map/ppermute | solution.py:433
  203.2 13.9 %collective-permute-start.4 = (f32[128,512]{1,0:T(8,128)S(1)}, f32[128,512]{1,0:T(8,128)S(1)}, u32[]{:S(2)}, u32[]{:S(2)}) collective-permute-start(f32[128,512]{1,0:T(8,128)S(1)} %get-tuple-element.29), channel_id=1, source_target_pairs={{0,1},{1,2},{2,3},{3,0},{4,5},{5,6},{6,7},{7,4},{8,9},{9,10},{10,1... | collective-permute-start | bytes 786440 | tf_op jit(solution)/shard_map/ppermute | solution.py:433
  203.4 17.9 %all-to-all-start.4 = ((f32[64,1,1280]{2,1,0:T(1,128)}), f32[64,1,1280]{2,1,0:T(1,128)S(1)}, u32[]{:S(2)}, u32[]{:S(2)}) async-start(f32[64,1,1280]{2,1,0:T(1,128)} %broadcast_in_dim.61), calls=%async_computation.4 | async-start | bytes 655360 | tf_op jit(solution)/shard_map/all_to_all | solution.py:430
  221.3 1.7 collective-permute-start.1
  221.5 22.4 %collective-permute-start.5 = (f32[512,512]{1,0:T(8,128)S(1)}, f32[512,512]{1,0:T(8,128)S(1)}, u32[]{:S(2)}, u32[]{:S(2)}) collective-permute-start(f32[512,512]{1,0:T(8,128)S(1)} %bitcast.44), channel_id=1, source_target_pairs={{0,4},{4,0},{1,5},{5,1},{2,6},{6,2},{3,7},{7,3},{8,12},{12,8},{9,1... | collective-permute-start | bytes 3145736 | tf_op jit(solution)/shard_map/ppermute | solution.py:439
  252.2 19.6 %collective-permute-start.29 = (bf16[96,3328]{1,0:T(8,128)(2,1)S(1)}, bf16[96,3328]{1,0:T(8,128)(2,1)S(1)}, u32[]{:S(2)}, u32[]{:S(2)}) collective-permute-start(bf16[96,3328]{1,0:T(8,128)(2,1)S(1)} %get-tuple-element.45), channel_id=1, source_target_pairs={{0,24},{8,0},{16,8},{24,16},{32,56},{40,32},{48,40},{56,48},{64,88... | collective-permute-start | bytes 1916936 | tf_op jit(solution)/shard_map/ppermute | solution.py:466
  252.9 19.1 %collective-permute-start.28 = (bf16[96,3328]{1,0:T(8,128)(2,1)S(1)}, bf16[96,3328]{1,0:T(8,128)(2,1)S(1)}, u32[]{:S(2)}, u32[]{:S(2)}) collective-permute-start(bf16[96,3328]{1,0:T(8,128)(2,1)S(1)} %get-tuple-element.44), channel_id=1, source_target_pairs={{0,8},{8,16},{16,24},{24,0},{32,40},{40,48},{48,56},{56,32},{64,72... | collective-permute-start | bytes 1916936 | tf_op jit(solution)/shard_map/ppermute | solution.py:466
  258.7 17.2 %collective-permute-start.22 = (bf16[96,3328]{1,0:T(8,128)(2,1)S(1)}, bf16[96,3328]{1,0:T(8,128)(2,1)S(1)}, u32[]{:S(2)}, u32[]{:S(2)}) collective-permute-start(bf16[96,3328]{1,0:T(8,128)(2,1)S(1)} %get-tuple-element.42), channel_id=1, source_target_pairs={{0,96},{8,104},{16,112},{24,120},{32,0},{40,8},{48,16},{56,24},{64... | collective-permute-start | bytes 1916936 | tf_op jit(solution)/shard_map/ppermute | solution.py:466
  259.8 17.0 %collective-permute-start.21 = (bf16[96,3328]{1,0:T(8,128)(2,1)S(1)}, bf16[96,3328]{1,0:T(8,128)(2,1)S(1)}, u32[]{:S(2)}, u32[]{:S(2)}) collective-permute-start(bf16[96,3328]{1,0:T(8,128)(2,1)S(1)} %get-tuple-element.41), channel_id=1, source_target_pairs={{0,32},{8,40},{16,48},{24,56},{32,64},{40,72},{48,80},{56,88},{64,... | collective-permute-start | bytes 1916936 | tf_op jit(solution)/shard_map/ppermute | solution.py:466
  265.2 18.0 %collective-permute-start.15 = (bf16[96,3328]{1,0:T(8,128)(2,1)S(1)}, bf16[96,3328]{1,0:T(8,128)(2,1)S(1)}, u32[]{:S(2)}, u32[]{:S(2)}) collective-permute-start(bf16[96,3328]{1,0:T(8,128)(2,1)S(1)} %get-tuple-element.39), channel_id=1, source_target_pairs={{0,24},{8,0},{16,8},{24,16},{32,56},{40,32},{48,40},{56,48},{64,88... | collective-permute-start | bytes 1916936 | tf_op jit(solution)/shard_map/ppermute | solution.py:466
  271.8 18.6 %collective-permute-start.14 = (bf16[96,3328]{1,0:T(8,128)(2,1)S(1)}, bf16[96,3328]{1,0:T(8,128)(2,1)S(1)}, u32[]{:S(2)}, u32[]{:S(2)}) collective-permute-start(bf16[96,3328]{1,0:T(8,128)(2,1)S(1)} %get-tuple-element.38), channel_id=1, source_target_pairs={{0,8},{8,16},{16,24},{24,0},{32,40},{40,48},{48,56},{56,32},{64,72... | collective-permute-start | bytes 1916936 | tf_op jit(solution)/shard_map/ppermute | solution.py:466
  272.0 20.5 %collective-permute-start.8 = (bf16[96,3328]{1,0:T(8,128)(2,1)S(1)}, bf16[96,3328]{1,0:T(8,128)(2,1)S(1)}, u32[]{:S(2)}, u32[]{:S(2)}) collective-permute-start(bf16[96,3328]{1,0:T(8,128)(2,1)S(1)} %get-tuple-element.35), channel_id=1, source_target_pairs={{0,96},{8,104},{16,112},{24,120},{32,0},{40,8},{48,16},{56,24},{64... | collective-permute-start | bytes 1916936 | tf_op jit(solution)/shard_map/ppermute | solution.py:466
  275.9 16.7 %collective-permute-start.7 = (bf16[96,3328]{1,0:T(8,128)(2,1)S(1)}, bf16[96,3328]{1,0:T(8,128)(2,1)S(1)}, u32[]{:S(2)}, u32[]{:S(2)}) collective-permute-start(bf16[96,3328]{1,0:T(8,128)(2,1)S(1)} %get-tuple-element.34), channel_id=1, source_target_pairs={{0,32},{8,40},{16,48},{24,56},{32,64},{40,72},{48,80},{56,88},{64,... | collective-permute-start | bytes 1916936 | tf_op jit(solution)/shard_map/ppermute | solution.py:466
  276.8 17.1 %collective-permute-start.31 = (bf16[32,3328]{1,0:T(8,128)(2,1)S(1)}, bf16[32,3328]{1,0:T(8,128)(2,1)S(1)}, u32[]{:S(2)}, u32[]{:S(2)}) collective-permute-start(bf16[32,3328]{1,0:T(8,128)(2,1)S(1)} %slice.179), channel_id=1, source_target_pairs={{0,24},{8,0},{16,8},{24,16},{32,56},{40,32},{48,40},{56,48},{64,88... | collective-permute-start | bytes 638984 | tf_op jit(solution)/shard_map/ppermute | solution.py:467
  283.2 11.7 %collective-permute-start.30 = (bf16[32,3328]{1,0:T(8,128)(2,1)S(1)}, bf16[32,3328]{1,0:T(8,128)(2,1)S(1)}, u32[]{:S(2)}, u32[]{:S(2)}) collective-permute-start(bf16[32,3328]{1,0:T(8,128)(2,1)S(1)} %slice.178), channel_id=1, source_target_pairs={{0,8},{8,16},{16,24},{24,0},{32,40},{40,48},{48,56},{56,32},{64,72... | collective-permute-start | bytes 638984 | tf_op jit(solution)/shard_map/ppermute | solution.py:467
  290.4 8.1 %collective-permute-start.24 = (bf16[32,3328]{1,0:T(8,128)(2,1)S(1)}, bf16[32,3328]{1,0:T(8,128)(2,1)S(1)}, u32[]{:S(2)}, u32[]{:S(2)}) collective-permute-start(bf16[32,3328]{1,0:T(8,128)(2,1)S(1)} %slice.171), channel_id=1, source_target_pairs={{0,96},{8,104},{16,112},{24,120},{32,0},{40,8},{48,16},{56,24},{64... | collective-permute-start | bytes 638984 | tf_op jit(solution)/shard_map/ppermute | solution.py:467
  292.5 10.5 %collective-permute-start.23 = (bf16[32,3328]{1,0:T(8,128)(2,1)S(1)}, bf16[32,3328]{1,0:T(8,128)(2,1)S(1)}, u32[]{:S(2)}, u32[]{:S(2)}) collective-permute-start(bf16[32,3328]{1,0:T(8,128)(2,1)S(1)} %slice.170), channel_id=1, source_target_pairs={{0,32},{8,40},{16,48},{24,56},{32,64},{40,72},{48,80},{56,88},{64,... | collective-permute-start | bytes 638984 | tf_op jit(solution)/shard_map/ppermute | solution.py:467
  292.6 10.6 %collective-permute-start.17 = (bf16[32,3328]{1,0:T(8,128)(2,1)S(1)}, bf16[32,3328]{1,0:T(8,128)(2,1)S(1)}, u32[]{:S(2)}, u32[]{:S(2)}) collective-permute-start(bf16[32,3328]{1,0:T(8,128)(2,1)S(1)} %slice.163), channel_id=1, source_target_pairs={{0,24},{8,0},{16,8},{24,16},{32,56},{40,32},{48,40},{56,48},{64,88... | collective-permute-start | bytes 638984 | tf_op jit(solution)/shard_map/ppermute | solution.py:467
  293.8 9.8 %collective-permute-start.16 = (bf16[32,3328]{1,0:T(8,128)(2,1)S(1)}, bf16[32,3328]{1,0:T(8,128)(2,1)S(1)}, u32[]{:S(2)}, u32[]{:S(2)}) collective-permute-start(bf16[32,3328]{1,0:T(8,128)(2,1)S(1)} %slice.162), channel_id=1, source_target_pairs={{0,8},{8,16},{16,24},{24,0},{32,40},{40,48},{48,56},{56,32},{64,72... | collective-permute-start | bytes 638984 | tf_op jit(solution)/shard_map/ppermute | solution.py:467
  294.8 10.9 %collective-permute-start.10 = (bf16[32,3328]{1,0:T(8,128)(2,1)S(1)}, bf16[32,3328]{1,0:T(8,128)(2,1)S(1)}, u32[]{:S(2)}, u32[]{:S(2)}) collective-permute-start(bf16[32,3328]{1,0:T(8,128)(2,1)S(1)} %slice.155), channel_id=1, source_target_pairs={{0,96},{8,104},{16,112},{24,120},{32,0},{40,8},{48,16},{56,24},{64... | collective-permute-start | bytes 638984 | tf_op jit(solution)/shard_map/ppermute | solution.py:467
  298.5 7.3 %collective-permute-start.9 = (bf16[32,3328]{1,0:T(8,128)(2,1)S(1)}, bf16[32,3328]{1,0:T(8,128)(2,1)S(1)}, u32[]{:S(2)}, u32[]{:S(2)}) collective-permute-start(bf16[32,3328]{1,0:T(8,128)(2,1)S(1)} %slice.154), channel_id=1, source_target_pairs={{0,32},{8,40},{16,48},{24,56},{32,64},{40,72},{48,80},{56,88},{64,... | collective-permute-start | bytes 638984 | tf_op jit(solution)/shard_map/ppermute | solution.py:467
  303.1 5.1 %collective-permute-start.34 = (bf16[16,3328]{1,0:T(8,128)(2,1)S(1)}, bf16[16,3328]{1,0:T(8,128)(2,1)S(1)}, u32[]{:S(2)}, u32[]{:S(2)}) collective-permute-start(bf16[16,3328]{1,0:T(8,128)(2,1)S(1)} %get-tuple-element.66), channel_id=1, source_target_pairs={{0,96},{8,104},{16,112},{24,120},{32,0},{40,8},{48,16},{56,24},{64... | collective-permute-start | bytes 319496 | tf_op jit(solution)/shard_map/ppermute | solution.py:473
  303.3 7.4 %collective-permute-start.33 = (bf16[16,3328]{1,0:T(8,128)(2,1)S(1)}, bf16[16,3328]{1,0:T(8,128)(2,1)S(1)}, u32[]{:S(2)}, u32[]{:S(2)}) collective-permute-start(bf16[16,3328]{1,0:T(8,128)(2,1)S(1)} %get-tuple-element.67), channel_id=1, source_target_pairs={{0,64},{8,72},{16,80},{24,88},{32,96},{40,104},{48,112},{56,120},{... | collective-permute-start | bytes 319496 | tf_op jit(solution)/shard_map/ppermute | solution.py:473
  303.7 8.6 %collective-permute-start.32 = (bf16[16,3328]{1,0:T(8,128)(2,1)S(1)}, bf16[16,3328]{1,0:T(8,128)(2,1)S(1)}, u32[]{:S(2)}, u32[]{:S(2)}) collective-permute-start(bf16[16,3328]{1,0:T(8,128)(2,1)S(1)} %get-tuple-element.65), channel_id=1, source_target_pairs={{0,32},{8,40},{16,48},{24,56},{32,64},{40,72},{48,80},{56,88},{64,... | collective-permute-start | bytes 319496 | tf_op jit(solution)/shard_map/ppermute | solution.py:473
  305.7 8.0 %collective-permute-start.27 = (bf16[16,3328]{1,0:T(8,128)(2,1)S(1)}, bf16[16,3328]{1,0:T(8,128)(2,1)S(1)}, u32[]{:S(2)}, u32[]{:S(2)}) collective-permute-start(bf16[16,3328]{1,0:T(8,128)(2,1)S(1)} %get-tuple-element.63), channel_id=1, source_target_pairs={{0,24},{8,0},{16,8},{24,16},{32,56},{40,32},{48,40},{56,48},{64,88... | collective-permute-start | bytes 319496 | tf_op jit(solution)/shard_map/ppermute | solution.py:473
  305.8 8.0 %collective-permute-start.26 = (bf16[16,3328]{1,0:T(8,128)(2,1)S(1)}, bf16[16,3328]{1,0:T(8,128)(2,1)S(1)}, u32[]{:S(2)}, u32[]{:S(2)}) collective-permute-start(bf16[16,3328]{1,0:T(8,128)(2,1)S(1)} %get-tuple-element.64), channel_id=1, source_target_pairs={{0,16},{8,24},{16,0},{24,8},{32,48},{40,56},{48,32},{56,40},{64,80... | collective-permute-start | bytes 319496 | tf_op jit(solution)/shard_map/ppermute | solution.py:473
  308.2 8.3 %collective-permute-start.25 = (bf16[16,3328]{1,0:T(8,128)(2,1)S(1)}, bf16[16,3328]{1,0:T(8,128)(2,1)S(1)}, u32[]{:S(2)}, u32[]{:S(2)}) collective-permute-start(bf16[16,3328]{1,0:T(8,128)(2,1)S(1)} %get-tuple-element.62), channel_id=1, source_target_pairs={{0,8},{8,16},{16,24},{24,0},{32,40},{40,48},{48,56},{56,32},{64,72... | collective-permute-start | bytes 319496 | tf_op jit(solution)/shard_map/ppermute | solution.py:473
  310.7 7.3 %collective-permute-start.20 = (bf16[16,3328]{1,0:T(8,128)(2,1)S(1)}, bf16[16,3328]{1,0:T(8,128)(2,1)S(1)}, u32[]{:S(2)}, u32[]{:S(2)}) collective-permute-start(bf16[16,3328]{1,0:T(8,128)(2,1)S(1)} %get-tuple-element.60), channel_id=1, source_target_pairs={{0,96},{8,104},{16,112},{24,120},{32,0},{40,8},{48,16},{56,24},{64... | collective-permute-start | bytes 319496 | tf_op jit(solution)/shard_map/ppermute | solution.py:473
  312.2 7.2 %collective-permute-start.19 = (bf16[16,3328]{1,0:T(8,128)(2,1)S(1)}, bf16[16,3328]{1,0:T(8,128)(2,1)S(1)}, u32[]{:S(2)}, u32[]{:S(2)}) collective-permute-start(bf16[16,3328]{1,0:T(8,128)(2,1)S(1)} %get-tuple-element.61), channel_id=1, source_target_pairs={{0,64},{8,72},{16,80},{24,88},{32,96},{40,104},{48,112},{56,120},{... | collective-permute-start | bytes 319496 | tf_op jit(solution)/shard_map/ppermute | solution.py:473
  313.7 6.0 %collective-permute-start.18 = (bf16[16,3328]{1,0:T(8,128)(2,1)S(1)}, bf16[16,3328]{1,0:T(8,128)(2,1)S(1)}, u32[]{:S(2)}, u32[]{:S(2)}) collective-permute-start(bf16[16,3328]{1,0:T(8,128)(2,1)S(1)} %get-tuple-element.59), channel_id=1, source_target_pairs={{0,32},{8,40},{16,48},{24,56},{32,64},{40,72},{48,80},{56,88},{64,... | collective-permute-start | bytes 319496 | tf_op jit(solution)/shard_map/ppermute | solution.py:473
  313.8 5.9 %collective-permute-start.13 = (bf16[16,3328]{1,0:T(8,128)(2,1)S(1)}, bf16[16,3328]{1,0:T(8,128)(2,1)S(1)}, u32[]{:S(2)}, u32[]{:S(2)}) collective-permute-start(bf16[16,3328]{1,0:T(8,128)(2,1)S(1)} %get-tuple-element.57), channel_id=1, source_target_pairs={{0,24},{8,0},{16,8},{24,16},{32,56},{40,32},{48,40},{56,48},{64,88... | collective-permute-start | bytes 319496 | tf_op jit(solution)/shard_map/ppermute | solution.py:473
  316.5 6.2 %collective-permute-start.12 = (bf16[16,3328]{1,0:T(8,128)(2,1)S(1)}, bf16[16,3328]{1,0:T(8,128)(2,1)S(1)}, u32[]{:S(2)}, u32[]{:S(2)}) collective-permute-start(bf16[16,3328]{1,0:T(8,128)(2,1)S(1)} %get-tuple-element.58), channel_id=1, source_target_pairs={{0,16},{8,24},{16,0},{24,8},{32,48},{40,56},{48,32},{56,40},{64,80... | collective-permute-start | bytes 319496 | tf_op jit(solution)/shard_map/ppermute | solution.py:473
  318.0 6.0 %collective-permute-start.11 = (bf16[16,3328]{1,0:T(8,128)(2,1)S(1)}, bf16[16,3328]{1,0:T(8,128)(2,1)S(1)}, u32[]{:S(2)}, u32[]{:S(2)}) collective-permute-start(bf16[16,3328]{1,0:T(8,128)(2,1)S(1)} %get-tuple-element.56), channel_id=1, source_target_pairs={{0,8},{8,16},{16,24},{24,0},{32,40},{40,48},{48,56},{56,32},{64,72... | collective-permute-start | bytes 319496 | tf_op jit(solution)/shard_map/ppermute | solution.py:473

commit v10 on v9

--- a/solution.py
+++ b/solution.py
@@ -461,12 +461,16 @@
     def multiply(first, count, factor):
         return product(factor, tile, other_tile, first, count // 2, 2, 1.0 / math.sqrt(total_rows))
 
-    def scatter(ahead, behind, total, x_first):
+    def first_axis(ahead, behind, total, x_first):
         forward, backward = shift(x_first, 1), shift(x_first, -1)
         ahead, behind = forward(ahead), backward(behind)
         far, back_far = forward(ahead[: FAR * ranks]), backward(behind[: FAR * ranks])
         total += ahead[FAR * ranks :].astype(jnp.float32) + behind[FAR * ranks :].astype(jnp.float32)
         total += jnp.concatenate([far, back_far], axis=0).astype(jnp.float32)
+        return total
+
+    def second_axis(totals, x_first):
+        total = jnp.concatenate(totals, axis=1)
         terms = [total[i * ranks : (i + 1) * ranks] for i in range(along)]
         result = terms[0]
         for i in range(1, along):
@@ -474,12 +478,13 @@
         return result
 
     quarter = cols // 4
+    totals = [None] * 4
+    for i in (0, 2, 1, 3):
+        x_first = i < 2
+        parts = multiply(i * quarter, quarter, left if x_first else turned)
+        totals[i] = first_axis(*parts, x_first)
     coefficients = jnp.concatenate(
-        [
-            scatter(*multiply(i * quarter, quarter, (left, turned)[i % 2]), i % 2 == 0)
-            for i in range(4)
-        ],
-        axis=1,
+        [second_axis(totals[:2], True), second_axis(totals[2:], False)], axis=1
     )
     return basis, coefficients
 

time: 325 us -> 329 us (1.012)
  waiting for transfers between devices: 164 us -> 172 us
    ppermute x28 -> x22, waiting for transfers between devices: 25.7 us -> 33.4 us  [the longest x8 20.7 us: first_axis(): ahead, behind = (forward(ahead), backward(behind))]
    ppermute x28 -> x22, starting transfers between devices: 31.6 us -> 29.5 us  [the longest x4 10.4 us: first_axis(): backward(behind[:FAR * ranks])]
  transfers between devices with their start and end apart: 39 -> 33, of which waited for: 18 -> 18; matrix products, arithmetic and copies ran while one was open for 2% -> 2% of each run, Pallas kernels for 13% -> 13%
where the time goes in v10:
time: 329 us; the launch traced here: 328 us
  waiting for transfers between devices  172 us (52%)
  Pallas kernels  66.3 us (20%)
  starting transfers between devices  61.5 us (19%)
  blocking collectives  18 us (5%)
  other arithmetic  6.09 us (2%)
    all_to_all x1, waiting for transfers between devices, on_device(): lax.all_to_all(send_blocks.reshape(devices_all, capacity, BLK, BLK), ever...  106 us
    pallas_call x1, Pallas kernels, inverse_factor(): pl.pallas_call(functools.partial(factor_kernel, scale), grid_spec=pltpu.P...  20.9 us
    ppermute x8, waiting for transfers between devices, first_axis(): ahead, behind = (forward(ahead), backward(behind))  20.7 us
    pallas_call x1, Pallas kernels, tile_and_sketch(): pl.pallas_call(tile_kernel, grid_spec=pltpu.PrefetchScalarGridSpec(num_sc...  18.1 us
    all_to_all x1, blocking collectives, on_device(): lax.all_to_all((keep + swap(send)).reshape(gram_rows), same_core, 0, 0, t...  18 us
    pallas_call x4, Pallas kernels, product(): pl.pallas_call(functools.partial(product_kernel, scale), grid=(steps,), i...  17.6 us
    all_to_all x1, waiting for transfers between devices, on_device(): lax.all_to_all(part.reshape(col_devices, share, rank), 'cols', 0, 0, tile...  16 us
    all_to_all x1, starting transfers between devices, on_device(): lax.all_to_all(send_where.reshape(devices_all, capacity), everywhere, 0,...  11.1 us
  transfers between devices with their start and end apart: 33, of which 18 were waited for; matrix products, arithmetic and copies ran while one was open for 2% of the time, Pallas kernels for 13%

profile of v10, /device:TPU:0, one launch (start us, length us, event | category | flops | bytes accessed | tf_op | source)
XLA Modules:
  0.0 327.6 jit_solution(6759653809135856310)
XLA Ops:
  0.6 0.9 convert_reduce_fusion.1
  1.5 0.7 multiply_add_fusion
  2.3 0.8 all_to_all.18
  3.1 11.1 %all-to-all-start = ((s32[128,1,2]{2,1,0:T(1,128)}), s32[128,1,2]{2,1,0:T(1,128)S(1)}, u32[]{:S(2)}, u32[]{:S(2)}) async-start(s32[128,1,2]{2,1,0:T(1,128)} %bitcast.19), calls=%async_computation | async-start | bytes 131072 | tf_op jit(solution)/shard_map/all_to_all | solution.py:399
  14.3 5.0 %bucket.1 = bf16[256,128,128]{2,1,0:T(8,128)(2,1)} custom-call(s32[128]{0:T(128)} %copy-done, bf16[128,128,128]{2,1,0:T(8,128)(2,1)} %blocks_ref.1), custom_call_target="tpu_custom_call" | custom-call | bytes 8388608 | tf_op jit(solution)/shard_map/bucket/pallas_call | solution.py:30
  19.3 4.0 %all-to-all-done = s32[128,1,2]{2,1,0:T(1,128)S(1)} async-done(((s32[128,1,2]{2,1,0:T(1,128)}), s32[128,1,2]{2,1,0:T(1,128)S(1)}, u32[]{:S(2)}, u32[]{:S(2)}) %all-to-all-start) | async-done | bytes 1056 | tf_op jit(solution)/shard_map/all_to_all | solution.py:399
  23.2 6.3 %all-to-all-start.1 = ((bf16[128,2,128,128]{3,2,1,0:T(8,128)(2,1)}), bf16[128,2,128,128]{3,2,1,0:T(8,128)(2,1)}, u32[]{:S(2)}, u32[]{:S(2)}) async-start(bf16[128,2,128,128]{3,2,1,0:T(8,128)(2,1)} %bitcast.48), calls=%async_computation.1 | async-start | bytes 16777216 | tf_op jit(solution)/shard_map/all_to_all | solution.py:396
  29.6 0.9 fusion.19
  30.7 0.2 convert_reduce_fusion
  31.2 0.7 pad_add_fusion.code_ref
  31.9 105.8 %all-to-all-done.1 = bf16[128,2,128,128]{3,2,1,0:T(8,128)(2,1)} async-done(((bf16[128,2,128,128]{3,2,1,0:T(8,128)(2,1)}), bf16[128,2,128,128]{3,2,1,0:T(8,128)(2,1)}, u32[]{:S(2)}, u32[]{:S(2)}) %all-to-all-start.1) | async-done | bytes 8388640 | tf_op jit(solution)/shard_map/all_to_all | solution.py:396
  137.7 18.1 %tile_and_sketch.1 = (bf16[512,13312]{1,0:T(8,128)(2,1)}, f32[512,512]{1,0:T(8,128)}) custom-call(s32[257]{0:T(512)S(1)} %pad_add_fusion.code_ref, bf16[256,128,128]{2,1,0:T(8,128)(2,1)} %bitcast.22.got_hbm, bf16[13312,512]{1,0:T(8,128)(2,1)} %omega_hbm.1), custom_call_target="tpu_custom_call" | custom-call | flops 6979321856 | bytes 35651584 | tf_op jit(solution)/shard_map/tile_and_sketch/pallas_call | solution.py:103
  155.9 3.5 %all-to-all-start.2 = ((f32[4,128,512]{2,1,0:T(8,128)}), f32[4,128,512]{2,1,0:T(8,128)S(1)}, u32[]{:S(2)}, u32[]{:S(2)}) async-start(f32[4,128,512]{2,1,0:T(8,128)} %bitcast.23), calls=%async_computation.2 | async-start | bytes 2097152 | tf_op jit(solution)/shard_map/all_to_all | solution.py:421
  159.4 16.0 %all-to-all-done.2.parts_ref = f32[4,128,512]{2,1,0:T(8,128)S(1)} async-done(((f32[4,128,512]{2,1,0:T(8,128)}), f32[4,128,512]{2,1,0:T(8,128)S(1)}, u32[]{:S(2)}, u32[]{:S(2)}) %all-to-all-start.2) | async-done | bytes 1048608 | tf_op jit(solution)/shard_map/all_to_all | solution.py:421
  175.4 0.8 share_and_gram.1
  176.3 1.6 collective-permute-done
  177.9 0.3 copy.9
  178.3 18.0 %all_to_all.29 = f32[64,1,1280]{2,1,0:T(1,128)S(1)} all-to-all(f32[64,1,1280]{2,1,0:T(1,128)S(1)} %copy.9), channel_id=1, replica_groups=mesh['chips'=16,'core'=2,'cols'=4] {'chips','cols'}, dimensions={0} | all-to-all | bytes 655360 | tf_op jit(solution)/shard_map/all_to_all | solution.py:426
  196.3 0.2 reduce_sum.59
  196.5 0.9 broadcast_in_dim.61
  197.4 1.0 collective-permute-start.2
  198.4 1.7 collective-permute-start.3
  200.3 7.1 %all-to-all-start.4 = ((f32[64,1,1280]{2,1,0:T(1,128)}), f32[64,1,1280]{2,1,0:T(1,128)S(1)}, u32[]{:S(2)}, u32[]{:S(2)}) async-start(f32[64,1,1280]{2,1,0:T(1,128)} %broadcast_in_dim.61), calls=%async_computation.4 | async-start | bytes 655360 | tf_op jit(solution)/shard_map/all_to_all | solution.py:430
  207.5 1.7 collective-permute-done.3
  209.2 4.9 %collective-permute-done.4 = f32[128,512]{1,0:T(8,128)S(1)} collective-permute-done((f32[128,512]{1,0:T(8,128)S(1)}, f32[128,512]{1,0:T(8,128)S(1)}, u32[]{:S(2)}, u32[]{:S(2)}) %collective-permute-start.4) | collective-permute-done | bytes 262176 | tf_op jit(solution)/shard_map/ppermute | solution.py:433
  214.2 4.0 %all-to-all-done.4 = f32[64,1,1280]{2,1,0:T(1,128)S(1)} async-done(((f32[64,1,1280]{2,1,0:T(1,128)}), f32[64,1,1280]{2,1,0:T(1,128)S(1)}, u32[]{:S(2)}, u32[]{:S(2)}) %all-to-all-start.4) | async-done | bytes 327712 | tf_op jit(solution)/shard_map/all_to_all | solution.py:430
  218.4 0.8 collective-permute-start.5
  219.2 0.7 collective-permute-done.1.other_ref
  219.9 20.9 %inverse_factor.1.inverse_ref = f32[512,512]{1,0:T(8,128)S(1)} custom-call(s32[1]{0:T(128)} %bitcast.17.core_ref, f32[64,1280]{1,0:T(8,128)S(1)} %bitcast.47, f32[64,1280]{1,0:T(8,128)S(1)} %collective-permute-done.1.other_ref), custom_call_target="tpu_custom_call" | custom-call | flops 34359738368 | bytes 2097152 | tf_op jit(solution)/shard_map/inverse_factor/pallas_call | solution.py:256
  240.8 3.9 %basis_parts.1 = (bf16[256,1024]{1,0:T(8,128)(2,1)S(1)}, bf16[256,1024]{1,0:T(8,128)(2,1)S(1)}, bf16[512,128]{1,0:T(8,128)(2,1)}) custom-call(s32[17]{0:T(128)S(1)} %stack.90.at_ref, f32[512,512]{1,0:T(8,128)S(1)} %inverse_factor.1.inverse_ref, f32[512,512]{1,0:T(8,128)S(1)} %bitcast.45, f32[512,512]{1,0:T(8,128)S(1)} %collective-permute-done.5.other_ref), custom_call_target="tpu_custom_call" | custom-call | flops 2013265920 | bytes 1572864 | tf_op jit(solution)/shard_map/basis_parts/pallas_call | solution.py:311
  244.7 4.4 %product.5 = (bf16[96,3328]{1,0:T(8,128)(2,1)S(1)}, bf16[96,3328]{1,0:T(8,128)(2,1)S(1)}, f32[64,3328]{1,0:T(8,128)S(1)}) custom-call(bf16[256,1024]{1,0:T(8,128)(2,1)S(1)} %get-tuple-element.31.left_ref, bf16[512,13312]{1,0:T(8,128)(2,1)} %get-tuple-element.32.own_ref, bf16[512,13312]{1,0:T(8,128)(2,1)} %collective-permute-done.6.other_ref), custom_call_target="tpu_custom_call" | custom-call | flops 1744830464 | bytes 8519680 | tf_op jit(solution)/shard_map/product/pallas_call | solution.py:354
  249.1 0.7 collective-permute-start.11
  249.9 2.6 collective-permute-start.12
  252.5 4.4 %product.4 = (bf16[96,3328]{1,0:T(8,128)(2,1)S(1)}, bf16[96,3328]{1,0:T(8,128)(2,1)S(1)}, f32[64,3328]{1,0:T(8,128)S(1)}) custom-call(bf16[256,1024]{1,0:T(8,128)(2,1)S(1)} %get-tuple-element.31.left_ref, bf16[512,13312]{1,0:T(8,128)(2,1)} %get-tuple-element.32.own_ref, bf16[512,13312]{1,0:T(8,128)(2,1)} %collective-permute-done.6.other_ref), custom_call_target="tpu_custom_call" | custom-call | flops 1744830464 | bytes 8519680 | tf_op jit(solution)/shard_map/product/pallas_call | solution.py:354
  256.9 2.0 collective-permute-start.7
  259.0 4.4 %product.7 = (bf16[96,3328]{1,0:T(8,128)(2,1)S(1)}, bf16[96,3328]{1,0:T(8,128)(2,1)S(1)}, f32[64,3328]{1,0:T(8,128)S(1)}) custom-call(bf16[256,1024]{1,0:T(8,128)(2,1)S(1)} %get-tuple-element.39.left_ref, bf16[512,13312]{1,0:T(8,128)(2,1)} %get-tuple-element.32.own_ref, bf16[512,13312]{1,0:T(8,128)(2,1)} %collective-permute-done.6.other_ref), custom_call_target="tpu_custom_call" | custom-call | flops 1744830464 | bytes 8519680 | tf_op jit(solution)/shard_map/product/pallas_call | solution.py:354
  263.4 0.9 collective-permute-start.22
  264.2 4.4 %product.6 = (bf16[96,3328]{1,0:T(8,128)(2,1)S(1)}, bf16[96,3328]{1,0:T(8,128)(2,1)S(1)}, f32[64,3328]{1,0:T(8,128)S(1)}) custom-call(bf16[256,1024]{1,0:T(8,128)(2,1)S(1)} %get-tuple-element.39.left_ref, bf16[512,13312]{1,0:T(8,128)(2,1)} %get-tuple-element.32.own_ref, bf16[512,13312]{1,0:T(8,128)(2,1)} %collective-permute-done.6.other_ref), custom_call_target="tpu_custom_call" | custom-call | flops 1744830464 | bytes 8519680 | tf_op jit(solution)/shard_map/product/pallas_call | solution.py:354
  268.7 2.7 collective-permute-start.23
  271.4 8.4 %collective-permute-done.8 = bf16[96,3328]{1,0:T(8,128)(2,1)S(1)} collective-permute-done((bf16[96,3328]{1,0:T(8,128)(2,1)S(1)}, bf16[96,3328]{1,0:T(8,128)(2,1)S(1)}, u32[]{:S(2)}, u32[]{:S(2)}) %collective-permute-start.8) | collective-permute-done | bytes 639008 | tf_op jit(solution)/shard_map/ppermute | solution.py:466
  279.8 0.7 collective-permute-start.19
  280.5 0.9 collective-permute-start.13
  281.5 0.7 collective-permute-done.22
  282.2 2.2 collective-permute-start.14
  284.5 1.7 collective-permute-done.23
  286.2 1.3 collective-permute-start.10
  287.5 6.3 %collective-permute-done.18 = bf16[96,3328]{1,0:T(8,128)(2,1)S(1)} collective-permute-done((bf16[96,3328]{1,0:T(8,128)(2,1)S(1)}, bf16[96,3328]{1,0:T(8,128)(2,1)S(1)}, u32[]{:S(2)}, u32[]{:S(2)}) %collective-permute-start.18) | collective-permute-done | bytes 639008 | tf_op jit(solution)/shard_map/ppermute | solution.py:466
  293.9 0.3 collective-permute-start.9
  294.2 3.4 %collective-permute-done.19 = bf16[96,3328]{1,0:T(8,128)(2,1)S(1)} collective-permute-done((bf16[96,3328]{1,0:T(8,128)(2,1)S(1)}, bf16[96,3328]{1,0:T(8,128)(2,1)S(1)}, u32[]{:S(2)}, u32[]{:S(2)}) %collective-permute-start.19) | collective-permute-done | bytes 639008 | tf_op jit(solution)/shard_map/ppermute | solution.py:466
  297.8 3.6 %collective-permute-start.25 = (bf16[32,3328]{1,0:T(8,128)(2,1)S(1)}, bf16[32,3328]{1,0:T(8,128)(2,1)S(1)}, u32[]{:S(2)}, u32[]{:S(2)}) collective-permute-start(bf16[32,3328]{1,0:T(8,128)(2,1)S(1)} %slice.134), channel_id=1, source_target_pairs={{0,24},{8,0},{16,8},{24,16},{32,56},{40,32},{48,40},{56,48},{64,88... | collective-permute-start | bytes 638984 | tf_op jit(solution)/shard_map/ppermute | solution.py:467
  301.4 0.2 convert_add_fusion.2
  301.6 3.3 %collective-permute-start.21 = (bf16[32,3328]{1,0:T(8,128)(2,1)S(1)}, bf16[32,3328]{1,0:T(8,128)(2,1)S(1)}, u32[]{:S(2)}, u32[]{:S(2)}) collective-permute-start(bf16[32,3328]{1,0:T(8,128)(2,1)S(1)} %slice.130), channel_id=1, source_target_pairs={{0,24},{8,0},{16,8},{24,16},{32,56},{40,32},{48,40},{56,48},{64,88... | collective-permute-start | bytes 638984 | tf_op jit(solution)/shard_map/ppermute | solution.py:467
  304.9 0.2 convert_add_fusion.3
  305.3 2.1 collective-permute-done.24
  307.4 1.1 collective-permute-start.16
  308.5 3.6 %collective-permute-start.17 = (bf16[16,6656]{1,0:T(8,128)(2,1)S(1)}, bf16[16,6656]{1,0:T(8,128)(2,1)S(1)}, u32[]{:S(2)}, u32[]{:S(2)}) collective-permute-start(bf16[16,6656]{1,0:T(8,128)(2,1)S(1)} %get-tuple-element.49), channel_id=1, source_target_pairs={{0,24},{8,0},{16,8},{24,16},{32,56},{40,32},{48,40},{56,48},{64,88... | collective-permute-start | bytes 638984 | tf_op jit(solution)/shard_map/ppermute | solution.py:477
  312.1 0.2 convert_add_fusion
  312.3 3.7 %collective-permute-done.21 = bf16[32,3328]{1,0:T(8,128)(2,1)S(1)} collective-permute-done((bf16[32,3328]{1,0:T(8,128)(2,1)S(1)}, bf16[32,3328]{1,0:T(8,128)(2,1)S(1)}, u32[]{:S(2)}, u32[]{:S(2)}) %collective-permute-start.21) | collective-permute-done | bytes 213024 | tf_op jit(solution)/shard_map/ppermute | solution.py:467
  316.3 0.5 collective-permute-start.26
  316.8 2.8 collective-permute-start.27
  319.7 3.7 %collective-permute-done.26 = bf16[16,6656]{1,0:T(8,128)(2,1)S(1)} collective-permute-done((bf16[16,6656]{1,0:T(8,128)(2,1)S(1)}, bf16[16,6656]{1,0:T(8,128)(2,1)S(1)}, u32[]{:S(2)}, u32[]{:S(2)}) %collective-permute-start.26) | collective-permute-done | bytes 213024 | tf_op jit(solution)/shard_map/ppermute | solution.py:477
  323.4 2.3 collective-permute-done.27
  325.7 0.9 collective-permute-done.28
  326.7 1.0 pad_maximum_fusion.2
  (62 shorter events, 2.5 us)
Async XLA Ops:
  2.2 12.0 %copy-start = (s32[128]{0:T(128)}, s32[128]{0:T(128)S(1)}, u32[]{:S(2)}) copy-start(s32[128]{0:T(128)S(1)} %get-tuple-element.54.place_ref) | copy-start | bytes 1540
  3.1 20.1 %all-to-all-start = ((s32[128,1,2]{2,1,0:T(1,128)}), s32[128,1,2]{2,1,0:T(1,128)S(1)}, u32[]{:S(2)}, u32[]{:S(2)}) async-start(s32[128,1,2]{2,1,0:T(1,128)} %bitcast.19), calls=%async_computation | async-start | bytes 131072 | tf_op jit(solution)/shard_map/all_to_all | solution.py:399
  23.2 114.4 %all-to-all-start.1 = ((bf16[128,2,128,128]{3,2,1,0:T(8,128)(2,1)}), bf16[128,2,128,128]{3,2,1,0:T(8,128)(2,1)}, u32[]{:S(2)}, u32[]{:S(2)}) async-start(bf16[128,2,128,128]{3,2,1,0:T(8,128)(2,1)} %bitcast.48), calls=%async_computation.1 | async-start | bytes 16777216 | tf_op jit(solution)/shard_map/all_to_all | solution.py:396
  155.8 89.0 %collective-permute-start.6 = (bf16[512,13312]{1,0:T(8,128)(2,1)}, bf16[512,13312]{1,0:T(8,128)(2,1)}, u32[]{:S(2)}, u32[]{:S(2)}) collective-permute-start(bf16[512,13312]{1,0:T(8,128)(2,1)} %get-tuple-element.32.own_ref), channel_id=1, source_target_pairs={{0,4},{4,0},{1,5},{5,1},{2,6},{6,2},{3,7},{7,3},{8,12},{12,8},{9,1... | collective-permute-start | bytes 40894472 | tf_op jit(solution)/shard_map/ppermute | solution.py:418
  155.9 19.5 %all-to-all-start.2 = ((f32[4,128,512]{2,1,0:T(8,128)}), f32[4,128,512]{2,1,0:T(8,128)S(1)}, u32[]{:S(2)}, u32[]{:S(2)}) async-start(f32[4,128,512]{2,1,0:T(8,128)} %bitcast.23), calls=%async_computation.2 | async-start | bytes 2097152 | tf_op jit(solution)/shard_map/all_to_all | solution.py:421
  176.2 1.7 collective-permute-start
  197.4 10.0 %collective-permute-start.2 = (f32[128,512]{1,0:T(8,128)S(1)}, f32[128,512]{1,0:T(8,128)S(1)}, u32[]{:S(2)}, u32[]{:S(2)}) collective-permute-start(f32[128,512]{1,0:T(8,128)S(1)} %get-tuple-element.29), channel_id=1, source_target_pairs={{0,3},{1,0},{2,1},{3,2},{4,7},{5,4},{6,5},{7,6},{8,11},{9,8},{10,9... | collective-permute-start | bytes 786440 | tf_op jit(solution)/shard_map/ppermute | solution.py:433
  198.4 10.8 %collective-permute-start.3 = (f32[128,512]{1,0:T(8,128)S(1)}, f32[128,512]{1,0:T(8,128)S(1)}, u32[]{:S(2)}, u32[]{:S(2)}) collective-permute-start(f32[128,512]{1,0:T(8,128)S(1)} %get-tuple-element.29), channel_id=1, source_target_pairs={{0,2},{1,3},{2,0},{3,1},{4,6},{5,7},{6,4},{7,5},{8,10},{9,11},{10,... | collective-permute-start | bytes 786440 | tf_op jit(solution)/shard_map/ppermute | solution.py:433
  200.2 13.9 %collective-permute-start.4 = (f32[128,512]{1,0:T(8,128)S(1)}, f32[128,512]{1,0:T(8,128)S(1)}, u32[]{:S(2)}, u32[]{:S(2)}) collective-permute-start(f32[128,512]{1,0:T(8,128)S(1)} %get-tuple-element.29), channel_id=1, source_target_pairs={{0,1},{1,2},{2,3},{3,0},{4,5},{5,6},{6,7},{7,4},{8,9},{9,10},{10,1... | collective-permute-start | bytes 786440 | tf_op jit(solution)/shard_map/ppermute | solution.py:433
  200.3 17.9 %all-to-all-start.4 = ((f32[64,1,1280]{2,1,0:T(1,128)}), f32[64,1,1280]{2,1,0:T(1,128)S(1)}, u32[]{:S(2)}, u32[]{:S(2)}) async-start(f32[64,1,1280]{2,1,0:T(1,128)} %broadcast_in_dim.61), calls=%async_computation.4 | async-start | bytes 655360 | tf_op jit(solution)/shard_map/all_to_all | solution.py:430
  218.2 1.7 collective-permute-start.1
  218.4 22.4 %collective-permute-start.5 = (f32[512,512]{1,0:T(8,128)S(1)}, f32[512,512]{1,0:T(8,128)S(1)}, u32[]{:S(2)}, u32[]{:S(2)}) collective-permute-start(f32[512,512]{1,0:T(8,128)S(1)} %bitcast.44), channel_id=1, source_target_pairs={{0,4},{4,0},{1,5},{5,1},{2,6},{6,2},{3,7},{7,3},{8,12},{12,8},{9,1... | collective-permute-start | bytes 3145736 | tf_op jit(solution)/shard_map/ppermute | solution.py:439
  249.1 19.5 %collective-permute-start.11 = (bf16[96,3328]{1,0:T(8,128)(2,1)S(1)}, bf16[96,3328]{1,0:T(8,128)(2,1)S(1)}, u32[]{:S(2)}, u32[]{:S(2)}) collective-permute-start(bf16[96,3328]{1,0:T(8,128)(2,1)S(1)} %get-tuple-element.37), channel_id=1, source_target_pairs={{0,32},{8,40},{16,48},{24,56},{32,64},{40,72},{48,80},{56,88},{64,... | collective-permute-start | bytes 1916936 | tf_op jit(solution)/shard_map/ppermute | solution.py:466
  249.9 21.5 %collective-permute-start.12 = (bf16[96,3328]{1,0:T(8,128)(2,1)S(1)}, bf16[96,3328]{1,0:T(8,128)(2,1)S(1)}, u32[]{:S(2)}, u32[]{:S(2)}) collective-permute-start(bf16[96,3328]{1,0:T(8,128)(2,1)S(1)} %get-tuple-element.38), channel_id=1, source_target_pairs={{0,96},{8,104},{16,112},{24,120},{32,0},{40,8},{48,16},{56,24},{64... | collective-permute-start | bytes 1916936 | tf_op jit(solution)/shard_map/ppermute | solution.py:466
  256.9 23.0 %collective-permute-start.8 = (bf16[96,3328]{1,0:T(8,128)(2,1)S(1)}, bf16[96,3328]{1,0:T(8,128)(2,1)S(1)}, u32[]{:S(2)}, u32[]{:S(2)}) collective-permute-start(bf16[96,3328]{1,0:T(8,128)(2,1)S(1)} %get-tuple-element.35), channel_id=1, source_target_pairs={{0,96},{8,104},{16,112},{24,120},{32,0},{40,8},{48,16},{56,24},{64... | collective-permute-start | bytes 1916936 | tf_op jit(solution)/shard_map/ppermute | solution.py:466
  256.9 23.6 %collective-permute-start.7 = (bf16[96,3328]{1,0:T(8,128)(2,1)S(1)}, bf16[96,3328]{1,0:T(8,128)(2,1)S(1)}, u32[]{:S(2)}, u32[]{:S(2)}) collective-permute-start(bf16[96,3328]{1,0:T(8,128)(2,1)S(1)} %get-tuple-element.34), channel_id=1, source_target_pairs={{0,32},{8,40},{16,48},{24,56},{32,64},{40,72},{48,80},{56,88},{64,... | collective-permute-start | bytes 1916936 | tf_op jit(solution)/shard_map/ppermute | solution.py:466
  263.4 18.8 %collective-permute-start.22 = (bf16[96,3328]{1,0:T(8,128)(2,1)S(1)}, bf16[96,3328]{1,0:T(8,128)(2,1)S(1)}, u32[]{:S(2)}, u32[]{:S(2)}) collective-permute-start(bf16[96,3328]{1,0:T(8,128)(2,1)S(1)} %get-tuple-element.44), channel_id=1, source_target_pairs={{0,8},{8,16},{16,24},{24,0},{32,40},{40,48},{48,56},{56,32},{64,72... | collective-permute-start | bytes 1916936 | tf_op jit(solution)/shard_map/ppermute | solution.py:466
  268.7 17.6 %collective-permute-start.23 = (bf16[96,3328]{1,0:T(8,128)(2,1)S(1)}, bf16[96,3328]{1,0:T(8,128)(2,1)S(1)}, u32[]{:S(2)}, u32[]{:S(2)}) collective-permute-start(bf16[96,3328]{1,0:T(8,128)(2,1)S(1)} %get-tuple-element.45), channel_id=1, source_target_pairs={{0,24},{8,0},{16,8},{24,16},{32,56},{40,32},{48,40},{56,48},{64,88... | collective-permute-start | bytes 1916936 | tf_op jit(solution)/shard_map/ppermute | solution.py:466
  271.4 22.5 %collective-permute-start.18 = (bf16[96,3328]{1,0:T(8,128)(2,1)S(1)}, bf16[96,3328]{1,0:T(8,128)(2,1)S(1)}, u32[]{:S(2)}, u32[]{:S(2)}) collective-permute-start(bf16[96,3328]{1,0:T(8,128)(2,1)S(1)} %get-tuple-element.41), channel_id=1, source_target_pairs={{0,8},{8,16},{16,24},{24,0},{32,40},{40,48},{48,56},{56,32},{64,72... | collective-permute-start | bytes 1916936 | tf_op jit(solution)/shard_map/ppermute | solution.py:466
  279.8 17.8 %collective-permute-start.19 = (bf16[96,3328]{1,0:T(8,128)(2,1)S(1)}, bf16[96,3328]{1,0:T(8,128)(2,1)S(1)}, u32[]{:S(2)}, u32[]{:S(2)}) collective-permute-start(bf16[96,3328]{1,0:T(8,128)(2,1)S(1)} %get-tuple-element.42), channel_id=1, source_target_pairs={{0,24},{8,0},{16,8},{24,16},{32,56},{40,32},{48,40},{56,48},{64,88... | collective-permute-start | bytes 1916936 | tf_op jit(solution)/shard_map/ppermute | solution.py:466
  280.5 17.2 %collective-permute-start.13 = (bf16[32,3328]{1,0:T(8,128)(2,1)S(1)}, bf16[32,3328]{1,0:T(8,128)(2,1)S(1)}, u32[]{:S(2)}, u32[]{:S(2)}) collective-permute-start(bf16[32,3328]{1,0:T(8,128)(2,1)S(1)} %slice.120), channel_id=1, source_target_pairs={{0,32},{8,40},{16,48},{24,56},{32,64},{40,72},{48,80},{56,88},{64,... | collective-permute-start | bytes 638984 | tf_op jit(solution)/shard_map/ppermute | solution.py:467
  282.2 19.2 %collective-permute-start.14 = (bf16[32,3328]{1,0:T(8,128)(2,1)S(1)}, bf16[32,3328]{1,0:T(8,128)(2,1)S(1)}, u32[]{:S(2)}, u32[]{:S(2)}) collective-permute-start(bf16[32,3328]{1,0:T(8,128)(2,1)S(1)} %slice.121), channel_id=1, source_target_pairs={{0,96},{8,104},{16,112},{24,120},{32,0},{40,8},{48,16},{56,24},{64... | collective-permute-start | bytes 638984 | tf_op jit(solution)/shard_map/ppermute | solution.py:467
  286.2 15.4 %collective-permute-start.10 = (bf16[32,3328]{1,0:T(8,128)(2,1)S(1)}, bf16[32,3328]{1,0:T(8,128)(2,1)S(1)}, u32[]{:S(2)}, u32[]{:S(2)}) collective-permute-start(bf16[32,3328]{1,0:T(8,128)(2,1)S(1)} %slice.117), channel_id=1, source_target_pairs={{0,96},{8,104},{16,112},{24,120},{32,0},{40,8},{48,16},{56,24},{64... | collective-permute-start | bytes 638984 | tf_op jit(solution)/shard_map/ppermute | solution.py:467
  293.9 11.0 %collective-permute-start.9 = (bf16[32,3328]{1,0:T(8,128)(2,1)S(1)}, bf16[32,3328]{1,0:T(8,128)(2,1)S(1)}, u32[]{:S(2)}, u32[]{:S(2)}) collective-permute-start(bf16[32,3328]{1,0:T(8,128)(2,1)S(1)} %slice.116), channel_id=1, source_target_pairs={{0,32},{8,40},{16,48},{24,56},{32,64},{40,72},{48,80},{56,88},{64,... | collective-permute-start | bytes 638984 | tf_op jit(solution)/shard_map/ppermute | solution.py:467
  297.6 9.8 %collective-permute-start.24 = (bf16[32,3328]{1,0:T(8,128)(2,1)S(1)}, bf16[32,3328]{1,0:T(8,128)(2,1)S(1)}, u32[]{:S(2)}, u32[]{:S(2)}) collective-permute-start(bf16[32,3328]{1,0:T(8,128)(2,1)S(1)} %slice.133), channel_id=1, source_target_pairs={{0,8},{8,16},{16,24},{24,0},{32,40},{40,48},{48,56},{56,32},{64,72... | collective-permute-start | bytes 638984 | tf_op jit(solution)/shard_map/ppermute | solution.py:467
  297.8 10.7 %collective-permute-start.25 = (bf16[32,3328]{1,0:T(8,128)(2,1)S(1)}, bf16[32,3328]{1,0:T(8,128)(2,1)S(1)}, u32[]{:S(2)}, u32[]{:S(2)}) collective-permute-start(bf16[32,3328]{1,0:T(8,128)(2,1)S(1)} %slice.134), channel_id=1, source_target_pairs={{0,24},{8,0},{16,8},{24,16},{32,56},{40,32},{48,40},{56,48},{64,88... | collective-permute-start | bytes 638984 | tf_op jit(solution)/shard_map/ppermute | solution.py:467
  301.4 10.8 %collective-permute-start.20 = (bf16[32,3328]{1,0:T(8,128)(2,1)S(1)}, bf16[32,3328]{1,0:T(8,128)(2,1)S(1)}, u32[]{:S(2)}, u32[]{:S(2)}) collective-permute-start(bf16[32,3328]{1,0:T(8,128)(2,1)S(1)} %slice.129), channel_id=1, source_target_pairs={{0,8},{8,16},{16,24},{24,0},{32,40},{40,48},{48,56},{56,32},{64,72... | collective-permute-start | bytes 638984 | tf_op jit(solution)/shard_map/ppermute | solution.py:467
  301.6 14.4 %collective-permute-start.21 = (bf16[32,3328]{1,0:T(8,128)(2,1)S(1)}, bf16[32,3328]{1,0:T(8,128)(2,1)S(1)}, u32[]{:S(2)}, u32[]{:S(2)}) collective-permute-start(bf16[32,3328]{1,0:T(8,128)(2,1)S(1)} %slice.130), channel_id=1, source_target_pairs={{0,24},{8,0},{16,8},{24,16},{32,56},{40,32},{48,40},{56,48},{64,88... | collective-permute-start | bytes 638984 | tf_op jit(solution)/shard_map/ppermute | solution.py:467
  305.2 14.3 %collective-permute-start.15 = (bf16[16,6656]{1,0:T(8,128)(2,1)S(1)}, bf16[16,6656]{1,0:T(8,128)(2,1)S(1)}, u32[]{:S(2)}, u32[]{:S(2)}) collective-permute-start(bf16[16,6656]{1,0:T(8,128)(2,1)S(1)} %get-tuple-element.48), channel_id=1, source_target_pairs={{0,8},{8,16},{16,24},{24,0},{32,40},{40,48},{48,56},{56,32},{64,72... | collective-permute-start | bytes 638984 | tf_op jit(solution)/shard_map/ppermute | solution.py:477
  307.4 12.2 %collective-permute-start.16 = (bf16[16,6656]{1,0:T(8,128)(2,1)S(1)}, bf16[16,6656]{1,0:T(8,128)(2,1)S(1)}, u32[]{:S(2)}, u32[]{:S(2)}) collective-permute-start(bf16[16,6656]{1,0:T(8,128)(2,1)S(1)} %get-tuple-element.50), channel_id=1, source_target_pairs={{0,16},{8,24},{16,0},{24,8},{32,48},{40,56},{48,32},{56,40},{64,80... | collective-permute-start | bytes 638984 | tf_op jit(solution)/shard_map/ppermute | solution.py:477
  308.5 11.1 %collective-permute-start.17 = (bf16[16,6656]{1,0:T(8,128)(2,1)S(1)}, bf16[16,6656]{1,0:T(8,128)(2,1)S(1)}, u32[]{:S(2)}, u32[]{:S(2)}) collective-permute-start(bf16[16,6656]{1,0:T(8,128)(2,1)S(1)} %get-tuple-element.49), channel_id=1, source_target_pairs={{0,24},{8,0},{16,8},{24,16},{32,56},{40,32},{48,40},{56,48},{64,88... | collective-permute-start | bytes 638984 | tf_op jit(solution)/shard_map/ppermute | solution.py:477
  316.3 7.1 %collective-permute-start.26 = (bf16[16,6656]{1,0:T(8,128)(2,1)S(1)}, bf16[16,6656]{1,0:T(8,128)(2,1)S(1)}, u32[]{:S(2)}, u32[]{:S(2)}) collective-permute-start(bf16[16,6656]{1,0:T(8,128)(2,1)S(1)} %get-tuple-element.51), channel_id=1, source_target_pairs={{0,32},{8,40},{16,48},{24,56},{32,64},{40,72},{48,80},{56,88},{64,... | collective-permute-start | bytes 638984 | tf_op jit(solution)/shard_map/ppermute | solution.py:477
  316.8 8.9 %collective-permute-start.27 = (bf16[16,6656]{1,0:T(8,128)(2,1)S(1)}, bf16[16,6656]{1,0:T(8,128)(2,1)S(1)}, u32[]{:S(2)}, u32[]{:S(2)}) collective-permute-start(bf16[16,6656]{1,0:T(8,128)(2,1)S(1)} %get-tuple-element.53), channel_id=1, source_target_pairs={{0,64},{8,72},{16,80},{24,88},{32,96},{40,104},{48,112},{56,120},{... | collective-permute-start | bytes 638984 | tf_op jit(solution)/shard_map/ppermute | solution.py:477
  319.5 7.0 %collective-permute-start.28 = (bf16[16,6656]{1,0:T(8,128)(2,1)S(1)}, bf16[16,6656]{1,0:T(8,128)(2,1)S(1)}, u32[]{:S(2)}, u32[]{:S(2)}) collective-permute-start(bf16[16,6656]{1,0:T(8,128)(2,1)S(1)} %get-tuple-element.52), channel_id=1, source_target_pairs={{0,96},{8,104},{16,112},{24,120},{32,0},{40,8},{48,16},{56,24},{64... | collective-permute-start | bytes 638984 | tf_op jit(solution)/shard_map/ppermute | solution.py:477
